TPU v7x, 256 devices: a whole 4x4x8 slice. The times are simulated.
256 devices in a mesh: sess: 8 (over x, z_lo), ctx: 32 (over y, z_hi, core).
Axes of the slice: x: 4, y: 4, z: 8 (z_hi: 4, z_lo: 2; z = z_hi * 2 + z_lo), core: 2. Of those that a mesh axis runs over, the one named last changes fastest.
Arguments:
- mamba_input: bfloat16 [8, 4096, 8192], P('sess', 'ctx'), may hold values from -6 to 6
- step_size: bfloat16 [8, 4096, 64], P('sess', 'ctx'), may hold values from 0.19921875 to 1.5
- decay_log: bfloat16 [8, 4096, 64], P('sess', 'ctx'), may hold values from -0.8 to 0
- state_write: bfloat16 [8, 4096, 512], P('sess', 'ctx'), may hold values from -0.375 to 0.375
- state_read: bfloat16 [8, 4096, 512], P('sess', 'ctx'), may hold values from -0.75 to 0.75
- skip_gain: float32 [64], replicated, may hold values from 0.1 to 1.9
- saved_states: float32 [8, 3, 64, 8192], P('sess', None, 'ctx'), may hold values from -6 to 6
- home_slot: int32 [24], replicated, may hold values from 0 to 23, each once
- turn_lengths: int32 [8, 3], P('sess'), may hold values from 1 to 2048, 4096 in all within a row
- history_lengths: int32 [8, 3], P('sess'), may hold values from 4 to 1023
- queries: bfloat16 [8, 4096, 4096], P('sess', 'ctx'), may hold values from -150 to 150
- turn_keys: bfloat16 [8, 4096, 512], P('sess', 'ctx'), may hold values from -6 to 6
- turn_values: bfloat16 [8, 4096, 512], P('sess', 'ctx'), may hold values from -6 to 6
- cache_keys: bfloat16 [8, 3, 512, 512], P('sess', None, 'ctx'), may hold values from -6 to 6
- cache_values: bfloat16 [8, 3, 512, 512], P('sess', None, 'ctx'), may hold values from -6 to 6
- sink_keys: bfloat16 [8, 3, 4, 512], P('sess'), may hold values from -12 to 12
- sink_values: bfloat16 [8, 3, 4, 512], P('sess'), may hold values from -6 to 6
Outputs:
- mixed: bfloat16 [8, 4096, 8192], P('sess', 'ctx')
- attended: bfloat16 [8, 4096, 4096], P('sess', 'ctx')
Inputs may be any that keep to these rules, and one draw needn't show every extreme that they name: `home_slot`: entry g * 3 + s names the stored state, in the group-major list of saved_states, from which session s of group g resumes.
All inputs are finite; a program needn't handle non-finite values.
Results may differ from a plain program's by a relative error of at most 0.004.
Values may be sent and summed in bfloat16 or wider, within the bound.
A program may use at most 256 MiB of HBM per device.

v0:
```python
import math

import jax
import jax.numpy as jnp
from jax import lax
from jax.sharding import PartitionSpec as P

REACH = 4
SEQS = 3
SINKS = 4
H = 64
P_SIZE = 128
N = 64
G = 8
QH = 32
KVH = 4
HD = 128
WINDOW = 512


precise = lax.Precision.HIGHEST


def carried_in(array, axis, combine, identity):
    length, place = (lax.axis_size(axis), lax.axis_index(axis))
    everything = jax.tree.map(lambda part: lax.all_gather(part, axis), array)
    start = jax.tree.map(
        lambda part, zero: jnp.broadcast_to(jnp.asarray(zero, part.dtype), part.shape),
        array,
        identity,
    )

    def turn(k, before):
        reached = k < place
        new = combine(before, jax.tree.map(lambda part: part[k], everything))
        return jax.tree.map(lambda a, b: jnp.where(reached, a, b), new, before)

    return lax.fori_loop(0, length, turn, start)


def shifted(block, axis, distance):
    devices = range(lax.axis_size(axis))
    route = [(i - distance, i) for i in devices if i - distance in devices]
    return lax.ppermute(block, axis, route)


def session_starts(lengths):
    ends = jnp.cumsum(lengths)
    return jnp.concatenate([jnp.zeros((1,), jnp.int32), ends[:-1]])


def session_of(positions, starts):
    later = positions[:, None] >= starts[None, 1:]
    return jnp.sum(later.astype(jnp.int32), axis=1)


def stretch_terms(inputs, step_sizes, log_rates, writes, read_rows, segment, relative, states):
    stretch_len = inputs.shape[0]
    sessions = states.shape[0]
    positions = jnp.arange(stretch_len, dtype=jnp.int32)
    log_rate = jnp.transpose(log_rates.astype(jnp.float32), (1, 2, 0))
    running = jnp.cumsum(log_rate, axis=2)
    before = running - log_rate
    causal = (segment[:, None] == segment[None, :]) & (positions[:, None] >= positions[None, :])
    differences = running[:, :, :, None] - running[:, :, None, :]
    decays = jnp.exp(jnp.where(causal, differences, -jnp.inf))
    intersection = jnp.einsum("tgn,sgn->gts", read_rows, writes, preferred_element_type=jnp.float32)
    step_scale = jnp.transpose(step_sizes.astype(jnp.float32), (1, 2, 0))
    mixing = (intersection[:, None] * decays * step_scale[:, :, None, :]).astype(jnp.bfloat16)
    intra_part = jnp.einsum("gkts,sgkp->tgkp", mixing, inputs, preferred_element_type=jnp.float32)
    session_ids = jnp.arange(sessions, dtype=jnp.int32)
    inside = (relative >= 0) & (relative < stretch_len)
    at_start = positions[None, :] == relative[:, None]
    base_log = jnp.sum(jnp.where(at_start[None, None], before[:, :, None, :], 0.0), axis=3)
    owned = segment[:, None] == session_ids[None, :]
    starts_here = owned & inside[None, :]
    exponent = running[:, :, None, :] - base_log[:, :, :, None]
    from_saved = jnp.exp(jnp.where(jnp.transpose(starts_here)[None, None], exponent, -jnp.inf))
    read_float = read_rows.astype(jnp.float32)
    readout = jnp.einsum("tgn,sgkpn->sgktp", read_float, states, precision=precise)
    intra_part = intra_part + jnp.einsum("gkst,sgktp->tgkp", from_saved, readout, precision=precise)
    earlier = jnp.any(owned & (relative[None, :] < 0), axis=1)
    from_incoming = jnp.where(earlier[None, None, :], jnp.exp(running), 0.0)
    last_session = segment[stretch_len - 1]
    tail_decay = jnp.exp(
        jnp.where(
            (segment == last_session)[None, None, :],
            running[:, :, stretch_len - 1 :] - running,
            -jnp.inf,
        )
    )
    loadings = (
        (tail_decay * step_scale)[:, :, :, None]
        * jnp.transpose(writes.astype(jnp.float32), (1, 0, 2))[:, None]
    ).astype(jnp.bfloat16)
    summary = jnp.einsum("sgkp,gksn->gkpn", inputs, loadings, preferred_element_type=jnp.float32)
    ending = owned[stretch_len - 1] & inside
    end_decay = jnp.exp(
        jnp.where(ending[None, None, :], running[:, :, stretch_len - 1 :] - base_log, -jnp.inf)
    )
    summary = summary + jnp.einsum("gks,sgkpn->gkpn", end_decay, states, precision=precise)
    carry_factor = jnp.where(earlier[stretch_len - 1], jnp.exp(running[:, :, stretch_len - 1]), 0.0)
    return (intra_part, from_incoming, carry_factor, summary)


def finish(intra_part, from_incoming, read_rows, state_in, inputs, skip_gains):
    carried = jnp.einsum(
        "tgn,gkpn->tgkp", read_rows.astype(jnp.float32), state_in, precision=precise
    )
    weight = jnp.transpose(from_incoming, (2, 0, 1))[..., None]
    result = (
        intra_part + weight * carried + skip_gains[None, :, :, None] * inputs.astype(jnp.float32)
    )
    return result.astype(jnp.bfloat16)


def chain_step(earlier, later):
    return (earlier[0] * later[0], later[0][:, None] * earlier[1] + later[1])


def visible(query_pos, turn_pos, starts, history):
    sessions = starts.shape[0]
    session_ids = jnp.arange(sessions, dtype=jnp.int32)
    owner = session_of(query_pos, starts)
    in_session = owner[:, None] == session_ids[None, :]
    offset = query_pos - jnp.sum(jnp.where(in_session, starts[None, :], 0), axis=1)
    sink_owner = jnp.arange(sessions * SINKS, dtype=jnp.int32) // SINKS
    sink_ok = owner[:, None] == sink_owner[None, :]
    slot_ids = jnp.arange(sessions * WINDOW, dtype=jnp.int32)
    slot_owner = slot_ids // WINDOW
    slot_place = slot_ids % WINDOW
    slot_history = jnp.sum(
        jnp.where(slot_owner[:, None] == session_ids[None, :], history[None, :], 0), axis=1
    )
    cache_ok = (
        (owner[:, None] == slot_owner[None, :])
        & (slot_place[None, :] > offset[:, None])
        & (slot_history - WINDOW + slot_place >= SINKS)[None, :]
    )
    key_owner = session_of(turn_pos, starts)
    distance = query_pos[:, None] - turn_pos[None, :]
    turn_ok = (
        (turn_pos[None, :] >= 0)
        & (key_owner[None, :] == owner[:, None])
        & (distance >= 0)
        & (distance < WINDOW)
    )
    return jnp.concatenate([sink_ok, cache_ok, turn_ok], axis=1)


def attend(queries, keys, payload_elements, valid):
    row_count = queries.shape[0]
    per_group = QH // KVH
    factor = 1.0 / math.sqrt(HD)

    def one_head(number):
        query_h = lax.dynamic_slice_in_dim(
            queries, number * per_group * HD, per_group * HD, 1
        ).reshape(row_count, per_group, HD)
        key_h = lax.dynamic_slice_in_dim(keys, number * HD, HD, 1)
        value_h = lax.dynamic_slice_in_dim(payload_elements, number * HD, HD, 1)
        scores = (
            jnp.einsum("tgd,nd->gtn", query_h, key_h, preferred_element_type=jnp.float32) * factor
        )
        scores = jnp.where(valid[None], scores, -jnp.inf)
        row_max = jnp.max(scores, axis=2, keepdims=True)
        weights = jnp.exp(scores - row_max)
        denominator = jnp.sum(weights, axis=2)
        rounded = weights.astype(jnp.bfloat16)
        mixed = jnp.einsum("gtn,nd->tgd", rounded, value_h, preferred_element_type=jnp.float32)
        return mixed / jnp.transpose(denominator)[:, :, None]

    outputs = lax.map(one_head, jnp.arange(KVH, dtype=jnp.int32))
    return jnp.transpose(outputs, (1, 0, 2, 3)).reshape(row_count, QH * HD).astype(jnp.bfloat16)


def shards(
    mamba_input,
    step_size,
    decay_log,
    state_write,
    state_read,
    skip_gain,
    saved_states,
    home_slot,
    turn_lengths,
    history_lengths,
    queries,
    turn_keys,
    turn_values,
    cache_keys,
    cache_values,
    sink_keys,
    sink_values,
):
    device_index = lax.axis_index("ctx")
    row_count = mamba_input.shape[1]
    local_heads = saved_states.shape[2]
    state_width = P_SIZE * N
    heads_per = H // G
    starts = session_starts(turn_lengths[0])
    own_slots = lax.dynamic_slice_in_dim(home_slot, lax.axis_index("sess") * SEQS, SEQS, 0)
    zeros_init = jnp.zeros((SEQS, local_heads, state_width), jnp.float32)
    piece = lax.all_gather(saved_states, "sess", axis=0, tiled=True)
    span_groups = piece.shape[0]
    slots = (
        jnp.arange(span_groups, dtype=jnp.int32)[:, None] * SEQS
        + jnp.arange(SEQS, dtype=jnp.int32)[None, :]
    ).reshape(span_groups * SEQS)
    selector = (own_slots[:, None] == slots[None, :]).astype(jnp.float32)
    flattened = piece.reshape(span_groups * SEQS, local_heads * state_width)
    restored = jnp.dot(selector, flattened, precision=precise).reshape(zeros_init.shape)
    gathered = lax.all_gather(restored, "ctx", axis=1, tiled=True)
    saved = gathered.reshape(SEQS, G, heads_per, P_SIZE, N)
    tokens_in = mamba_input[0].reshape(row_count, G, heads_per, P_SIZE)
    step_view = step_size[0].reshape(row_count, G, heads_per)
    rate_view = decay_log[0].reshape(row_count, G, heads_per)
    write_view = state_write[0].reshape(row_count, G, N)
    read_view = state_read[0].reshape(row_count, G, N)
    first_row = device_index * row_count
    segment = session_of(first_row + jnp.arange(row_count, dtype=jnp.int32), starts)
    intra_part, incoming, carry_factor, summary = stretch_terms(
        tokens_in, step_view, rate_view, write_view, read_view, segment, starts - first_row, saved
    )
    flat_factor = carry_factor.reshape(H)
    flat_summary = summary.reshape(H, state_width)
    prefix = carried_in(
        (flat_factor, flat_summary),
        "ctx",
        chain_step,
        (jnp.ones_like(flat_factor), jnp.zeros_like(flat_summary)),
    )
    state_in = prefix[1].reshape(G, heads_per, P_SIZE, N)
    mixed = finish(
        intra_part, incoming, read_view, state_in, tokens_in, skip_gain.reshape(G, heads_per)
    ).reshape(1, row_count, H * P_SIZE)
    features = turn_keys.shape[2]
    key_value = jnp.stack([turn_keys[0], turn_values[0]])
    blocks = [key_value]
    moving = key_value
    for number in range(REACH):
        moving = shifted(moving, "ctx", 1)
        blocks.append(moving)
    band_keys = jnp.concatenate(blocks[::-1], axis=1)
    history_k, history_v = (
        lax.all_gather(cache_keys, "ctx", axis=2, tiled=True),
        lax.all_gather(cache_values, "ctx", axis=2, tiled=True),
    )
    all_keys = jnp.concatenate(
        [
            sink_keys[0].reshape(SEQS * SINKS, features),
            history_k[0].reshape(SEQS * WINDOW, features),
            band_keys[0],
        ],
        axis=0,
    )
    all_values = jnp.concatenate(
        [
            sink_values[0].reshape(SEQS * SINKS, features),
            history_v[0].reshape(SEQS * WINDOW, features),
            band_keys[1],
        ],
        axis=0,
    )
    first_row = device_index * row_count
    query_pos = first_row + jnp.arange(row_count, dtype=jnp.int32)
    turn_pos = first_row - REACH * row_count + jnp.arange((REACH + 1) * row_count, dtype=jnp.int32)
    valid = visible(query_pos, turn_pos, starts, history_lengths[0])
    attended = attend(queries[0], all_keys, all_values, valid).reshape(1, row_count, QH * HD)
    return (mixed, attended)


def solution(mesh):
    return jax.shard_map(
        shards,
        mesh=mesh,
        in_specs=(
            P("sess", "ctx", None),
            P("sess", "ctx", None),
            P("sess", "ctx", None),
            P("sess", "ctx", None),
            P("sess", "ctx", None),
            P(),
            P("sess", None, "ctx", None),
            P(),
            P("sess", None),
            P("sess", None),
            P("sess", "ctx", None),
            P("sess", "ctx", None),
            P("sess", "ctx", None),
            P("sess", None, "ctx", None),
            P("sess", None, "ctx", None),
            P("sess", None, None, None),
            P("sess", None, None, None),
        ),
        out_specs=(P("sess", "ctx", None), P("sess", "ctx", None)),
        check_vma=False,
    )
```

profile of v0, /device:TPU:33, one launch (start us, length us, event | category | flops | bytes accessed | tf_op | source)
XLA Modules:
  0.0 726.6 jit_solution(10140657534218644516)
XLA Ops:
  8.9 45.8 %all-gather.7.cloned.1.call-done = f32[8,3,2,8192]{3,2,1,0:T(2,128)} async-done(((f32[1,3,2,8192]{3,2,1,0:T(2,128)}), f32[8,3,2,8192]{3,2,1,0:T(2,128)}) %all-gather.7.cloned.1.call-update) | async-done | bytes 1572880 | tf_op jit(solution)/shard_map/all_gather | solution.py:204
  54.6 3.6 fusion.39
  61.4 3.2 copy.54
  69.5 70.6 %all-gather.9.cloned.1.call-done = f32[3,64,8192]{2,0,1:T(4,128)} async-done(((f32[3,2,8192]{2,0,1:T(4,128)}), f32[3,64,8192]{2,0,1:T(4,128)}) %all-gather.9.cloned.1.call-update) | async-done | bytes 6291472 | tf_op jit(solution)/shard_map/all_gather | solution.py:213
  140.0 9.7 %copy.57 = f32[3,64,8192]{2,1,0:T(8,128)} copy(f32[3,64,8192]{2,0,1:T(4,128)} %all-gather.9.cloned.1.call-done) | data formatting | bytes 12582912 | tf_op jit(solution)/shard_map/all_gather | solution.py:213
  149.7 10.9 %reshape.308 = f32[3,8,8,128,64]{4,3,2,1,0:T(8,128)} reshape(f32[3,64,8192]{2,1,0:T(8,128)} %copy.57) | data formatting | bytes 12582912 | tf_op jit(solution)/shard_map/reshape | solution.py:214
  160.7 8.1 %multiply_reduce_fusion = f32[8,8,128,64]{3,2,1,0:T(8,128)} fusion(f32[3,8,8,128,64]{4,3,2,1,0:T(8,128)} %reshape.308, f32[8,8,3]{1,0,2:T(8,128)S(1)} %copy.88), kind=kLoop, calls=%fused_computation.24 | loop fusion | flops 2621440 | bytes 8389376
  168.8 3.8 copy.82
  172.6 4.5 bitcast_add_fusion.2
  177.1 3.8 copy.60
  180.9 4.8 all_gather_reshape.4
  185.8 3.5 collective-permute-start
  195.4 5.3 collective-permute-start.1
  200.9 5.1 collective-permute-done.1
  206.0 5.4 collective-permute-start.2
  215.9 40.1 %all-gather = f32[32,1,64]{2,1,0:T(1,128)S(1)} all-gather(f32[1,1,64]{2,1,0:T(1,128)S(1)} %reshape.313), channel_id=1, replica_groups=mesh['sess'=8,'ctx'=32] {'ctx'}, dimensions={0}, use_global_device_ids=true | all-gather | bytes 8448 | tf_op jit(solution)/shard_map/all_gather | solution.py:26
  256.3 3.2 collective-permute-start.3
  259.5 4.6 fusion.32
  267.3 13.0 %concatenate.32 = bf16[2188,512]{1,0:T(8,128)(2,1)} concatenate(bf16[12,512]{1,0:T(8,128)(2,1)S(1)} %reshape_squeeze.26, bf16[1536,512]{1,0:T(8,128)(2,1)} %bitcast.167, bf16[640,512]{1,0:T(8,128)(2,1)} %get-tuple-element.244), dimensions={0} | concatenate | bytes 4481024 | tf_op jit(solution)/shard_map/concatenate | solution.py:257
  280.3 12.2 %concatenate.34 = bf16[2188,512]{1,0:T(8,128)(2,1)} concatenate(bf16[12,512]{1,0:T(8,128)(2,1)S(1)} %reshape_squeeze.28, bf16[1536,512]{1,0:T(8,128)(2,1)} %bitcast.168, bf16[640,512]{1,0:T(8,128)(2,1)S(1)} %get-tuple-element.243), dimensions={0} | concatenate | bytes 4481024 | tf_op jit(solution)/shard_map/concatenate | solution.py:249
  292.6 40.4 %while.26 = (s32[]{:T(128)}, bf16[4,128,8,128]{1,3,2,0:T(8,128)(2,1)}, s32[4]{0:T(128)S(1)}, bf16[2188,512]{1,0:T(8,128)(2,1)}, pred[128,2188]{0,1:T(8,128)(4,1)...) while((s32[]{:T(128)}, ...), condition=%wide.region_13.14_spmd, body=%wide.region_10.13_spmd.sunk | while | flops 1162954752 | bytes 38025012 | solution.py:173
  298.9 2.7 fusion.87
  309.0 2.7 fusion.87
  319.1 2.7 fusion.87
  329.2 2.7 fusion.87
  335.2 13.3 %fusion.24 = f32[128,8,8,128]{0,3,2,1:T(8,128)} fusion(f32[128,8,8,3]{0,2,3,1:T(8,128)S(1)} %copy.87, bf16[128,8,64,1,1]{0,2,4,3,1:T(8,128)(2,1)S(1)} %bitcast.165, f32[3,8,8,128,64]{4,3,2,1,0:T(8,128)} %reshape.308), kind=kOutput, calls=%fused_computation.21 | convolution fusion | flops 2421161984 | bytes 10715136 | tf_op jit(solution)/shard_map/tgn,sgkpn->sgktp/dot_general | solution.py:80
  348.5 274.5 %all-gather.11.cloned.1.call-done = f32[32,64,8192]{2,1,0:T(8,128)} async-done(((f32[1,64,8192]{2,1,0:T(8,128)}), f32[32,64,8192]{2,1,0:T(8,128)}) %all-gather.11.cloned.1.call-update) | async-done | bytes 67108880 | tf_op jit(solution)/shard_map/all_gather | solution.py:26
  623.0 82.8 %while.27 = (s32[]{:T(128)}, f32[64,8192]{1,0:T(8,128)S(1)}, s32[]{:T(128)}, f32[32,64]{1,0:T(8,128)S(1)}, f32[32,64,8192]{2,1,0:T(8,128)}, /*index=5*/s32[]{:T(128)}, s32[]{:T(128)}) while((s32[]{:T(128)}, f32[64,8192]{1,0:T(8,128)S(1)}, s32[]{:T(128)}, f32[32,64]{1,0:T(8,128)S(1)}, f32[32,64,8192]{2,1,0:T(8,128)}, ...), condition=%wide.region_6.7_spmd.clone, body=%wide.region_5.6_spmd.clone.sunk | while | flops 2097156 | bytes 6292337 | solution.py:38
  638.5 2.5 fusion.88
  705.8 3.0 reshape.309
  708.8 8.3 %fusion.29 = bf16[128,8,8,128]{0,3,2,1:T(8,128)(2,1)S(1)} fusion(f32[128,8,8,128]{0,3,2,1:T(8,128)} %fusion.24, f32[8,8,128,128]{2,3,1,0:T(8,128)} %fusion.32, bf16[128,8,8,128]{0,3,2,1:T(8,128)(2,1)} %bitcast.161, f32[8,8,128,64]{3,2,1,0:T(8,128)} %reshape.309, bf16[128,8,64,1]{0,2,3,1:T(8,128)(2,1)S(1)} %bitcast.166, f32[8,8]{1,0:T(8,128)S(1)} %mul.131, ...), kind=kOutput, calls=%fused_computation.28 | convolution fusion | flops 812646400 | bytes 14844160 | tf_op jit(solution)/shard_map/tgn,gkpn->tgkp/dot_general | solution.py:107
  717.2 2.9 copy.64
  (210 shorter events, 129.9 us)
Async XLA Ops:
  7.2 52.4 %copy-start.19 = (s32[1,3]{1,0:T(1,128)S(1)}, s32[1,3]{1,0:T(1,128)}, u32[]{:S(2)}) copy-start(s32[1,3]{1,0:T(1,128)} %param.29) | copy-start | bytes 40
  7.2 47.5 %all-gather.7.cloned.1.call-start = ((), (), s32[]{:S(2)}) async-start(), calls=%async_computation | async-start | bytes 1769472 | tf_op jit(solution)/shard_map/all_gather | solution.py:204
  7.9 132.1 %all-gather.9.cloned.1.call-start = ((), (), s32[]{:S(2)}) async-start(), calls=%async_computation.1 | async-start | bytes 8650752 | tf_op jit(solution)/shard_map/all_gather | solution.py:213
  58.2 6.5 copy-start.11
  58.2 209.1 %all-gather.13.cloned.1.call-start = ((), (), s32[]{:S(2)}) async-start(), calls=%async_computation.3 | async-start | bytes 1622016 | tf_op jit(solution)/shard_map/all_gather | solution.py:247
  59.0 221.4 %all-gather.15.cloned.1.call-start = ((), (), s32[]{:S(2)}) async-start(), calls=%async_computation.4 | async-start | bytes 1622016 | tf_op jit(solution)/shard_map/all_gather | solution.py:246
  59.5 563.4 %all-gather.11.cloned.1.call-start = ((), (), s32[]{:S(2)}) async-start(), calls=%async_computation.2 | async-start | bytes 69206016 | tf_op jit(solution)/shard_map/all_gather | solution.py:26
  59.8 5.0 copy-start.13
  61.4 7.1 copy-start.14
  64.7 107.9 %copy-start = (bf16[1,128,8192]{1,2,0:T(8,128)(2,1)}, bf16[1,128,8192]{1,2,0:T(8,128)(2,1)S(1)}, u32[]{:S(2)}) copy-start(bf16[1,128,8192]{1,2,0:T(8,128)(2,1)S(1)} %copy.54) | copy-start | bytes 6291460
  67.1 133.6 %copy-start.6 = (f32[8,8,128]{2,1,0:T(8,128)}, f32[8,8,128]{2,1,0:T(8,128)S(1)}, u32[]{:S(2)}) copy-start(f32[8,8,128]{2,1,0:T(8,128)S(1)} %reduce_window_sum.18) | copy-start | bytes 98308
  180.9 4.9 copy-start.3
  180.9 4.9 copy-start.4
  185.7 3.8 copy-start.17
  185.7 25.8 %copy-start.12 = (bf16[1,128,512]{2,1,0:T(8,128)(2,1)S(1)}, bf16[1,128,512]{2,1,0:T(8,128)(2,1)}, u32[]{:S(2)}) copy-start(bf16[1,128,512]{2,1,0:T(8,128)(2,1)} %param.25) | copy-start | bytes 393220
  185.7 26.0 %copy-start.18 = (f32[64]{0:T(128)S(1)}, f32[64]{0:T(128)}, u32[]{:S(2)}) copy-start(f32[64]{0:T(128)} %param.26) | copy-start | bytes 772
  185.7 26.1 %copy-start.15 = (bf16[1,3,4,512]{3,2,1,0:T(4,128)(2,1)S(1)}, bf16[1,3,4,512]{3,2,1,0:T(4,128)(2,1)}, u32[]{:S(2)}) copy-start(bf16[1,3,4,512]{3,2,1,0:T(4,128)(2,1)} %param.37) | copy-start | bytes 36868
  185.7 26.1 %copy-start.16 = (bf16[1,3,4,512]{3,2,1,0:T(4,128)(2,1)S(1)}, bf16[1,3,4,512]{3,2,1,0:T(4,128)(2,1)}, u32[]{:S(2)}) copy-start(bf16[1,3,4,512]{3,2,1,0:T(4,128)(2,1)} %param.36) | copy-start | bytes 36868
  185.8 9.5 %collective-permute-start = (bf16[2,128,512]{2,1,0:T(8,128)(2,1)S(1)}, bf16[2,128,512]{2,1,0:T(8,128)(2,1)S(1)}, u32[]{:S(2)}, u32[]{:S(2)}) collective-permute-start(bf16[2,128,512]{2,1,0:T(8,128)(2,1)S(1)} %pad_maximum_fusion), channel_id=1, source_target_pairs={{0,1},{1,2},{2,3},{3,4},{4,5},{5,6},{6,7},{7,8},{8,9},{9,10},{10,1... | collective-permute-start | bytes 786440 | tf_op jit(solution)/shard_map/ppermute | solution.py:44
  195.3 16.1 %copy-start.8 = (bf16[2,128,512]{2,1,0:T(8,128)(2,1)}, bf16[2,128,512]{2,1,0:T(8,128)(2,1)S(1)}, u32[]{:S(2)}) copy-start(bf16[2,128,512]{2,1,0:T(8,128)(2,1)S(1)} %collective-permute-done) | copy-start | bytes 786436
  195.4 10.6 %collective-permute-start.1 = (bf16[2,128,512]{2,1,0:T(8,128)(2,1)S(1)}, bf16[2,128,512]{2,1,0:T(8,128)(2,1)}, u32[]{:S(2)}, u32[]{:S(2)}) collective-permute-start(bf16[2,128,512]{2,1,0:T(8,128)(2,1)S(1)} %collective-permute-done), channel_id=1, source_target_pairs={{0,1},{1,2},{2,3},{3,4},{4,5},{5,6},{6,7},{7,8},{8,9},{9,10},{10,1... | collective-permute-start | bytes 786440 | tf_op jit(solution)/shard_map/ppermute | solution.py:44
  206.0 50.3 %collective-permute-start.2 = (bf16[2,128,512]{2,1,0:T(8,128)(2,1)}, bf16[2,128,512]{2,1,0:T(8,128)(2,1)}, u32[]{:S(2)}, u32[]{:S(2)}) collective-permute-start(bf16[2,128,512]{2,1,0:T(8,128)(2,1)} %collective-permute-done.1), channel_id=1, source_target_pairs={{0,1},{1,2},{2,3},{3,4},{4,5},{5,6},{6,7},{7,8},{8,9},{9,10},{10,1... | collective-permute-start | bytes 786440 | tf_op jit(solution)/shard_map/ppermute | solution.py:44
  211.5 48.0 %copy-start.7 = (f32[8,8,128]{2,1,0:T(8,128)S(1)}, f32[8,8,128]{2,1,0:T(8,128)}, u32[]{:S(2)}) copy-start(f32[8,8,128]{2,1,0:T(8,128)} %copy-done.6) | copy-start | bytes 98308
  256.3 10.0 %copy-start.9 = (bf16[2,128,512]{2,1,0:T(8,128)(2,1)S(1)}, bf16[2,128,512]{2,1,0:T(8,128)(2,1)}, u32[]{:S(2)}) copy-start(bf16[2,128,512]{2,1,0:T(8,128)(2,1)} %copy-done.8) | copy-start | bytes 786436
  256.3 7.9 %collective-permute-start.3 = (bf16[2,128,512]{2,1,0:T(8,128)(2,1)}, bf16[2,128,512]{2,1,0:T(8,128)(2,1)S(1)}, u32[]{:S(2)}, u32[]{:S(2)}) collective-permute-start(bf16[2,128,512]{2,1,0:T(8,128)(2,1)} %collective-permute-done.2), channel_id=1, source_target_pairs={{0,1},{1,2},{2,3},{3,4},{4,5},{5,6},{6,7},{7,8},{8,9},{9,10},{10,1... | collective-permute-start | bytes 786440 | tf_op jit(solution)/shard_map/ppermute | solution.py:44
  264.1 2.2 copy-start.5
  297.6 1.3 copy-start.1
  301.6 1.0 copy-start.2
  307.8 1.2 copy-start.1
  317.8 1.3 copy-start.1
  327.9 1.2 copy-start.1
  705.8 3.0 copy-start.10
  (3 other events, 3.1 us)
Sparse Core Ops, SparseCore 0:
  9.8 44.7 all-gather.6
  58.3 81.6 all-gather.8
  142.7 50.5 all-gather.12
  195.8 51.8 all-gather.14
  250.1 372.8 all-gather.10
where the time goes:
time: 734 us; the launch traced here: 727 us
  waiting for transfers between devices  400 us (54%)
  other arithmetic  103 us (14%)
  local copies, waits for them, and re-layouts  90.3 us (12%)
  matrix products  55.1 us (8%)
  blocking collectives  40.1 us (5%)
  starting transfers between devices  17.6 us (2%)
  between operations  14.3 us (2%)
    all_gather x1, waiting for transfers between devices, carried_in(): everything = jax.tree.map(lambda part: lax.all_gather(part, axis), array)  275 us
    select_n x32, other arithmetic, turn(): return jax.tree.map(lambda a, b: jnp.where(reached, a, b), new, before)  81.4 us
    all_gather x1, waiting for transfers between devices, shards(): gathered = lax.all_gather(restored, 'ctx', axis=1, tiled=True)  70.6 us
    all_gather x1, waiting for transfers between devices, shards(): piece = lax.all_gather(saved_states, 'sess', axis=0, tiled=True)  45.8 us
    all_gather x1, blocking collectives, carried_in(): everything = jax.tree.map(lambda part: lax.all_gather(part, axis), array)  40.1 us
    ppermute x4, starting transfers between devices, shifted(): return lax.ppermute(block, axis, route)  17.4 us
  transfers between devices with their start and end apart: 9, of which 5 were waited for; matrix products, arithmetic and copies ran while one was open for 20% of the time, Pallas kernels for 0%

commit v1 on v0

v1 whole, which is shorter than its diff:
```python
import functools
import math

import jax
import jax.numpy as jnp
from jax import lax
from jax.experimental import pallas as pl
from jax.experimental.pallas import tpu as pltpu
from jax.sharding import PartitionSpec as P

TOK = 128
REACH = 4
SEQS = 3
SINKS = 4
H = 64
P_SIZE = 128
N = 64
G = 8
QH = 32
KVH = 4
HD = 128
WINDOW = 512
CTX = 32

F32 = jnp.float32
BF16 = jnp.bfloat16
I32 = jnp.int32
PAIR = 2 * P_SIZE
ROWS = N + 16
STEPS = 4
HEADS = H // STEPS
WIDE = HEADS * P_SIZE
BLOCKS = REACH + 1 + 1 + SEQS * 4 + 1
SINK_BLOCK = REACH + 1
CACHE_BLOCK = SINK_BLOCK + 1
NULL_BLOCK = BLOCKS - 1


def iota(shape, axis):
    return lax.broadcasted_iota(I32, shape, axis)


def nn(a, b):
    return lax.dot_general(a, b, (((1,), (0,)), ((), ())), preferred_element_type=F32)


def nt(a, b):
    return lax.dot_general(a, b, (((1,), (1,)), ((), ())), preferred_element_type=F32)


def starts_of(lengths):
    first = lengths[0, 0]
    return first, first + lengths[0, 1]


def segment(positions, one, two):
    return (positions >= one).astype(I32) + (positions >= two).astype(I32)


def same_causal(one, two):
    t, u = iota((TOK, TOK), 0), iota((TOK, TOK), 1)
    return (segment(t, one, two) == segment(u, one, two)) & (t >= u)


def spread_matrix(step):
    rows = iota((H, WIDE), 0)
    lanes = iota((H, WIDE), 1)
    return jnp.where(rows == step * HEADS + lanes // P_SIZE, 1.0, 0.0).astype(BF16)


def summary_kernel(lengths, x, dt, dlog, write, send, weight):
    step = pl.program_id(0)
    first = lax.axis_index("ctx") * TOK
    one, two = starts_of(lengths)
    one, two = one - first, two - first
    mask = jnp.where(same_causal(one, two), 1.0, 0.0).astype(BF16)
    rates = dlog[...]

    @pl.when(step == 0)
    def _():
        run = nn(mask, rates).T
        u = iota((1, TOK), 1)
        last = (TOK - 1 >= one).astype(I32) + (TOK - 1 >= two).astype(I32)
        held = segment(u, one, two) == last
        gap = jnp.where(held, run[:, TOK - 1 :] - run, -jnp.inf)
        weight[...] = jnp.exp(gap) * dt[...].astype(F32).T

    turned = write[...].astype(F32).T
    for k in range(HEADS):
        row = weight[pl.ds(step * HEADS + k, 1), :]
        b = k // G
        loads = (row * turned[b * N : (b + 1) * N]).astype(BF16)
        made = nn(loads, x[:, k * P_SIZE : (k + 1) * P_SIZE])
        lane = (k % 2) * P_SIZE
        send[k // 2, :N, lane : lane + P_SIZE] = made.astype(BF16)
    spread = nn(rates, spread_matrix(step)).astype(BF16)
    carry = jnp.exp(nn(mask[TOK - 16 :], spread)[15:16])
    high = carry.astype(BF16).astype(F32)
    low = carry - high
    tile = iota((16, PAIR), 0)
    for j in range(HEADS // 2):
        lanes = slice(j * PAIR, (j + 1) * PAIR)
        part = jnp.where(tile == 0, high[:, lanes], jnp.where(tile == 1, low[:, lanes], 0.0))
        send[j, N:, :] = part.astype(BF16)


def scan_kernel(home, lengths, recv, stored, entering, extra):
    group = lax.axis_index("sess")
    one, two = starts_of(lengths)
    back = [stored[home[group * SEQS + s]].astype(F32) for s in range(SEQS)]
    extra[0] = back[1].astype(BF16)
    extra[1] = back[2].astype(BF16)

    def turn(c, state):
        entering[c] = state.astype(BF16)
        end = c * TOK + TOK - 1
        inside_one = (end >= one) & (end < two) & (one >= c * TOK)
        inside_two = (end >= two) & (two >= c * TOK)
        base = jnp.where(inside_two, back[2], jnp.where(inside_one, back[1], state))
        carry = recv[c, N : N + 16, :].astype(F32)
        return (carry[0:1] + carry[1:2]) * base + recv[c, :N, :].astype(F32)

    lax.fori_loop(0, CTX, turn, back[0])


def output_kernel(lengths, x, dt, dlog, write, read, gain, state, extra, out, run_rows, step_rows):
    step = pl.program_id(0)
    first = lax.axis_index("ctx") * TOK
    one, two = starts_of(lengths)
    one, two = one - first, two - first
    seen = same_causal(one, two)
    mask = jnp.where(seen, 1.0, 0.0).astype(BF16)
    bias = jnp.where(seen, 0.0, -jnp.inf)
    rates = dlog[...]

    @pl.when(step == 0)
    def _():
        run_rows[...] = nn(mask, rates).T
        step_rows[...] = dt[...].astype(F32).T

    t = iota((TOK, N), 0)
    new_one = (t >= one) & (t < two) & (one >= 0)
    new_two = (t >= two) & (two >= 0)
    spread = nn(rates, spread_matrix(step)).astype(BF16)
    run = nn(mask, spread)
    for b in range(HEADS // G):
        c = read[:, b * N : (b + 1) * N].astype(F32)
        c_in = jnp.where(new_one | new_two, 0.0, c).astype(BF16)
        c_one = jnp.where(new_one, c, 0.0).astype(BF16)
        c_two = jnp.where(new_two, c, 0.0).astype(BF16)
        both = nt(read[:, b * N : (b + 1) * N], write[:, b * N : (b + 1) * N])
        for j in range(G // 2):
            chunk = b * (G // 2) + j
            from_state = (
                nn(c_in, state[chunk]) + nn(c_one, extra[chunk, 0]) + nn(c_two, extra[chunk, 1])
            )
            for i in range(2):
                k = chunk * 2 + i
                lanes = slice(k * P_SIZE, (k + 1) * P_SIZE)
                at = pl.ds(step * HEADS + k, 1)
                run_t = run[:, lanes]
                decay = jnp.exp(run_t - run_rows[at, :] + bias)
                mixing = (both * decay * step_rows[at, :]).astype(BF16)
                x_h = x[:, lanes]
                result = (
                    nn(mixing, x_h)
                    + jnp.exp(run_t) * from_state[:, i * P_SIZE : (i + 1) * P_SIZE]
                    + gain[:, lanes] * x_h.astype(F32)
                )
                out[:, lanes] = result.astype(BF16)


def attention_kernel(
    lengths,
    history,
    queries,
    band,
    sinks,
    cache,
    out,
    keys,
    rows,
    scores,
    top,
    total,
    sums,
    bias,
    listed,
    sems,
):
    place = lax.axis_index("ctx")
    first = place * TOK
    one, two = starts_of(lengths)
    copies = [
        pltpu.make_async_copy(band, keys.at[pl.ds(0, 8 * SINK_BLOCK)], sems.at[0]),
        pltpu.make_async_copy(sinks, keys.at[pl.ds(8 * SINK_BLOCK, 8)], sems.at[1]),
    ]
    for s in range(SEQS):
        for kv in range(2):
            copies.append(
                pltpu.make_async_copy(
                    cache.at[:, kv, s],
                    keys.at[pl.ds(8 * CACHE_BLOCK + 32 * s, 32), :, pl.ds(kv * KVH * HD, KVH * HD)],
                    sems.at[2 + 2 * s + kv],
                )
            )
    for copy in copies:
        copy.start()
    keys[8 * NULL_BLOCK :] = jnp.zeros((8, 16, 2 * KVH * HD), BF16)

    t = first + iota((TOK, TOK), 0)
    u = iota((TOK, TOK), 1)
    owner = segment(t, one, two)
    offset = t - jnp.where(owner == 2, two, jnp.where(owner == 1, one, 0))
    count = jnp.int32(0)
    head_owner = (first >= one).astype(I32) + (first >= two).astype(I32)
    for b in range(REACH + 1):
        pos = first + (b - REACH) * TOK + u
        gap = t - pos
        ok = (pos >= 0) & (segment(pos, one, two) == owner) & (gap >= 0) & (gap < WINDOW)
        bias[b] = jnp.where(ok, 0.0, -jnp.inf)
        end = first + (b - REACH) * TOK + TOK - 1
        end_owner = (end >= one).astype(I32) + (end >= two).astype(I32)
        live = (end >= 0) & (end_owner >= head_owner)
        listed[count] = b
        count = count + live.astype(I32)
    bias[SINK_BLOCK] = jnp.where(
        (u < SEQS * SINKS) & (u // SINKS == owner), 0.0, -jnp.inf
    )
    listed[count] = SINK_BLOCK
    count = count + 1
    edges = [jnp.int32(0), one, two, jnp.int32(CTX * TOK)]
    for s in range(SEQS):
        begin = jnp.maximum(edges[s], first)
        present = begin < jnp.minimum(edges[s + 1], first + TOK)
        for j in range(4):
            live = (
                present
                & (begin - edges[s] < j * TOK + TOK - 1)
                & (history[0, s] - WINDOW + j * TOK + TOK - 1 >= SINKS)
            )
            block = CACHE_BLOCK + 4 * s + j

            @pl.when(live)
            def _():
                slot = j * TOK + u
                ok = (owner == s) & (slot > offset) & (history[0, s] - WINDOW + slot >= SINKS)
                bias[block] = jnp.where(ok, 0.0, -jnp.inf)

            listed[count] = block
            count = count + live.astype(I32)
    bias[NULL_BLOCK] = jnp.full((TOK, TOK), -jnp.inf, F32)
    listed[count] = NULL_BLOCK
    pairs = lax.div(count + 1, jnp.int32(2))
    for copy in copies:
        copy.wait()

    per = QH // KVH
    scale = 1.0 / math.sqrt(HD) / math.log(2.0)

    def one_head(number, nothing):
        lanes = pl.ds(pl.multiple_of(number * HD, HD), HD)
        value_lanes = pl.ds(pl.multiple_of(number * HD + KVH * HD, HD), HD)
        for r in range(per):
            wide = pl.ds(pl.multiple_of((number * per + r) * HD, HD), HD)
            rows[r * TOK : (r + 1) * TOK, :] = queries[:, wide]
        top[...] = jnp.full(top.shape, -jnp.inf, F32)
        total[...] = jnp.zeros(total.shape, F32)
        sums[...] = jnp.zeros(sums.shape, F32)

        def score(i, nothing):
            for part in range(2):
                block = listed[2 * i + part]
                key = keys[pl.ds(block * 8, 8), :, lanes].reshape(TOK, HD)
                offset_rows = bias[block]
                for r in range(per):
                    at = slice(r * TOK, (r + 1) * TOK)
                    got = nt(rows[at, :], key) * scale + offset_rows
                    scores[2 * i + part, at, :] = got
                    top[at, :] = jnp.maximum(top[at, :], got)
            return nothing

        lax.fori_loop(0, pairs, score, 0)
        top[...] = jnp.broadcast_to(jnp.max(top[...], axis=1, keepdims=True), top.shape)

        def weigh(i, nothing):
            values = []
            for part in range(2):
                block = listed[2 * i + part]
                values.append(keys[pl.ds(block * 8, 8), :, value_lanes].reshape(TOK, HD))
            value = jnp.concatenate(values, axis=0)
            for r in range(per):
                at = slice(r * TOK, (r + 1) * TOK)
                left = jnp.exp2(scores[2 * i, at, :] - top[at, :])
                right = jnp.exp2(scores[2 * i + 1, at, :] - top[at, :])
                total[at, :] += left + right
                both = jnp.concatenate([left.astype(BF16), right.astype(BF16)], axis=1)
                sums[at, :] += nn(both, value)
            return nothing

        lax.fori_loop(0, pairs, weigh, 0)
        for r in range(per):
            at = slice(r * TOK, (r + 1) * TOK)
            whole = jnp.sum(total[at, :], axis=1, keepdims=True)
            wide = pl.ds(pl.multiple_of((number * per + r) * HD, HD), HD)
            out[:, wide] = (sums[at, :] / whole).astype(BF16)
        return nothing

    lax.fori_loop(0, KVH, one_head, 0)


SMEM = pl.BlockSpec(memory_space=pltpu.SMEM)
VMEM = pl.BlockSpec(memory_space=pltpu.VMEM)
ANY = pl.BlockSpec(memory_space=pl.ANY)
LIMIT = pltpu.CompilerParams(vmem_limit_bytes=48 * 2**20)


def full(shape):
    return pl.BlockSpec(shape, lambda i: (0,) * len(shape))


def lane_block(rows, width):
    return pl.BlockSpec((rows, width), lambda i: (0, i))


def summaries(lengths, x, dt, dlog, write):
    return pl.pallas_call(
        summary_kernel,
        grid=(STEPS,),
        out_shape=jax.ShapeDtypeStruct((CTX, ROWS, PAIR), BF16),
        in_specs=[
            SMEM,
            lane_block(TOK, WIDE),
            full((TOK, H)),
            full((TOK, H)),
            lane_block(TOK, 2 * N),
        ],
        out_specs=pl.BlockSpec((CTX // STEPS, ROWS, PAIR), lambda i: (i, 0, 0)),
        scratch_shapes=[pltpu.VMEM((H, TOK), F32)],
        compiler_params=LIMIT,
    )(lengths, x, dt, dlog, write)


def scan(home, lengths, recv, stored):
    return pl.pallas_call(
        scan_kernel,
        out_shape=(
            jax.ShapeDtypeStruct((CTX, N, PAIR), BF16),
            jax.ShapeDtypeStruct((2, N, PAIR), BF16),
        ),
        in_specs=[SMEM, SMEM, VMEM, VMEM],
        out_specs=(VMEM, VMEM),
        compiler_params=LIMIT,
    )(home, lengths, recv, stored)


def outputs(lengths, x, dt, dlog, write, read, gain, state, extra):
    return pl.pallas_call(
        output_kernel,
        grid=(STEPS,),
        out_shape=jax.ShapeDtypeStruct((TOK, H * P_SIZE), BF16),
        in_specs=[
            SMEM,
            lane_block(TOK, WIDE),
            full((TOK, H)),
            full((TOK, H)),
            lane_block(TOK, 2 * N),
            lane_block(TOK, 2 * N),
            lane_block(1, WIDE),
            pl.BlockSpec((CTX // STEPS, N, PAIR), lambda i: (i, 0, 0)),
            pl.BlockSpec((CTX // STEPS, 2, N, PAIR), lambda i: (i, 0, 0, 0)),
        ],
        out_specs=lane_block(TOK, WIDE),
        scratch_shapes=[pltpu.VMEM((H, TOK), F32), pltpu.VMEM((H, TOK), F32)],
        compiler_params=LIMIT,
    )(lengths, x, dt, dlog, write, read, gain, state, extra)


def attention(lengths, history, queries, band, sinks, cache):
    rows = (QH // KVH) * TOK
    return pl.pallas_call(
        attention_kernel,
        out_shape=jax.ShapeDtypeStruct((TOK, QH * HD), BF16),
        in_specs=[SMEM, SMEM, VMEM, ANY, ANY, ANY],
        out_specs=VMEM,
        scratch_shapes=[
            pltpu.VMEM((8 * BLOCKS, 16, 2 * KVH * HD), BF16),
            pltpu.VMEM((rows, HD), BF16),
            pltpu.VMEM((BLOCKS + 1, rows, TOK), F32),
            pltpu.VMEM((rows, TOK), F32),
            pltpu.VMEM((rows, TOK), F32),
            pltpu.VMEM((rows, HD), F32),
            pltpu.VMEM((BLOCKS, TOK, TOK), F32),
            pltpu.SMEM((BLOCKS + 1,), I32),
            pltpu.SemaphoreType.DMA((8,)),
        ],
        compiler_params=LIMIT,
        cost_estimate=pl.CostEstimate(
            flops=2_500_000_000, bytes_accessed=8_000_000, transcendentals=5_000_000
        ),
    )(lengths, history, queries, band, sinks, cache)


def shifted(block, distance):
    route = [(i - distance, i) for i in range(distance, CTX)]
    return lax.ppermute(block, "ctx", route)


def shards(
    mamba_input,
    step_size,
    decay_log,
    state_write,
    state_read,
    skip_gain,
    saved_states,
    home_slot,
    turn_lengths,
    history_lengths,
    queries,
    turn_keys,
    turn_values,
    cache_keys,
    cache_values,
    sink_keys,
    sink_values,
):
    x, dt, dlog = mamba_input[0], step_size[0], decay_log[0]
    write, read = state_write[0], state_read[0]
    saved = saved_states[0].astype(BF16).reshape(SEQS, 2, P_SIZE, N)
    saved = saved.transpose(0, 3, 1, 2).reshape(SEQS, N, PAIR)
    stored = lax.all_gather(saved, "sess", axis=0, tiled=True)
    cache = jnp.stack([cache_keys[0], cache_values[0]])
    cache = lax.all_gather(cache, "ctx", axis=0)
    key_value = jnp.concatenate([turn_keys[0], turn_values[0]], axis=1)
    band = [shifted(key_value, d) for d in range(REACH, 0, -1)] + [key_value]
    band = jnp.concatenate(band, axis=0).reshape(8 * (REACH + 1), 16, 2 * KVH * HD)
    sinks = jnp.concatenate(
        [sink_keys[0].reshape(SEQS * SINKS, -1), sink_values[0].reshape(SEQS * SINKS, -1)], axis=1
    )
    sinks = jnp.pad(sinks, ((0, TOK - SEQS * SINKS), (0, 0))).reshape(8, 16, 2 * KVH * HD)
    gain = jnp.repeat(skip_gain, P_SIZE)[None]

    send = summaries(turn_lengths, x, dt, dlog, write)
    recv = lax.all_to_all(send, "ctx", 0, 0, tiled=True)
    entering, extra = scan(home_slot, turn_lengths, recv, stored)
    state = lax.all_to_all(entering, "ctx", 0, 0, tiled=True)
    extras = lax.all_gather(extra, "ctx", axis=0)
    attended = attention(turn_lengths, history_lengths, queries[0], band, sinks, cache)
    mixed = outputs(turn_lengths, x, dt, dlog, write, read, gain, state, extras)
    return (mixed[None], attended[None])


def solution(mesh):
    token = P("sess", "ctx", None)
    spread = P("sess", None, "ctx", None)
    return jax.shard_map(
        shards,
        mesh=mesh,
        in_specs=(
            token,
            token,
            token,
            token,
            token,
            P(),
            spread,
            P(),
            P("sess", None),
            P("sess", None),
            token,
            token,
            token,
            spread,
            spread,
            P("sess", None, None, None),
            P("sess", None, None, None),
        ),
        out_specs=(token, token),
        check_vma=False,
    )
```

time: 734 us -> 222 us (0.30)
  waiting for transfers between devices: 400 us -> 51.4 us
  other arithmetic: 103 us -> 2.31 us
  local copies, waits for them, and re-layouts: 90.3 us -> 15.3 us
  matrix products: 55.1 us -> 0 us
  Pallas kernels: 0 us -> 28.3 us
  starting transfers between devices: 17.6 us -> 43.6 us
  blocking collectives: 40.1 us -> 63 us
    all_gather x5 -> x2, waiting for transfers between devices: 391 us -> 10 us  [the longest x1 10 us: shards(): extras = lax.all_gather(extra, 'ctx', axis=0)]
    select_n x35 -> x0, other arithmetic: 82 us -> none  [the longest x32 81.4 us: turn(): return jax.tree.map(lambda a, b: jnp.where(reached, a, b), new, before)]
    dot_general x14 -> x0, matrix products: 55.1 us -> none  [the longest x1 13.3 us: stretch_terms(): jnp.einsum('tgn,sgkpn->sgktp', read_float, states, precision=precise)]
    ppermute x4, waiting for transfers between devices: 7.53 us -> 41.3 us  [shifted(): return lax.ppermute(block, 'ctx', route)]
    pallas_call x0 -> x4, Pallas kernels: none -> 28.3 us  [the longest x1 14.4 us: attention(): pl.pallas_call(attention_kernel, out_shape=jax.ShapeDtypeStruct((TOK, QH...]
    concatenate x4 -> x0, local copies, waits for them, and re-layouts: 27 us -> none  [the longest x1 13 us: shards(): jnp.concatenate([sink_values[0].reshape(SEQS * SINKS, features), history_...]
    all_to_all x0 -> x2, starting transfers between devices: none -> 26.4 us  [the longest x1 15.3 us: shards(): state = lax.all_to_all(entering, 'ctx', 0, 0, tiled=True)]
    all_gather x1, blocking collectives: 40.1 us -> 63 us  [shards(): stored = lax.all_gather(saved, 'sess', axis=0, tiled=True)]
  transfers between devices with their start and end apart: 9 -> 8, of which waited for: 5 -> 4; matrix products, arithmetic and copies ran while one was open for 20% -> 2% of each run, Pallas kernels for 0% -> 10%
where the time goes in v1:
time: 222 us; the launch traced here: 218 us
  blocking collectives  63 us (28%)
  waiting for transfers between devices  51.4 us (23%)
  starting transfers between devices  43.6 us (20%)
  Pallas kernels  28.3 us (13%)
  local copies, waits for them, and re-layouts  15.3 us (7%)
  between operations  14.3 us (6%)
  other arithmetic  2.31 us (1%)
    all_gather x1, blocking collectives, shards(): stored = lax.all_gather(saved, 'sess', axis=0, tiled=True)  63 us
    ppermute x4, waiting for transfers between devices, shifted(): return lax.ppermute(block, 'ctx', route)  41.3 us
    ppermute x4, starting transfers between devices, shifted(): return lax.ppermute(block, 'ctx', route)  17.1 us
    all_to_all x1, starting transfers between devices, shards(): state = lax.all_to_all(entering, 'ctx', 0, 0, tiled=True)  15.3 us
    unnamed x48, local copies, waits for them, and re-layouts  14.9 us
    pallas_call x1, Pallas kernels, attention(): pl.pallas_call(attention_kernel, out_shape=jax.ShapeDtypeStruct((TOK, QH...  14.4 us
    all_to_all x1, starting transfers between devices, shards(): recv = lax.all_to_all(send, 'ctx', 0, 0, tiled=True)  11.2 us
    all_gather x1, waiting for transfers between devices, shards(): extras = lax.all_gather(extra, 'ctx', axis=0)  10 us
  transfers between devices with their start and end apart: 8, of which 4 were waited for; matrix products, arithmetic and copies ran while one was open for 2% of the time, Pallas kernels for 10%

profile of v1, /device:TPU:33, one launch (start us, length us, event | category | flops | bytes accessed | tf_op | source)
XLA Modules:
  0.0 218.1 jit_solution(254814835002661101)
XLA Ops:
  7.2 1.5 pad_maximum_fusion.1
  8.7 0.8 copy.25
  9.5 0.8 copy.26
  10.4 1.6 copy-done
  12.0 0.9 copy-done.3
  12.9 0.7 copy-done.9
  13.5 4.3 %shard_map.176 = bf16[32,80,256]{2,1,0:T(8,128)(2,1)} custom-call(s32[1,3]{1,0:T(1,128)S(1)} %copy-done.9, bf16[128,8192]{1,0:T(8,128)(2,1)S(1)} %bitcast.18, bf16[128,64]{1,0:T(8,128)(2,1)S(1)} %bitcast.23, bf16[128,64]{1,0:T(8,128)(2,1)S(1)} %bitcast.25, bf16[128,512]{1,0:T(8,128)(2,1)S(1)} %bitcast.21), custom_call_target="tpu_custom_call" | custom-call | tf_op jit(solution)/shard_map/pallas_call | solution.py:327
  17.8 11.2 %all-to-all-start = ((bf16[32,80,256]{2,1,0:T(8,128)(2,1)}), bf16[32,80,256]{2,1,0:T(8,128)(2,1)S(1)}, u32[]{:S(2)}, u32[]{:S(2)}) async-start(bf16[32,80,256]{2,1,0:T(8,128)(2,1)} %shard_map.176), calls=%async_computation | async-start | bytes 2621440 | tf_op jit(solution)/shard_map/all_to_all | solution.py:445
  29.2 0.2 convert_element_type.10
  29.4 0.1 copy.27
  29.5 63.0 %all_gather.15.stored = bf16[24,64,256]{2,1,0:T(8,128)(2,1)S(1)} all-gather(bf16[3,64,256]{2,1,0:T(8,128)(2,1)S(1)} %copy.27), channel_id=1, replica_groups=mesh['sess'=8,'ctx'=32] {'sess'}, dimensions={0}, use_global_device_ids=true | all-gather | bytes 884736 | tf_op jit(solution)/shard_map/all_gather | solution.py:432
  92.5 2.3 %shard_map.177 = (bf16[32,64,256]{2,1,0:T(8,128)(2,1)}, bf16[2,64,256]{2,1,0:T(8,128)(2,1)}) custom-call(s32[24]{0:T(128)S(1)} %copy-done.11, s32[1,3]{1,0:T(1,128)S(1)} %copy-done.10, bf16[32,80,256]{2,1,0:T(8,128)(2,1)S(1)} %all-to-all-done.recv, bf16[24,64,256]{2,1,0:T(8,128)(2,1)S(1)} %all_gather.15.stored), custom_call_target="tpu_custom_call" | custom-call | tf_op jit(solution)/shard_map/pallas_call | solution.py:345
  94.9 15.3 %all-to-all-start.1 = ((bf16[32,64,256]{2,1,0:T(8,128)(2,1)}), bf16[32,64,256]{2,1,0:T(8,128)(2,1)S(1)}, u32[]{:S(2)}, u32[]{:S(2)}) async-start(bf16[32,64,256]{2,1,0:T(8,128)(2,1)} %get-tuple-element.4), calls=%async_computation.1 | async-start | bytes 2097152 | tf_op jit(solution)/shard_map/all_to_all | solution.py:447
  110.2 7.9 %collective-permute-start = (bf16[128,1024]{1,0:T(8,128)(2,1)S(1)}, bf16[128,1024]{1,0:T(8,128)(2,1)}, u32[]{:S(2)}, u32[]{:S(2)}) collective-permute-start(bf16[128,1024]{1,0:T(8,128)(2,1)S(1)} %pad_maximum_fusion), channel_id=1, source_target_pairs={{0,4},{1,5},{2,6},{3,7},{4,8},{5,9},{6,10},{7,11},{8,12},{9,13},{1... | collective-permute-start | bytes 786440 | tf_op jit(solution)/shard_map/ppermute | solution.py:406
  118.1 3.6 %collective-permute-start.1 = (bf16[128,1024]{1,0:T(8,128)(2,1)S(1)}, bf16[128,1024]{1,0:T(8,128)(2,1)}, u32[]{:S(2)}, u32[]{:S(2)}) collective-permute-start(bf16[128,1024]{1,0:T(8,128)(2,1)S(1)} %pad_maximum_fusion), channel_id=1, source_target_pairs={{0,3},{1,4},{2,5},{3,6},{4,7},{5,8},{6,9},{7,10},{8,11},{9,12},{10... | collective-permute-start | bytes 786440 | tf_op jit(solution)/shard_map/ppermute | solution.py:406
  121.7 3.3 %collective-permute-start.2 = (bf16[128,1024]{1,0:T(8,128)(2,1)S(1)}, bf16[128,1024]{1,0:T(8,128)(2,1)S(1)}, u32[]{:S(2)}, u32[]{:S(2)}) collective-permute-start(bf16[128,1024]{1,0:T(8,128)(2,1)S(1)} %pad_maximum_fusion), channel_id=1, source_target_pairs={{0,2},{1,3},{2,4},{3,5},{4,6},{5,7},{6,8},{7,9},{8,10},{9,11},{10,... | collective-permute-start | bytes 786440 | tf_op jit(solution)/shard_map/ppermute | solution.py:406
  125.0 2.2 %collective-permute-start.3 = (bf16[128,1024]{1,0:T(8,128)(2,1)S(1)}, bf16[128,1024]{1,0:T(8,128)(2,1)S(1)}, u32[]{:S(2)}, u32[]{:S(2)}) collective-permute-start(bf16[128,1024]{1,0:T(8,128)(2,1)S(1)} %pad_maximum_fusion), channel_id=1, source_target_pairs={{0,1},{1,2},{2,3},{3,4},{4,5},{5,6},{6,7},{7,8},{8,9},{9,10},{10,1... | collective-permute-start | bytes 786440 | tf_op jit(solution)/shard_map/ppermute | solution.py:406
  127.3 0.7 fusion.2
  128.0 17.0 %collective-permute-done = bf16[128,1024]{1,0:T(8,128)(2,1)} collective-permute-done((bf16[128,1024]{1,0:T(8,128)(2,1)S(1)}, bf16[128,1024]{1,0:T(8,128)(2,1)}, u32[]{:S(2)}, u32[]{:S(2)}) %collective-permute-start) | collective-permute-done | bytes 262176 | tf_op jit(solution)/shard_map/ppermute | solution.py:406
  145.0 1.0 constant_dynamic-update-slice_fusion.4
  146.0 6.2 %collective-permute-done.1 = bf16[128,1024]{1,0:T(8,128)(2,1)} collective-permute-done((bf16[128,1024]{1,0:T(8,128)(2,1)S(1)}, bf16[128,1024]{1,0:T(8,128)(2,1)}, u32[]{:S(2)}, u32[]{:S(2)}) %collective-permute-start.1) | collective-permute-done | bytes 262176 | tf_op jit(solution)/shard_map/ppermute | solution.py:406
  152.2 1.0 constant_dynamic-update-slice_fusion.3
  153.2 18.1 %collective-permute-done.3 = bf16[128,1024]{1,0:T(8,128)(2,1)S(1)} collective-permute-done((bf16[128,1024]{1,0:T(8,128)(2,1)S(1)}, bf16[128,1024]{1,0:T(8,128)(2,1)S(1)}, u32[]{:S(2)}, u32[]{:S(2)}) %collective-permute-start.3) | collective-permute-done | bytes 262176 | tf_op jit(solution)/shard_map/ppermute | solution.py:406
  171.4 1.0 copy-done.7
  172.4 0.9 copy-done.5
  173.4 1.3 copy-done.8
  174.7 1.9 copy-done.12
  176.6 1.2 copy-done.13
  177.8 14.4 %shard_map.179 = bf16[128,4096]{1,0:T(8,128)(2,1)} custom-call(s32[1,3]{1,0:T(1,128)S(1)} %copy-done.10, s32[1,3]{1,0:T(1,128)S(1)} %copy-done.14, bf16[128,4096]{1,0:T(8,128)(2,1)S(1)} %bitcast.32, bf16[40,16,1024]{2,1,0:T(8,128)(2,1)S(1)} %bitcast.30, bf16[8,16,1024]{2,1,0:T(8,128)(2,1)S(1)} %bitcast.27, bf16[32,2,3,16,512]{4,3,2,1,0:T(8,128)(2,1)S(1)} %bitcast.31), custom_call_target="tpu_custom_call" | custom-call | flops 2500000000 | bytes 8000000 | tf_op jit(solution)/shard_map/pallas_call | solution.py:381
  192.3 10.0 %all-gather.5.cloned.1.call-done = bf16[64,64,256]{2,1,0:T(8,128)(2,1)} async-done(((bf16[2,64,256]{2,1,0:T(8,128)(2,1)}), bf16[64,64,256]{2,1,0:T(8,128)(2,1)}) %all-gather.5.cloned.1.call-update) | async-done | bytes 2097168 | tf_op jit(solution)/shard_map/all_gather | solution.py:448
  202.4 1.6 copy-done.2
  204.0 7.2 %shard_map.178 = bf16[128,8192]{1,0:T(8,128)(2,1)} custom-call(s32[1,3]{1,0:T(1,128)S(1)} %copy-done.10, bf16[128,8192]{1,0:T(8,128)(2,1)S(1)} %bitcast.19, bf16[128,64]{1,0:T(8,128)(2,1)S(1)} %bitcast.24, bf16[128,64]{1,0:T(8,128)(2,1)S(1)} %bitcast.26, bf16[128,512]{1,0:T(8,128)(2,1)S(1)} %bitcast.22, bf16[128,512]{1,0:T(8,128)(2,1)S(1)} %bitcast.28, ...), custom_call_target="tpu_custom_call" | custom-call | tf_op jit(solution)/shard_map/pallas_call | solution.py:358
  (49 shorter events, 0.4 us)
Async XLA Ops:
  7.2 165.3 %all-gather.7.cloned.1.call-start = ((), (), s32[]{:S(2)}) async-start(), calls=%async_computation.3 | async-start | bytes 3244032 | tf_op jit(solution)/shard_map/all_gather | solution.py:434
  10.4 1.6 copy-start
  12.0 0.9 copy-start.3
  12.9 0.7 copy-start.9
  17.8 11.2 %copy-start.17 = (f32[1,3,2,8192]{3,2,1,0:T(2,128)S(1)}, f32[1,3,2,8192]{3,2,1,0:T(2,128)}, u32[]{:S(2)}) copy-start(f32[1,3,2,8192]{3,2,1,0:T(2,128)} %param.23) | copy-start | bytes 589828
  17.8 74.7 %all-to-all-start = ((bf16[32,80,256]{2,1,0:T(8,128)(2,1)}), bf16[32,80,256]{2,1,0:T(8,128)(2,1)S(1)}, u32[]{:S(2)}, u32[]{:S(2)}) async-start(bf16[32,80,256]{2,1,0:T(8,128)(2,1)} %shard_map.176), calls=%async_computation | async-start | bytes 2621440 | tf_op jit(solution)/shard_map/all_to_all | solution.py:445
  29.0 63.5 %copy-start.10 = (s32[1,3]{1,0:T(1,128)S(1)}, s32[1,3]{1,0:T(1,128)}, u32[]{:S(2)}) copy-start(s32[1,3]{1,0:T(1,128)} %lengths.7) | copy-start | bytes 40
  29.0 63.5 %copy-start.11 = (s32[24]{0:T(128)S(1)}, s32[24]{0:T(128)}, u32[]{:S(2)}) copy-start(s32[24]{0:T(128)} %home.1) | copy-start | bytes 292
  29.0 173.3 %all-gather.5.cloned.1.call-start = ((), (), s32[]{:S(2)}) async-start(), calls=%async_computation.2 | async-start | bytes 2162688 | tf_op jit(solution)/shard_map/all_gather | solution.py:448
  94.8 15.3 %copy-start.15 = (bf16[1,128,512]{2,1,0:T(8,128)(2,1)S(1)}, bf16[1,128,512]{2,1,0:T(8,128)(2,1)}, u32[]{:S(2)}) copy-start(bf16[1,128,512]{2,1,0:T(8,128)(2,1)} %param.29) | copy-start | bytes 393220
  94.8 15.3 %copy-start.16 = (bf16[1,128,512]{2,1,0:T(8,128)(2,1)S(1)}, bf16[1,128,512]{2,1,0:T(8,128)(2,1)}, u32[]{:S(2)}) copy-start(bf16[1,128,512]{2,1,0:T(8,128)(2,1)} %param.28) | copy-start | bytes 393220
  94.8 32.4 %copy-start.18 = (bf16[1,3,4,512]{3,2,1,0:T(4,128)(2,1)S(1)}, bf16[1,3,4,512]{3,2,1,0:T(4,128)(2,1)}, u32[]{:S(2)}) copy-start(bf16[1,3,4,512]{3,2,1,0:T(4,128)(2,1)} %param.32) | copy-start | bytes 36868
  94.8 32.4 %copy-start.19 = (bf16[1,3,4,512]{3,2,1,0:T(4,128)(2,1)S(1)}, bf16[1,3,4,512]{3,2,1,0:T(4,128)(2,1)}, u32[]{:S(2)}) copy-start(bf16[1,3,4,512]{3,2,1,0:T(4,128)(2,1)} %param.33) | copy-start | bytes 36868
  94.9 97.4 %all-to-all-start.1 = ((bf16[32,64,256]{2,1,0:T(8,128)(2,1)}), bf16[32,64,256]{2,1,0:T(8,128)(2,1)S(1)}, u32[]{:S(2)}, u32[]{:S(2)}) async-start(bf16[32,64,256]{2,1,0:T(8,128)(2,1)} %get-tuple-element.4), calls=%async_computation.1 | async-start | bytes 2097152 | tf_op jit(solution)/shard_map/all_to_all | solution.py:447
  110.2 34.8 %collective-permute-start = (bf16[128,1024]{1,0:T(8,128)(2,1)S(1)}, bf16[128,1024]{1,0:T(8,128)(2,1)}, u32[]{:S(2)}, u32[]{:S(2)}) collective-permute-start(bf16[128,1024]{1,0:T(8,128)(2,1)S(1)} %pad_maximum_fusion), channel_id=1, source_target_pairs={{0,4},{1,5},{2,6},{3,7},{4,8},{5,9},{6,10},{7,11},{8,12},{9,13},{1... | collective-permute-start | bytes 786440 | tf_op jit(solution)/shard_map/ppermute | solution.py:406
  118.1 34.1 %collective-permute-start.1 = (bf16[128,1024]{1,0:T(8,128)(2,1)S(1)}, bf16[128,1024]{1,0:T(8,128)(2,1)}, u32[]{:S(2)}, u32[]{:S(2)}) collective-permute-start(bf16[128,1024]{1,0:T(8,128)(2,1)S(1)} %pad_maximum_fusion), channel_id=1, source_target_pairs={{0,3},{1,4},{2,5},{3,6},{4,7},{5,8},{6,9},{7,10},{8,11},{9,12},{10... | collective-permute-start | bytes 786440 | tf_op jit(solution)/shard_map/ppermute | solution.py:406
  121.7 31.4 %collective-permute-start.2 = (bf16[128,1024]{1,0:T(8,128)(2,1)S(1)}, bf16[128,1024]{1,0:T(8,128)(2,1)S(1)}, u32[]{:S(2)}, u32[]{:S(2)}) collective-permute-start(bf16[128,1024]{1,0:T(8,128)(2,1)S(1)} %pad_maximum_fusion), channel_id=1, source_target_pairs={{0,2},{1,3},{2,4},{3,5},{4,6},{5,7},{6,8},{7,9},{8,10},{9,11},{10,... | collective-permute-start | bytes 786440 | tf_op jit(solution)/shard_map/ppermute | solution.py:406
  125.0 46.3 %collective-permute-start.3 = (bf16[128,1024]{1,0:T(8,128)(2,1)S(1)}, bf16[128,1024]{1,0:T(8,128)(2,1)S(1)}, u32[]{:S(2)}, u32[]{:S(2)}) collective-permute-start(bf16[128,1024]{1,0:T(8,128)(2,1)S(1)} %pad_maximum_fusion), channel_id=1, source_target_pairs={{0,1},{1,2},{2,3},{3,4},{4,5},{5,6},{6,7},{7,8},{8,9},{9,10},{10,1... | collective-permute-start | bytes 786440 | tf_op jit(solution)/shard_map/ppermute | solution.py:406
  128.0 44.4 %copy-start.14 = (s32[1,3]{1,0:T(1,128)S(1)}, s32[1,3]{1,0:T(1,128)}, u32[]{:S(2)}) copy-start(s32[1,3]{1,0:T(1,128)} %history.1) | copy-start | bytes 40
  171.4 1.1 copy-start.7
  172.4 1.0 copy-start.5
  173.4 1.3 copy-start.8
  174.7 1.9 copy-start.12
  176.6 1.2 copy-start.13
  177.8 24.5 %copy-start.20 = (f32[64]{0:T(128)S(1)}, f32[64]{0:T(128)}, u32[]{:S(2)}) copy-start(f32[64]{0:T(128)} %param.22) | copy-start | bytes 772
  177.8 24.6 %copy-start.1 = (bf16[1,128,8192]{2,1,0:T(8,128)(2,1)S(1)}, bf16[1,128,8192]{2,1,0:T(8,128)(2,1)}, u32[]{:S(2)}) copy-start(bf16[1,128,8192]{2,1,0:T(8,128)(2,1)} %param.17) | copy-start | bytes 6291460
  177.8 24.6 %copy-start.4 = (bf16[1,128,512]{2,1,0:T(8,128)(2,1)S(1)}, bf16[1,128,512]{2,1,0:T(8,128)(2,1)}, u32[]{:S(2)}) copy-start(bf16[1,128,512]{2,1,0:T(8,128)(2,1)} %param.20) | copy-start | bytes 393220
  177.8 24.6 %copy-start.6 = (bf16[1,128,512]{2,1,0:T(8,128)(2,1)S(1)}, bf16[1,128,512]{2,1,0:T(8,128)(2,1)}, u32[]{:S(2)}) copy-start(bf16[1,128,512]{2,1,0:T(8,128)(2,1)} %param.21) | copy-start | bytes 393220
  202.4 1.6 copy-start.2
Sparse Core Ops, SparseCore 0:
  10.5 72.1 all-gather.6
  95.0 107.3 all-gather.4

commit v2 on v1

--- a/solution.py
+++ b/solution.py
@@ -21,6 +21,7 @@
 HD = 128
 WINDOW = 512
 CTX = 32
+MESH = pl.DeviceIdType.MESH
 
 F32 = jnp.float32
 BF16 = jnp.bfloat16
@@ -104,23 +105,180 @@
         send[j, N:, :] = part.astype(BF16)
 
 
-def scan_kernel(home, lengths, recv, stored, entering, extra):
-    group = lax.axis_index("sess")
-    one, two = starts_of(lengths)
-    back = [stored[home[group * SEQS + s]].astype(F32) for s in range(SEQS)]
+def await_bytes(ref, sem):
+    pltpu.make_async_copy(ref, ref, sem).wait()
+
+
+def exchange_kernel(
+    home,
+    lengths,
+    saved,
+    send,
+    cache,
+    key_value,
+    state,
+    extras,
+    caches,
+    band,
+    recv,
+    stored,
+    entering,
+    extra,
+    sent,
+    got,
+    local,
+):
+    group, me = lax.axis_index("sess"), lax.axis_index("ctx")
+    groups = lax.axis_size("sess")
+    y, z, core = me // 8, (me // 2) % 4, me % 2
+    sibling = me + 1 - 2 * core
+    z_peers = [y * 8 + ((z + i) % 4) * 2 + core for i in range(1, 4)]
+    y_peers = [((y + i) % 4) * 8 + z * 2 + core for i in range(1, 4)]
+    KIND = {name: i for i, name in enumerate(EXCHANGES)}
+
+    barrier = pltpu.get_barrier_semaphore()
+
+    def greet(i, nothing):
+        pl.semaphore_signal(barrier, inc=1, device_id=(group, (me + i) % CTX), device_id_type=MESH)
+        return nothing
+
+    lax.fori_loop(1, CTX, greet, 0)
+    for i in range(1, groups):
+        pl.semaphore_signal(
+            barrier, inc=1, device_id=((group + i) % groups, me), device_id_type=MESH
+        )
+    pl.semaphore_wait(barrier, CTX - 1 + groups - 1)
+
+    def push(kind, src, dst, peer, to=None):
+        at = KIND[kind]
+        pltpu.make_async_remote_copy(
+            src_ref=src,
+            dst_ref=dst,
+            send_sem=sent.at[at],
+            recv_sem=got.at[at],
+            device_id=(group if to is None else to, peer),
+            device_id_type=MESH,
+        ).start()
+
+    keep = []
+
+    def hold(src, dst):
+        copy = pltpu.make_async_copy(src, dst, local.at[len(keep)])
+        copy.start()
+        keep.append(copy)
+        return copy
+
+    for i in range(1, groups):
+        push("home", saved, stored.at[group], me, (group + i) % groups)
+    own_saved = hold(saved, stored.at[group])
+
+    def pass_summary(i, nothing):
+        peer = (me + i) % CTX
+        push("summary", send.at[peer], recv.at[me], peer)
+        return nothing
+
+    lax.fori_loop(1, CTX, pass_summary, 0)
+    own_summary = hold(send.at[me], recv.at[me])
+    for peer in z_peers:
+        push("cache_z", cache, caches.at[me], peer)
+    for peer in y_peers:
+        push("cache_y", cache, caches.at[me], peer)
+    push("cache_core", cache, caches.at[me], sibling)
+    own_cache = hold(cache, caches.at[me])
+    for d in range(1, REACH + 1):
+        push("band", key_value, band.at[pl.ds(8 * (REACH - d), 8)], (me + d) % CTX)
+    own_band = hold(key_value, band.at[pl.ds(8 * REACH, 8)])
+
+    def spread_z(name, array):
+        for peer in z_peers:
+            for to in y_peers:
+                push(name + "_y", array.at[peer], array.at[peer], to)
+            push(name + "_core", array.at[peer], array.at[peer], sibling)
+
+    def spread_y(name, array):
+        for i in range(4):
+            for j in range(1, 4):
+                at = ((y + j) % 4) * 8 + ((z + i) % 4) * 2 + core
+                push(name + "_core", array.at[at], array.at[at], sibling)
+
+    await_bytes(stored.at[pl.ds(0, groups - 1)], got.at[KIND["home"]])
+    own_saved.wait()
+    back = []
+    for s in range(SEQS):
+        at = home[group * SEQS + s]
+        back.append(stored[at // SEQS, at % SEQS].astype(F32))
     extra[0] = back[1].astype(BF16)
     extra[1] = back[2].astype(BF16)
-
-    def turn(c, state):
-        entering[c] = state.astype(BF16)
+    for peer in z_peers:
+        push("extra_z", extra, extras.at[me], peer)
+    for peer in y_peers:
+        push("extra_y", extra, extras.at[me], peer)
+    push("extra_core", extra, extras.at[me], sibling)
+    own_extra = hold(extra, extras.at[me])
+
+    await_bytes(recv.at[pl.ds(0, CTX - 1)], got.at[KIND["summary"]])
+    own_summary.wait()
+    one, two = starts_of(lengths)
+
+    def turn(c, held):
+        entering[c] = held.astype(BF16)
+
+        @pl.when(c != me)
+        def _():
+            push("state", entering.at[c], state.at[me], c)
+
         end = c * TOK + TOK - 1
         inside_one = (end >= one) & (end < two) & (one >= c * TOK)
         inside_two = (end >= two) & (two >= c * TOK)
-        base = jnp.where(inside_two, back[2], jnp.where(inside_one, back[1], state))
+        base = jnp.where(inside_two, back[2], jnp.where(inside_one, back[1], held))
         carry = recv[c, N : N + 16, :].astype(F32)
         return (carry[0:1] + carry[1:2]) * base + recv[c, :N, :].astype(F32)
 
     lax.fori_loop(0, CTX, turn, back[0])
+    own_state = hold(entering.at[me], state.at[me])
+
+    await_bytes(caches.at[pl.ds(0, 3)], got.at[KIND["cache_z"]])
+    spread_z("cache", caches)
+    await_bytes(extras.at[pl.ds(0, 3)], got.at[KIND["extra_z"]])
+    spread_z("extra", extras)
+    await_bytes(caches.at[pl.ds(0, 12)], got.at[KIND["cache_y"]])
+    spread_y("cache", caches)
+    await_bytes(extras.at[pl.ds(0, 12)], got.at[KIND["extra_y"]])
+    spread_y("extra", extras)
+
+    await_bytes(caches.at[pl.ds(0, 16)], got.at[KIND["cache_core"]])
+    await_bytes(extras.at[pl.ds(0, 16)], got.at[KIND["extra_core"]])
+    await_bytes(state.at[pl.ds(0, CTX - 1)], got.at[KIND["state"]])
+    await_bytes(band.at[pl.ds(0, 8 * REACH)], got.at[KIND["band"]])
+    for copy in (own_cache, own_band, own_extra, own_state):
+        copy.wait()
+    for kind, ref in (
+        ("home", stored.at[pl.ds(0, groups - 1)]),
+        ("summary", recv.at[pl.ds(0, CTX - 1)]),
+        ("state", state.at[pl.ds(0, CTX - 1)]),
+        ("band", band.at[pl.ds(0, 8 * REACH)]),
+        ("cache_z", caches.at[pl.ds(0, 3)]),
+        ("cache_y", caches.at[pl.ds(0, 12)]),
+        ("cache_core", caches.at[pl.ds(0, 16)]),
+        ("extra_z", extras.at[pl.ds(0, 3)]),
+        ("extra_y", extras.at[pl.ds(0, 12)]),
+        ("extra_core", extras.at[pl.ds(0, 16)]),
+    ):
+        await_bytes(ref, sent.at[KIND[kind]])
+
+
+EXCHANGES = (
+    "home",
+    "summary",
+    "state",
+    "band",
+    "cache_z",
+    "cache_y",
+    "cache_core",
+    "extra_z",
+    "extra_y",
+    "extra_core",
+)
 
 
 def output_kernel(lengths, x, dt, dlog, write, read, gain, state, extra, out, run_rows, step_rows):
@@ -341,17 +499,30 @@
     )(lengths, x, dt, dlog, write)
 
 
-def scan(home, lengths, recv, stored):
+def exchange(groups, home, lengths, saved, send, cache, key_value):
     return pl.pallas_call(
-        scan_kernel,
+        exchange_kernel,
         out_shape=(
             jax.ShapeDtypeStruct((CTX, N, PAIR), BF16),
-            jax.ShapeDtypeStruct((2, N, PAIR), BF16),
+            jax.ShapeDtypeStruct((CTX, 2, N, PAIR), BF16),
+            jax.ShapeDtypeStruct((CTX,) + cache.shape, BF16),
+            jax.ShapeDtypeStruct((8 * (REACH + 1), 16, 2 * KVH * HD), BF16),
         ),
-        in_specs=[SMEM, SMEM, VMEM, VMEM],
-        out_specs=(VMEM, VMEM),
-        compiler_params=LIMIT,
-    )(home, lengths, recv, stored)
+        in_specs=[SMEM, SMEM, ANY, ANY, ANY, ANY],
+        out_specs=(ANY, ANY, ANY, ANY),
+        scratch_shapes=[
+            pltpu.VMEM((CTX, ROWS, PAIR), BF16),
+            pltpu.VMEM((groups, SEQS, N, PAIR), BF16),
+            pltpu.VMEM((CTX, N, PAIR), BF16),
+            pltpu.VMEM((2, N, PAIR), BF16),
+            pltpu.SemaphoreType.DMA((len(EXCHANGES),)),
+            pltpu.SemaphoreType.DMA((len(EXCHANGES),)),
+            pltpu.SemaphoreType.DMA((6,)),
+        ],
+        compiler_params=pltpu.CompilerParams(
+            collective_id=0, has_side_effects=True, vmem_limit_bytes=48 * 2**20
+        ),
+    )(home, lengths, saved, send, cache, key_value)
 
 
 def outputs(lengths, x, dt, dlog, write, read, gain, state, extra):
@@ -401,11 +572,6 @@
     )(lengths, history, queries, band, sinks, cache)
 
 
-def shifted(block, distance):
-    route = [(i - distance, i) for i in range(distance, CTX)]
-    return lax.ppermute(block, "ctx", route)
-
-
 def shards(
     mamba_input,
     step_size,
@@ -429,12 +595,9 @@
     write, read = state_write[0], state_read[0]
     saved = saved_states[0].astype(BF16).reshape(SEQS, 2, P_SIZE, N)
     saved = saved.transpose(0, 3, 1, 2).reshape(SEQS, N, PAIR)
-    stored = lax.all_gather(saved, "sess", axis=0, tiled=True)
     cache = jnp.stack([cache_keys[0], cache_values[0]])
-    cache = lax.all_gather(cache, "ctx", axis=0)
     key_value = jnp.concatenate([turn_keys[0], turn_values[0]], axis=1)
-    band = [shifted(key_value, d) for d in range(REACH, 0, -1)] + [key_value]
-    band = jnp.concatenate(band, axis=0).reshape(8 * (REACH + 1), 16, 2 * KVH * HD)
+    key_value = key_value.reshape(8, 16, 2 * KVH * HD)
     sinks = jnp.concatenate(
         [sink_keys[0].reshape(SEQS * SINKS, -1), sink_values[0].reshape(SEQS * SINKS, -1)], axis=1
     )
@@ -442,11 +605,11 @@
     gain = jnp.repeat(skip_gain, P_SIZE)[None]
 
     send = summaries(turn_lengths, x, dt, dlog, write)
-    recv = lax.all_to_all(send, "ctx", 0, 0, tiled=True)
-    entering, extra = scan(home_slot, turn_lengths, recv, stored)
-    state = lax.all_to_all(entering, "ctx", 0, 0, tiled=True)
-    extras = lax.all_gather(extra, "ctx", axis=0)
-    attended = attention(turn_lengths, history_lengths, queries[0], band, sinks, cache)
+    groups = lax.axis_size("sess")
+    state, extras, caches, band = exchange(
+        groups, home_slot, turn_lengths, saved, send, cache, key_value
+    )
+    attended = attention(turn_lengths, history_lengths, queries[0], band, sinks, caches)
     mixed = outputs(turn_lengths, x, dt, dlog, write, read, gain, state, extras)
     return (mixed[None], attended[None])
 

time: 222 us -> 188 us (0.85)
  the two profiles are of different devices: /device:TPU:33 before, /device:TPU:40 now
where the time goes in v2:
time: 188 us; the launch traced here: 187 us
  Pallas kernels  165 us (88%)
  local copies, waits for them, and re-layouts  18.2 us (10%)
  other arithmetic  2.55 us (1%)
    pallas_call x1, Pallas kernels, exchange(): pl.pallas_call(exchange_kernel, out_shape=(jax.ShapeDtypeStruct((CTX, N,...  133 us
    pallas_call x1, Pallas kernels, attention(): pl.pallas_call(attention_kernel, out_shape=jax.ShapeDtypeStruct((TOK, QH...  21.7 us
    unnamed x48, local copies, waits for them, and re-layouts  14.6 us
    pallas_call x1, Pallas kernels, outputs(): pl.pallas_call(output_kernel, grid=(STEPS,), out_shape=jax.ShapeDtypeStru...  7.32 us

profile of v2, /device:TPU:40, one launch (start us, length us, event | category | flops | bytes accessed | tf_op | source)
XLA Modules:
  0.0 187.0 jit_solution(18347857174349367459)
XLA Ops:
  0.6 0.8 copy.22
  1.5 0.8 copy.23
  2.3 0.0 copy-start
  2.3 1.6 copy-done
  3.9 0.9 copy-done.3
  4.8 0.7 copy-done.11
  5.5 3.6 %shard_map.176.send = bf16[32,80,256]{2,1,0:T(8,128)(2,1)S(1)} custom-call(s32[1,3]{1,0:T(1,128)S(1)} %copy-done.11, bf16[128,8192]{1,0:T(8,128)(2,1)S(1)} %bitcast.15, bf16[128,64]{1,0:T(8,128)(2,1)S(1)} %bitcast.19, bf16[128,64]{1,0:T(8,128)(2,1)S(1)} %bitcast.21, bf16[128,512]{1,0:T(8,128)(2,1)S(1)} %bitcast.17), custom_call_target="tpu_custom_call" | custom-call | tf_op jit(solution)/shard_map/pallas_call | solution.py:485
  9.1 0.0 copy-start.8
  9.1 0.6 copy-done.8
  9.7 0.7 convert_element_type.9
  10.4 1.8 convert_element_type.10
  12.2 1.7 copy.25.saved
  13.8 1.0 pad_maximum_fusion.key_value
  14.8 0.8 pad_maximum_fusion.1.cache
  15.7 0.0 copy-done.12
  15.7 0.0 copy-done.13
  15.7 0.0 copy-start.5
  15.7 0.9 copy-done.5
  16.6 132.9 %shard_map.177 = (bf16[32,64,256]{2,1,0:T(8,128)(2,1)S(1)}, bf16[32,2,64,256]{3,2,1,0:T(8,128)(2,1)}, bf16[32,2,3,16,512]{4,3,2,1,0:T(8,128)(2,1)}, bf16[40,16,1024]{2,1,0:T(8,128)(2,1)S(1)}) custom-call(s32[24]{0:T(128)S(1)} %copy-done.13, s32[1,3]{1,0:T(1,128)S(1)} %copy-done.12, bf16[3,64,256]{2,1,0:T(8,128)(2,1)S(1)} %copy-done.5, ...), custom_call_target="tpu_custom_call" | custom-call | tf_op jit(solution)/shard_map/pallas_call | solution.py:503
  149.5 1.1 copy-done.15
  150.6 0.0 copy-done.22
  150.6 0.1 broadcast_in_dim.9
  150.7 1.6 copy-done.2
  152.3 0.8 copy-done.7
  153.0 0.8 copy-done.9
  153.8 0.9 copy-done.10
  154.7 7.3 %shard_map.178 = bf16[128,8192]{1,0:T(8,128)(2,1)} custom-call(s32[1,3]{1,0:T(1,128)S(1)} %copy-done.12, bf16[128,8192]{1,0:T(8,128)(2,1)S(1)} %bitcast.16, bf16[128,64]{1,0:T(8,128)(2,1)S(1)} %bitcast.20, bf16[128,64]{1,0:T(8,128)(2,1)S(1)} %bitcast.22, bf16[128,512]{1,0:T(8,128)(2,1)S(1)} %bitcast.18, bf16[128,512]{1,0:T(8,128)(2,1)S(1)} %bitcast.24, ...), custom_call_target="tpu_custom_call" | custom-call | tf_op jit(solution)/shard_map/pallas_call | solution.py:529
  162.0 0.0 copy-done.21
  162.1 0.0 copy-done.17
  162.1 1.9 %copy-done.14 = bf16[32,2,3,16,512]{4,3,2,1,0:T(8,128)(2,1)S(1)} copy-done((bf16[32,2,3,16,512]{4,3,2,1,0:T(8,128)(2,1)S(1)}, bf16[32,2,3,16,512]{4,3,2,1,0:T(8,128)(2,1)}, u32[]{:S(2)}) %copy-start.14) | copy-done | bytes 3145752
  164.0 1.3 copy-done.16
  165.3 21.7 %shard_map.179 = bf16[128,4096]{1,0:T(8,128)(2,1)} custom-call(s32[1,3]{1,0:T(1,128)S(1)} %copy-done.12, s32[1,3]{1,0:T(1,128)S(1)} %copy-done.18, bf16[128,4096]{1,0:T(8,128)(2,1)S(1)} %bitcast.26, bf16[40,16,1024]{2,1,0:T(8,128)(2,1)S(1)} %copy-done.16, bf16[8,16,1024]{2,1,0:T(8,128)(2,1)S(1)} %bitcast.23, bf16[32,2,3,16,512]{4,3,2,1,0:T(8,128)(2,1)S(1)} %copy-done.14), custom_call_target="tpu_custom_call" | custom-call | flops 2500000000 | bytes 8000000 | tf_op jit(solution)/shard_map/pallas_call | solution.py:552
  (29 shorter events, 0.1 us)
Async XLA Ops:
  1.5 0.9 copy-start.6
  2.3 1.6 copy-start
  3.9 0.9 copy-start.3
  4.8 0.7 copy-start.11
  5.5 4.2 %copy-start.19 = (f32[1,3,2,8192]{3,2,1,0:T(2,128)S(1)}, f32[1,3,2,8192]{3,2,1,0:T(2,128)}, u32[]{:S(2)}) copy-start(f32[1,3,2,8192]{3,2,1,0:T(2,128)} %param.23) | copy-start | bytes 589828
  5.5 10.2 %copy-start.12 = (s32[1,3]{1,0:T(1,128)S(1)}, s32[1,3]{1,0:T(1,128)}, u32[]{:S(2)}) copy-start(s32[1,3]{1,0:T(1,128)} %lengths.7) | copy-start | bytes 40
  5.5 10.2 %copy-start.13 = (s32[24]{0:T(128)S(1)}, s32[24]{0:T(128)}, u32[]{:S(2)}) copy-start(s32[24]{0:T(128)} %home.1) | copy-start | bytes 292
  5.5 145.1 %copy-start.22 = (f32[64]{0:T(128)S(1)}, f32[64]{0:T(128)}, u32[]{:S(2)}) copy-start(f32[64]{0:T(128)} %param.22) | copy-start | bytes 772
  9.1 0.6 copy-start.8
  9.7 141.0 %copy-start.1 = (bf16[1,128,8192]{2,1,0:T(8,128)(2,1)S(1)}, bf16[1,128,8192]{2,1,0:T(8,128)(2,1)}, u32[]{:S(2)}) copy-start(bf16[1,128,8192]{2,1,0:T(8,128)(2,1)} %param.17) | copy-start | bytes 6291460
  9.7 141.0 %copy-start.4 = (bf16[1,128,512]{2,1,0:T(8,128)(2,1)S(1)}, bf16[1,128,512]{2,1,0:T(8,128)(2,1)}, u32[]{:S(2)}) copy-start(bf16[1,128,512]{2,1,0:T(8,128)(2,1)} %param.20) | copy-start | bytes 393220
  15.7 0.9 copy-start.5
  149.5 1.1 copy-start.15
  150.7 1.6 copy-start.2
  152.3 0.8 copy-start.7
  153.0 0.8 copy-start.9
  153.8 0.9 copy-start.10
  154.7 7.3 %copy-start.20 = (bf16[1,3,4,512]{3,2,1,0:T(4,128)(2,1)S(1)}, bf16[1,3,4,512]{3,2,1,0:T(4,128)(2,1)}, u32[]{:S(2)}) copy-start(bf16[1,3,4,512]{3,2,1,0:T(4,128)(2,1)} %param.32) | copy-start | bytes 36868
  154.7 7.3 %copy-start.21 = (bf16[1,3,4,512]{3,2,1,0:T(4,128)(2,1)S(1)}, bf16[1,3,4,512]{3,2,1,0:T(4,128)(2,1)}, u32[]{:S(2)}) copy-start(bf16[1,3,4,512]{3,2,1,0:T(4,128)(2,1)} %param.33) | copy-start | bytes 36868
  154.7 7.4 %copy-start.17 = (bf16[1,128,4096]{2,1,0:T(8,128)(2,1)S(1)}, bf16[1,128,4096]{2,1,0:T(8,128)(2,1)}, u32[]{:S(2)}) copy-start(bf16[1,128,4096]{2,1,0:T(8,128)(2,1)} %param.27) | copy-start | bytes 3145732
  154.7 7.4 %copy-start.18 = (s32[1,3]{1,0:T(1,128)S(1)}, s32[1,3]{1,0:T(1,128)}, u32[]{:S(2)}) copy-start(s32[1,3]{1,0:T(1,128)} %history.1) | copy-start | bytes 40
  162.1 1.9 %copy-start.14 = (bf16[32,2,3,16,512]{4,3,2,1,0:T(8,128)(2,1)S(1)}, bf16[32,2,3,16,512]{4,3,2,1,0:T(8,128)(2,1)}, u32[]{:S(2)}) copy-start(bf16[32,2,3,16,512]{4,3,2,1,0:T(8,128)(2,1)} %get-tuple-element.9.cache) | copy-start | bytes 9437188
  164.0 1.3 copy-start.16

commit v3 on v1

--- a/solution.py
+++ b/solution.py
@@ -21,6 +21,8 @@
 HD = 128
 WINDOW = 512
 CTX = 32
+CHIPS = CTX // 2
+MESH = pl.DeviceIdType.MESH
 
 F32 = jnp.float32
 BF16 = jnp.bfloat16
@@ -92,35 +94,288 @@
         loads = (row * turned[b * N : (b + 1) * N]).astype(BF16)
         made = nn(loads, x[:, k * P_SIZE : (k + 1) * P_SIZE])
         lane = (k % 2) * P_SIZE
-        send[k // 2, :N, lane : lane + P_SIZE] = made.astype(BF16)
+        j = k // 2
+        send[j % 2, j // 2, :N, lane : lane + P_SIZE] = made
     spread = nn(rates, spread_matrix(step)).astype(BF16)
     carry = jnp.exp(nn(mask[TOK - 16 :], spread)[15:16])
-    high = carry.astype(BF16).astype(F32)
-    low = carry - high
-    tile = iota((16, PAIR), 0)
     for j in range(HEADS // 2):
-        lanes = slice(j * PAIR, (j + 1) * PAIR)
-        part = jnp.where(tile == 0, high[:, lanes], jnp.where(tile == 1, low[:, lanes], 0.0))
-        send[j, N:, :] = part.astype(BF16)
-
-
-def scan_kernel(home, lengths, recv, stored, entering, extra):
-    group = lax.axis_index("sess")
+        row = carry[:, j * PAIR : (j + 1) * PAIR]
+        send[j % 2, j // 2, N:, :] = jnp.broadcast_to(row, (8, PAIR))
+
+
+def await_bytes(ref, sem):
+    pltpu.make_async_copy(ref, ref, sem).wait()
+
+
+def exchange_kernel(
+    home,
+    lengths,
+    saved,
+    made,
+    cache_keys,
+    cache_values,
+    turn_keys,
+    turn_values,
+    state,
+    extras,
+    caches,
+    band,
+    theirs,
+    packed,
+    recv,
+    stored,
+    entering,
+    arrived,
+    own_state,
+    other_state,
+    extra,
+    plane,
+    sent,
+    got,
+    local,
+):
+    group, me = lax.axis_index("sess"), lax.axis_index("ctx")
+    x, deep = group // 2, group % 2
+    y, z, core = me // 8, (me // 2) % 4, me % 2
+    chip = me // 2
+    sibling = me + 1 - 2 * core
+    partner = group + 1 - 2 * deep
+    x_groups = [((x + i) % 4) * 2 + deep for i in range(1, 4)]
+    y_peers = [((y + i) % 4) * 8 + z * 2 + core for i in range(1, 4)]
+    z_before = y * 8 + ((z + 3) % 4) * 2 + core
+    z_after = [y * 8 + ((z + i) % 4) * 2 + core for i in range(1, 4)]
+    onward = (me + 2) % CTX
+    kinds = {name: i for i, name in enumerate(EXCHANGES)}
+
+    def copy_in(src, dst, at):
+        copy = pltpu.make_async_copy(src, dst, local.at[at])
+        copy.start()
+        return copy
+
+    half = KVH * HD
+    mine = [
+        copy_in(cache_keys, caches.at[me, 0], 0),
+        copy_in(cache_values, caches.at[me, 1], 1),
+        copy_in(turn_keys, band.at[pl.ds(8 * REACH, 8), :, pl.ds(0, half)], 2),
+        copy_in(turn_values, band.at[pl.ds(8 * REACH, 8), :, pl.ds(half, half)], 3),
+        copy_in(saved, stored.at[group], 4),
+    ]
+
+    barrier = pltpu.get_barrier_semaphore()
+
+    def greet(i, nothing):
+        peer = ((chip + i) % CHIPS) * 2 + core
+        pl.semaphore_signal(barrier, inc=1, device_id=(group, peer), device_id_type=MESH)
+        return nothing
+
+    lax.fori_loop(1, CHIPS, greet, 0)
+    pl.semaphore_signal(barrier, inc=1, device_id=(group, sibling), device_id_type=MESH)
+    for to in [partner] + x_groups:
+        pl.semaphore_signal(barrier, inc=1, device_id=(to, me), device_id_type=MESH)
+    pl.semaphore_wait(barrier, CHIPS - 1 + 1 + 4)
+
+    def push(kind, src, dst, peer, to=None):
+        at = kinds[kind]
+        pltpu.make_async_remote_copy(
+            src_ref=src,
+            dst_ref=dst,
+            send_sem=sent.at[at],
+            recv_sem=got.at[at],
+            device_id=(group if to is None else to, peer),
+            device_id_type=MESH,
+        ).start()
+
+    counts = {}
+
+    def arrive(kind, ref):
+        counts[kind] = ref
+        await_bytes(ref, got.at[kinds[kind]])
+
+    def slot(distance):
+        return band.at[pl.ds(8 * (REACH - distance), 8)]
+
+    def spread(name, array, at):
+        for to in y_peers:
+            push(name + "_y", array.at[at], array.at[at], to)
+
+    push("home_z", saved, stored.at[group], me, partner)
+    for to in x_groups:
+        push("home_x", saved, stored.at[group], me, to)
+    push("pair", made.at[1 - core], theirs, sibling)
+    mine[2].wait()
+    mine[3].wait()
+    push("band_2", slot(0), slot(2), onward)
+    mine[0].wait()
+    mine[1].wait()
+    push("cache_1", caches.at[me], caches.at[me], z_before)
+    spread("cache", caches, me)
+    push("cache_core", caches.at[me], caches.at[me], sibling)
+
+    arrive("home_z", stored.at[0])
+    for to in x_groups:
+        push("home_x", stored.at[partner], stored.at[partner], me, to)
+
     one, two = starts_of(lengths)
-    back = [stored[home[group * SEQS + s]].astype(F32) for s in range(SEQS)]
+
+    def inside(c):
+        end = c * TOK + TOK - 1
+        first = (end >= one) & (end < two) & (one >= c * TOK)
+        second = (end >= two) & (two >= c * TOK)
+        return first, second
+
+    arrive("pair", theirs)
+    first_one, first_two = inside(2 * chip)
+    last_one, last_two = inside(2 * chip + 1)
+    fresh = last_one | last_two
+
+    def both(m):
+        own = made[core, m]
+        other = theirs[m]
+        even = jnp.where(core == 0, own, other)
+        odd = jnp.where(core == 0, other, own)
+        return even, odd
+
+    def combine(i, nothing):
+        m = (chip + i) % CHIPS
+        even, odd = both(m)
+        factor = odd[N : N + 1]
+        total = odd[:N] + jnp.where(fresh, 0.0, factor) * even[:N]
+        carry = factor * jnp.where(fresh, 1.0, even[N : N + 1])
+        packed[m, :N, :] = total.astype(BF16)
+        high = carry.astype(BF16).astype(F32)
+        tile = iota((16, PAIR), 0)
+        rows = jnp.where(tile == 0, high, jnp.where(tile == 1, carry - high, 0.0))
+        packed[m, N:, :] = rows.astype(BF16)
+
+        @pl.when(i != 0)
+        def _():
+            push("summary", packed.at[m], recv.at[chip], 2 * m + core)
+
+        return nothing
+
+    lax.fori_loop(0, CHIPS, combine, 0)
+    own_summary = copy_in(packed.at[chip], recv.at[chip], 0)
+
+    arrive("cache_1", caches.at[0])
+    push("cache_2", caches.at[z_after[0]], caches.at[z_after[0]], z_before)
+    spread("cache", caches, z_after[0])
+    push("cache_core", caches.at[z_after[0]], caches.at[z_after[0]], sibling)
+    arrive("band_2", slot(2))
+    push("band_4", slot(2), slot(4), onward)
+
+    mine[4].wait()
+    arrive("home_x", stored.at[pl.ds(0, 6)])
+    back = []
+    for s in range(SEQS):
+        at = home[group * SEQS + s]
+        back.append(stored[at // SEQS, at % SEQS].astype(F32))
     extra[0] = back[1].astype(BF16)
     extra[1] = back[2].astype(BF16)
-
-    def turn(c, state):
-        entering[c] = state.astype(BF16)
-        end = c * TOK + TOK - 1
-        inside_one = (end >= one) & (end < two) & (one >= c * TOK)
-        inside_two = (end >= two) & (two >= c * TOK)
-        base = jnp.where(inside_two, back[2], jnp.where(inside_one, back[1], state))
-        carry = recv[c, N : N + 16, :].astype(F32)
-        return (carry[0:1] + carry[1:2]) * base + recv[c, :N, :].astype(F32)
-
-    lax.fori_loop(0, CTX, turn, back[0])
+    push("extra_1", extra, plane.at[chip], z_before)
+    for to in y_peers:
+        push("extra_y", extra, plane.at[chip], to)
+    own_extra = copy_in(extra, plane.at[chip], 1)
+
+    arrive("cache_2", caches.at[0])
+    push("cache_3", caches.at[z_after[1]], caches.at[z_after[1]], z_before)
+    spread("cache", caches, z_after[1])
+    push("cache_core", caches.at[z_after[1]], caches.at[z_after[1]], sibling)
+
+    arrive("summary", recv.at[pl.ds(0, CHIPS - 1)])
+    own_summary.wait()
+
+    def turn(m, held):
+        entering[m] = held.astype(BF16)
+
+        @pl.when(m != chip)
+        def _():
+            push("state", entering.at[m], arrived.at[chip], 2 * m + core)
+
+        even_one, even_two = inside(2 * m)
+        odd_one, odd_two = inside(2 * m + 1)
+        base = jnp.where(even_two, back[2], jnp.where(even_one, back[1], held))
+        base = jnp.where(odd_two, back[2], jnp.where(odd_one, back[1], base))
+        carry = recv[m, N : N + 16, :].astype(F32)
+        return (carry[0:1] + carry[1:2]) * base + recv[m, :N, :].astype(F32)
+
+    lax.fori_loop(0, CHIPS, turn, back[0])
+    own_entering = copy_in(entering.at[chip], arrived.at[chip], 2)
+
+    arrive("extra_1", plane.at[0])
+    push("extra_2", plane.at[z_after[0] // 2], plane.at[z_after[0] // 2], z_before)
+    spread("extra", plane, z_after[0] // 2)
+    arrive("cache_3", caches.at[0])
+    spread("cache", caches, z_after[2])
+    push("cache_core", caches.at[z_after[2]], caches.at[z_after[2]], sibling)
+    arrive("extra_2", plane.at[0])
+    push("extra_3", plane.at[z_after[1] // 2], plane.at[z_after[1] // 2], z_before)
+    spread("extra", plane, z_after[1] // 2)
+    arrive("band_4", slot(4))
+    push("band_core", slot(2 * core), slot(1), sibling)
+    push("band_core", slot(2 * core + 2), slot(3), sibling)
+    arrive("cache_y", caches.at[pl.ds(0, 12)])
+    for i in range(4):
+        for j in range(1, 4):
+            at = ((y + j) % 4) * 8 + ((z + i) % 4) * 2 + core
+            push("cache_core", caches.at[at], caches.at[at], sibling)
+    arrive("extra_3", plane.at[0])
+    spread("extra", plane, z_after[2] // 2)
+    own_extra.wait()
+    arrive("extra_y", plane.at[pl.ds(0, 12)])
+    push("extra_core", plane, extras.at[core], sibling)
+    keep_extra = copy_in(plane, extras.at[core], 0)
+
+    arrive("state", arrived.at[pl.ds(0, CHIPS - 1)])
+    own_entering.wait()
+
+    def settle(m, nothing):
+        even, _ = both(m)
+        first = arrived[m].astype(F32)
+        base = jnp.where(
+            first_two,
+            plane[m, 1].astype(F32),
+            jnp.where(first_one, plane[m, 0].astype(F32), first),
+        )
+        second = even[N : N + 1] * base + even[:N]
+        own_state[m] = jnp.where(core == 0, first, second).astype(BF16)
+        other_state[m] = jnp.where(core == 0, second, first).astype(BF16)
+        return nothing
+
+    lax.fori_loop(0, CHIPS, settle, 0)
+    push("state_core", other_state, state.at[core], sibling)
+    keep_state = copy_in(own_state, state.at[core], 1)
+
+    arrive("extra_core", extras.at[0])
+    arrive("cache_core", caches.at[pl.ds(0, CHIPS)])
+    arrive("band_core", band.at[pl.ds(0, 16)])
+    arrive("state_core", state.at[0])
+    keep_extra.wait()
+    keep_state.wait()
+    for kind, ref in counts.items():
+        await_bytes(ref, sent.at[kinds[kind]])
+
+
+EXCHANGES = (
+    "home_z",
+    "home_x",
+    "pair",
+    "summary",
+    "state",
+    "state_core",
+    "band_2",
+    "band_4",
+    "band_core",
+    "cache_1",
+    "cache_2",
+    "cache_3",
+    "cache_y",
+    "cache_core",
+    "extra_1",
+    "extra_2",
+    "extra_3",
+    "extra_y",
+    "extra_core",
+)
 
 
 def output_kernel(lengths, x, dt, dlog, write, read, gain, state, extra, out, run_rows, step_rows):
@@ -152,7 +407,9 @@
         for j in range(G // 2):
             chunk = b * (G // 2) + j
             from_state = (
-                nn(c_in, state[chunk]) + nn(c_one, extra[chunk, 0]) + nn(c_two, extra[chunk, 1])
+                nn(c_in, state[chunk % 2, chunk // 2])
+                + nn(c_one, extra[chunk % 2, chunk // 2, 0])
+                + nn(c_two, extra[chunk % 2, chunk // 2, 1])
             )
             for i in range(2):
                 k = chunk * 2 + i
@@ -327,7 +584,7 @@
     return pl.pallas_call(
         summary_kernel,
         grid=(STEPS,),
-        out_shape=jax.ShapeDtypeStruct((CTX, ROWS, PAIR), BF16),
+        out_shape=jax.ShapeDtypeStruct((2, CHIPS, N + 8, PAIR), F32),
         in_specs=[
             SMEM,
             lane_block(TOK, WIDE),
@@ -335,23 +592,42 @@
             full((TOK, H)),
             lane_block(TOK, 2 * N),
         ],
-        out_specs=pl.BlockSpec((CTX // STEPS, ROWS, PAIR), lambda i: (i, 0, 0)),
+        out_specs=pl.BlockSpec((2, CHIPS // STEPS, N + 8, PAIR), lambda i: (0, i, 0, 0)),
         scratch_shapes=[pltpu.VMEM((H, TOK), F32)],
         compiler_params=LIMIT,
     )(lengths, x, dt, dlog, write)
 
 
-def scan(home, lengths, recv, stored):
+def exchange(groups, home, lengths, saved, made, cache_keys, cache_values, turn_keys, turn_values):
     return pl.pallas_call(
-        scan_kernel,
+        exchange_kernel,
         out_shape=(
-            jax.ShapeDtypeStruct((CTX, N, PAIR), BF16),
-            jax.ShapeDtypeStruct((2, N, PAIR), BF16),
+            jax.ShapeDtypeStruct((2, CHIPS, N, PAIR), BF16),
+            jax.ShapeDtypeStruct((2, CHIPS, 2, N, PAIR), BF16),
+            jax.ShapeDtypeStruct((CTX, 2) + cache_keys.shape, BF16),
+            jax.ShapeDtypeStruct((8 * (REACH + 1), 16, 2 * KVH * HD), BF16),
         ),
-        in_specs=[SMEM, SMEM, VMEM, VMEM],
-        out_specs=(VMEM, VMEM),
-        compiler_params=LIMIT,
-    )(home, lengths, recv, stored)
+        in_specs=[SMEM, SMEM, ANY, VMEM, ANY, ANY, ANY, ANY],
+        out_specs=(ANY, ANY, ANY, ANY),
+        scratch_shapes=[
+            pltpu.VMEM((CHIPS, N + 8, PAIR), F32),
+            pltpu.VMEM((CHIPS, ROWS, PAIR), BF16),
+            pltpu.VMEM((CHIPS, ROWS, PAIR), BF16),
+            pltpu.VMEM((groups, SEQS, N, PAIR), BF16),
+            pltpu.VMEM((CHIPS, N, PAIR), BF16),
+            pltpu.VMEM((CHIPS, N, PAIR), BF16),
+            pltpu.VMEM((CHIPS, N, PAIR), BF16),
+            pltpu.VMEM((CHIPS, N, PAIR), BF16),
+            pltpu.VMEM((2, N, PAIR), BF16),
+            pltpu.VMEM((CHIPS, 2, N, PAIR), BF16),
+            pltpu.SemaphoreType.DMA((len(EXCHANGES),)),
+            pltpu.SemaphoreType.DMA((len(EXCHANGES),)),
+            pltpu.SemaphoreType.DMA((5,)),
+        ],
+        compiler_params=pltpu.CompilerParams(
+            collective_id=0, has_side_effects=True, vmem_limit_bytes=48 * 2**20
+        ),
+    )(home, lengths, saved, made, cache_keys, cache_values, turn_keys, turn_values)
 
 
 def outputs(lengths, x, dt, dlog, write, read, gain, state, extra):
@@ -367,8 +643,8 @@
             lane_block(TOK, 2 * N),
             lane_block(TOK, 2 * N),
             lane_block(1, WIDE),
-            pl.BlockSpec((CTX // STEPS, N, PAIR), lambda i: (i, 0, 0)),
-            pl.BlockSpec((CTX // STEPS, 2, N, PAIR), lambda i: (i, 0, 0, 0)),
+            pl.BlockSpec((2, CHIPS // STEPS, N, PAIR), lambda i: (0, i, 0, 0)),
+            pl.BlockSpec((2, CHIPS // STEPS, 2, N, PAIR), lambda i: (0, i, 0, 0, 0)),
         ],
         out_specs=lane_block(TOK, WIDE),
         scratch_shapes=[pltpu.VMEM((H, TOK), F32), pltpu.VMEM((H, TOK), F32)],
@@ -401,11 +677,6 @@
     )(lengths, history, queries, band, sinks, cache)
 
 
-def shifted(block, distance):
-    route = [(i - distance, i) for i in range(distance, CTX)]
-    return lax.ppermute(block, "ctx", route)
-
-
 def shards(
     mamba_input,
     step_size,
@@ -429,24 +700,26 @@
     write, read = state_write[0], state_read[0]
     saved = saved_states[0].astype(BF16).reshape(SEQS, 2, P_SIZE, N)
     saved = saved.transpose(0, 3, 1, 2).reshape(SEQS, N, PAIR)
-    stored = lax.all_gather(saved, "sess", axis=0, tiled=True)
-    cache = jnp.stack([cache_keys[0], cache_values[0]])
-    cache = lax.all_gather(cache, "ctx", axis=0)
-    key_value = jnp.concatenate([turn_keys[0], turn_values[0]], axis=1)
-    band = [shifted(key_value, d) for d in range(REACH, 0, -1)] + [key_value]
-    band = jnp.concatenate(band, axis=0).reshape(8 * (REACH + 1), 16, 2 * KVH * HD)
     sinks = jnp.concatenate(
         [sink_keys[0].reshape(SEQS * SINKS, -1), sink_values[0].reshape(SEQS * SINKS, -1)], axis=1
     )
     sinks = jnp.pad(sinks, ((0, TOK - SEQS * SINKS), (0, 0))).reshape(8, 16, 2 * KVH * HD)
     gain = jnp.repeat(skip_gain, P_SIZE)[None]
 
-    send = summaries(turn_lengths, x, dt, dlog, write)
-    recv = lax.all_to_all(send, "ctx", 0, 0, tiled=True)
-    entering, extra = scan(home_slot, turn_lengths, recv, stored)
-    state = lax.all_to_all(entering, "ctx", 0, 0, tiled=True)
-    extras = lax.all_gather(extra, "ctx", axis=0)
-    attended = attention(turn_lengths, history_lengths, queries[0], band, sinks, cache)
+    made = summaries(turn_lengths, x, dt, dlog, write)
+    groups = lax.axis_size("sess")
+    state, extras, caches, band = exchange(
+        groups,
+        home_slot,
+        turn_lengths,
+        saved,
+        made,
+        cache_keys[0],
+        cache_values[0],
+        turn_keys[0].reshape(8, 16, KVH * HD),
+        turn_values[0].reshape(8, 16, KVH * HD),
+    )
+    attended = attention(turn_lengths, history_lengths, queries[0], band, sinks, caches)
     mixed = outputs(turn_lengths, x, dt, dlog, write, read, gain, state, extras)
     return (mixed[None], attended[None])
 

time: 222 us -> 125 us (0.56)
  the two profiles are of different devices: /device:TPU:33 before, /device:TPU:44 now
where the time goes in v3:
time: 125 us
  Pallas kernels  113 us (90%)
  local copies, waits for them, and re-layouts  11.2 us (9%)
    pallas_call x1, Pallas kernels, exchange(): pl.pallas_call(exchange_kernel, out_shape=(jax.ShapeDtypeStruct((2, CHIPS...  80.5 us
    pallas_call x1, Pallas kernels, attention(): pl.pallas_call(attention_kernel, out_shape=jax.ShapeDtypeStruct((TOK, QH...  21 us
    unnamed x46, local copies, waits for them, and re-layouts  10.7 us
    pallas_call x1, Pallas kernels, outputs(): pl.pallas_call(output_kernel, grid=(STEPS,), out_shape=jax.ShapeDtypeStru...  7.45 us
    pallas_call x1, Pallas kernels, summaries(): pl.pallas_call(summary_kernel, grid=(STEPS,), out_shape=jax.ShapeDtypeStr...  3.59 us

profile of v3, /device:TPU:44, one launch (start us, length us, event | category | flops | bytes accessed | tf_op | source)
XLA Modules:
  0.0 124.7 jit_solution(17402504184961220037)
XLA Ops:
  0.6 0.8 copy.22
  1.5 0.8 copy.23
  2.3 0.0 copy-start.1
  2.3 1.6 %copy-done.1 = bf16[1,128,8192]{2,1,0:T(8,128)(2,1)S(1)} copy-done((bf16[1,128,8192]{2,1,0:T(8,128)(2,1)S(1)}, bf16[1,128,8192]{2,1,0:T(8,128)(2,1)}, u32[]{:S(2)}) %copy-start.1) | copy-done | bytes 2097176
  3.9 0.9 copy-done.3
  4.8 0.7 copy-done.10
  5.5 0.0 copy-start.9
  5.5 0.0 copy-start.11
  5.5 0.0 copy-start.12
  5.5 3.6 %shard_map.176.made = f32[2,16,72,256]{3,2,1,0:T(8,128)S(1)} custom-call(s32[1,3]{1,0:T(1,128)S(1)} %copy-done.10, bf16[128,8192]{1,0:T(8,128)(2,1)S(1)} %bitcast.17, bf16[128,64]{1,0:T(8,128)(2,1)S(1)} %bitcast.21, bf16[128,64]{1,0:T(8,128)(2,1)S(1)} %bitcast.23, bf16[128,512]{1,0:T(8,128)(2,1)S(1)} %bitcast.19), custom_call_target="tpu_custom_call" | custom-call | tf_op jit(solution)/shard_map/pallas_call | solution.py:584
  9.1 0.0 copy-start
  9.1 1.4 %copy-done = f32[2,16,72,256]{3,2,1,0:T(8,128)} copy-done((f32[2,16,72,256]{3,2,1,0:T(8,128)}, f32[2,16,72,256]{3,2,1,0:T(8,128)S(1)}, u32[]{:S(2)}) %copy-start) | copy-done | bytes 2359320
  10.5 0.0 copy-done.18
  10.6 0.0 copy-start.5
  10.6 0.1 convert_element_type.9
  10.6 0.2 convert_element_type.10
  10.8 0.1 copy.25.saved
  11.0 0.0 copy-done.6
  11.0 0.0 copy-done.7
  11.0 80.5 %shard_map.177 = (bf16[2,16,64,256]{3,2,1,0:T(8,128)(2,1)S(1)}, bf16[2,16,2,64,256]{4,3,2,1,0:T(8,128)(2,1)S(1)}, bf16[32,2,3,16,512]{4,3,2,1,0:T(8,128)(2,1)}, bf16[40,16,1024]{2,1,0:T(8,128)(2,1)S(1)}) custom-call(s32[24]{0:T(128)S(1)} %copy-done.12, s32[1,3]{1,0:T(1,128)S(1)} %copy-done.11, bf16[3,64,256]{2,1,0:T(8,128)(2,1)S(1)} %copy.25.saved, ...), custom_call_target="tpu_custom_call" | custom-call | tf_op jit(solution)/shard_map/pallas_call | solution.py:602
  91.6 0.1 broadcast_in_dim.9
  91.6 0.0 copy-done.2
  91.7 0.0 copy-start.19
  91.7 0.0 copy-start.20
  91.7 0.0 copy-start.17
  91.7 7.5 %shard_map.178 = bf16[128,8192]{1,0:T(8,128)(2,1)} custom-call(s32[1,3]{1,0:T(1,128)S(1)} %copy-done.11, bf16[128,8192]{1,0:T(8,128)(2,1)S(1)} %bitcast.18, bf16[128,64]{1,0:T(8,128)(2,1)S(1)} %bitcast.22, bf16[128,64]{1,0:T(8,128)(2,1)S(1)} %bitcast.24, bf16[128,512]{1,0:T(8,128)(2,1)S(1)} %bitcast.20, bf16[128,512]{1,0:T(8,128)(2,1)S(1)} %bitcast.26, ...), custom_call_target="tpu_custom_call" | custom-call | tf_op jit(solution)/shard_map/pallas_call | solution.py:634
  99.2 0.0 copy-done.19
  99.2 0.0 copy-done.20
  99.2 1.9 %copy-done.13 = bf16[32,2,3,16,512]{4,3,2,1,0:T(8,128)(2,1)S(1)} copy-done((bf16[32,2,3,16,512]{4,3,2,1,0:T(8,128)(2,1)S(1)}, bf16[32,2,3,16,512]{4,3,2,1,0:T(8,128)(2,1)}, u32[]{:S(2)}) %copy-start.13) | copy-done | bytes 3145752
  101.1 1.3 %copy-done.15 = bf16[40,16,1024]{2,1,0:T(8,128)(2,1)S(1)} copy-done((bf16[40,16,1024]{2,1,0:T(8,128)(2,1)S(1)}, bf16[40,16,1024]{2,1,0:T(8,128)(2,1)}, u32[]{:S(2)}) %copy-start.15) | copy-done | bytes 1310744
  102.4 1.2 copy-done.16
  103.7 21.0 %shard_map.179 = bf16[128,4096]{1,0:T(8,128)(2,1)} custom-call(s32[1,3]{1,0:T(1,128)S(1)} %copy-done.11, s32[1,3]{1,0:T(1,128)S(1)} %copy-done.17, bf16[128,4096]{1,0:T(8,128)(2,1)S(1)} %bitcast.32, bf16[40,16,1024]{2,1,0:T(8,128)(2,1)S(1)} %copy-done.15, bf16[8,16,1024]{2,1,0:T(8,128)(2,1)S(1)} %bitcast.25, bf16[32,2,3,16,512]{4,3,2,1,0:T(8,128)(2,1)S(1)} %copy-done.13), custom_call_target="tpu_custom_call" | custom-call | flops 2500000000 | bytes 8000000 | tf_op jit(solution)/shard_map/pallas_call | solution.py:657
  (25 shorter events, 0.1 us)
Async XLA Ops:
  2.3 1.6 %copy-start.1 = (bf16[1,128,8192]{2,1,0:T(8,128)(2,1)S(1)}, bf16[1,128,8192]{2,1,0:T(8,128)(2,1)}, u32[]{:S(2)}) copy-start(bf16[1,128,8192]{2,1,0:T(8,128)(2,1)} %param.17) | copy-start | bytes 6291460
  3.9 0.9 copy-start.3
  4.8 0.7 copy-start.10
  5.5 5.1 %copy-start.18 = (f32[1,3,2,8192]{3,2,1,0:T(2,128)S(1)}, f32[1,3,2,8192]{3,2,1,0:T(2,128)}, u32[]{:S(2)}) copy-start(f32[1,3,2,8192]{3,2,1,0:T(2,128)} %param.23) | copy-start | bytes 589828
  5.5 5.5 %copy-start.6 = (bf16[1,128,512]{2,1,0:T(8,128)(2,1)S(1)}, bf16[1,128,512]{2,1,0:T(8,128)(2,1)}, u32[]{:S(2)}) copy-start(bf16[1,128,512]{2,1,0:T(8,128)(2,1)} %param.28) | copy-start | bytes 393220
  5.5 5.5 %copy-start.7 = (bf16[1,128,512]{2,1,0:T(8,128)(2,1)S(1)}, bf16[1,128,512]{2,1,0:T(8,128)(2,1)}, u32[]{:S(2)}) copy-start(bf16[1,128,512]{2,1,0:T(8,128)(2,1)} %param.29) | copy-start | bytes 393220
  5.5 5.5 %copy-start.8 = (bf16[1,3,16,512]{3,2,1,0:T(8,128)(2,1)S(1)}, bf16[1,3,16,512]{3,2,1,0:T(8,128)(2,1)}, u32[]{:S(2)}) copy-start(bf16[1,3,16,512]{3,2,1,0:T(8,128)(2,1)} %param.30) | copy-start | bytes 147460
  5.5 5.5 %copy-start.9 = (bf16[1,3,16,512]{3,2,1,0:T(8,128)(2,1)S(1)}, bf16[1,3,16,512]{3,2,1,0:T(8,128)(2,1)}, u32[]{:S(2)}) copy-start(bf16[1,3,16,512]{3,2,1,0:T(8,128)(2,1)} %param.31) | copy-start | bytes 147460
  5.5 5.5 %copy-start.11 = (s32[1,3]{1,0:T(1,128)S(1)}, s32[1,3]{1,0:T(1,128)}, u32[]{:S(2)}) copy-start(s32[1,3]{1,0:T(1,128)} %lengths.7) | copy-start | bytes 40
  5.5 5.5 %copy-start.12 = (s32[24]{0:T(128)S(1)}, s32[24]{0:T(128)}, u32[]{:S(2)}) copy-start(s32[24]{0:T(128)} %home.1) | copy-start | bytes 292
  9.1 1.4 %copy-start = (f32[2,16,72,256]{3,2,1,0:T(8,128)}, f32[2,16,72,256]{3,2,1,0:T(8,128)S(1)}, u32[]{:S(2)}) copy-start(f32[2,16,72,256]{3,2,1,0:T(8,128)S(1)} %shard_map.176.made) | copy-start | bytes 7077892
  10.5 81.0 %copy-start.21 = (f32[64]{0:T(128)S(1)}, f32[64]{0:T(128)}, u32[]{:S(2)}) copy-start(f32[64]{0:T(128)} %param.22) | copy-start | bytes 772
  10.5 81.1 %copy-start.2 = (bf16[1,128,8192]{2,1,0:T(8,128)(2,1)S(1)}, bf16[1,128,8192]{2,1,0:T(8,128)(2,1)}, u32[]{:S(2)}) copy-start(bf16[1,128,8192]{2,1,0:T(8,128)(2,1)} %param.17) | copy-start | bytes 6291460
  10.6 81.1 %copy-start.4 = (bf16[1,128,512]{2,1,0:T(8,128)(2,1)S(1)}, bf16[1,128,512]{2,1,0:T(8,128)(2,1)}, u32[]{:S(2)}) copy-start(bf16[1,128,512]{2,1,0:T(8,128)(2,1)} %param.20) | copy-start | bytes 393220
  10.6 81.1 %copy-start.5 = (bf16[1,128,512]{2,1,0:T(8,128)(2,1)S(1)}, bf16[1,128,512]{2,1,0:T(8,128)(2,1)}, u32[]{:S(2)}) copy-start(bf16[1,128,512]{2,1,0:T(8,128)(2,1)} %param.21) | copy-start | bytes 393220
  91.6 7.6 %copy-start.14 = (bf16[40,16,1024]{2,1,0:T(8,128)(2,1)}, bf16[40,16,1024]{2,1,0:T(8,128)(2,1)S(1)}, u32[]{:S(2)}) copy-start(bf16[40,16,1024]{2,1,0:T(8,128)(2,1)S(1)} %get-tuple-element.8.band) | copy-start | bytes 3932164
  91.7 7.5 %copy-start.19 = (bf16[1,3,4,512]{3,2,1,0:T(4,128)(2,1)S(1)}, bf16[1,3,4,512]{3,2,1,0:T(4,128)(2,1)}, u32[]{:S(2)}) copy-start(bf16[1,3,4,512]{3,2,1,0:T(4,128)(2,1)} %param.32) | copy-start | bytes 36868
  91.7 7.5 %copy-start.20 = (bf16[1,3,4,512]{3,2,1,0:T(4,128)(2,1)S(1)}, bf16[1,3,4,512]{3,2,1,0:T(4,128)(2,1)}, u32[]{:S(2)}) copy-start(bf16[1,3,4,512]{3,2,1,0:T(4,128)(2,1)} %param.33) | copy-start | bytes 36868
  91.7 7.5 %copy-start.17 = (s32[1,3]{1,0:T(1,128)S(1)}, s32[1,3]{1,0:T(1,128)}, u32[]{:S(2)}) copy-start(s32[1,3]{1,0:T(1,128)} %history.1) | copy-start | bytes 40
  99.2 1.9 %copy-start.13 = (bf16[32,2,3,16,512]{4,3,2,1,0:T(8,128)(2,1)S(1)}, bf16[32,2,3,16,512]{4,3,2,1,0:T(8,128)(2,1)}, u32[]{:S(2)}) copy-start(bf16[32,2,3,16,512]{4,3,2,1,0:T(8,128)(2,1)} %get-tuple-element.9.cache) | copy-start | bytes 9437188
  101.1 1.3 %copy-start.15 = (bf16[40,16,1024]{2,1,0:T(8,128)(2,1)S(1)}, bf16[40,16,1024]{2,1,0:T(8,128)(2,1)}, u32[]{:S(2)}) copy-start(bf16[40,16,1024]{2,1,0:T(8,128)(2,1)} %copy-done.14) | copy-start | bytes 3932164
  102.4 1.2 copy-start.16

commit v4 on v3

--- a/solution.py
+++ b/solution.py
@@ -281,6 +281,12 @@
     spread("cache", caches, z_after[1])
     push("cache_core", caches.at[z_after[1]], caches.at[z_after[1]], sibling)
 
+    arrive("extra_1", plane.at[0])
+    push("extra_2", plane.at[z_after[0] // 2], plane.at[z_after[0] // 2], z_before)
+    spread("extra", plane, z_after[0] // 2)
+    arrive("extra_2", plane.at[0])
+    push("extra_3", plane.at[z_after[1] // 2], plane.at[z_after[1] // 2], z_before)
+    spread("extra", plane, z_after[1] // 2)
     arrive("summary", recv.at[pl.ds(0, CHIPS - 1)])
     own_summary.wait()
 
@@ -301,30 +307,19 @@
     lax.fori_loop(0, CHIPS, turn, back[0])
     own_entering = copy_in(entering.at[chip], arrived.at[chip], 2)
 
-    arrive("extra_1", plane.at[0])
-    push("extra_2", plane.at[z_after[0] // 2], plane.at[z_after[0] // 2], z_before)
-    spread("extra", plane, z_after[0] // 2)
+
+    arrive("extra_3", plane.at[0])
+    spread("extra", plane, z_after[2] // 2)
     arrive("cache_3", caches.at[0])
     spread("cache", caches, z_after[2])
     push("cache_core", caches.at[z_after[2]], caches.at[z_after[2]], sibling)
-    arrive("extra_2", plane.at[0])
-    push("extra_3", plane.at[z_after[1] // 2], plane.at[z_after[1] // 2], z_before)
-    spread("extra", plane, z_after[1] // 2)
     arrive("band_4", slot(4))
     push("band_core", slot(2 * core), slot(1), sibling)
     push("band_core", slot(2 * core + 2), slot(3), sibling)
-    arrive("cache_y", caches.at[pl.ds(0, 12)])
-    for i in range(4):
-        for j in range(1, 4):
-            at = ((y + j) % 4) * 8 + ((z + i) % 4) * 2 + core
-            push("cache_core", caches.at[at], caches.at[at], sibling)
-    arrive("extra_3", plane.at[0])
-    spread("extra", plane, z_after[2] // 2)
     own_extra.wait()
     arrive("extra_y", plane.at[pl.ds(0, 12)])
     push("extra_core", plane, extras.at[core], sibling)
     keep_extra = copy_in(plane, extras.at[core], 0)
-
     arrive("state", arrived.at[pl.ds(0, CHIPS - 1)])
     own_entering.wait()
 
@@ -344,6 +339,11 @@
     lax.fori_loop(0, CHIPS, settle, 0)
     push("state_core", other_state, state.at[core], sibling)
     keep_state = copy_in(own_state, state.at[core], 1)
+    arrive("cache_y", caches.at[pl.ds(0, 12)])
+    for i in range(4):
+        for j in range(1, 4):
+            at = ((y + j) % 4) * 8 + ((z + i) % 4) * 2 + core
+            push("cache_core", caches.at[at], caches.at[at], sibling)
 
     arrive("extra_core", extras.at[0])
     arrive("cache_core", caches.at[pl.ds(0, CHIPS)])
@@ -448,21 +448,44 @@
     place = lax.axis_index("ctx")
     first = place * TOK
     one, two = starts_of(lengths)
+    edges = [jnp.int32(0), one, two, jnp.int32(CTX * TOK)]
+    lives = []
+    for s in range(SEQS):
+        begin = jnp.maximum(edges[s], first)
+        present = begin < jnp.minimum(edges[s + 1], first + TOK)
+        lives.append(
+            [
+                present
+                & (begin - edges[s] < j * TOK + TOK - 1)
+                & (history[0, s] - WINDOW + j * TOK + TOK - 1 >= SINKS)
+                for j in range(4)
+            ]
+        )
     copies = [
         pltpu.make_async_copy(band, keys.at[pl.ds(0, 8 * SINK_BLOCK)], sems.at[0]),
         pltpu.make_async_copy(sinks, keys.at[pl.ds(8 * SINK_BLOCK, 8)], sems.at[1]),
     ]
-    for s in range(SEQS):
-        for kv in range(2):
-            copies.append(
-                pltpu.make_async_copy(
-                    cache.at[:, kv, s],
-                    keys.at[pl.ds(8 * CACHE_BLOCK + 32 * s, 32), :, pl.ds(kv * KVH * HD, KVH * HD)],
-                    sems.at[2 + 2 * s + kv],
-                )
-            )
     for copy in copies:
         copy.start()
+
+    def history_copies(s):
+        return [
+            pltpu.make_async_copy(
+                cache.at[:, kv, s],
+                keys.at[pl.ds(8 * CACHE_BLOCK + 32 * s, 32), :, pl.ds(kv * KVH * HD, KVH * HD)],
+                sems.at[2 + 2 * s + kv],
+            )
+            for kv in range(2)
+        ]
+
+    wanted = [lives[s][0] | lives[s][1] | lives[s][2] | lives[s][3] for s in range(SEQS)]
+    for s in range(SEQS):
+
+        @pl.when(wanted[s])
+        def _():
+            for copy in history_copies(s):
+                copy.start()
+
     keys[8 * NULL_BLOCK :] = jnp.zeros((8, 16, 2 * KVH * HD), BF16)
 
     t = first + iota((TOK, TOK), 0)
@@ -486,16 +509,9 @@
     )
     listed[count] = SINK_BLOCK
     count = count + 1
-    edges = [jnp.int32(0), one, two, jnp.int32(CTX * TOK)]
     for s in range(SEQS):
-        begin = jnp.maximum(edges[s], first)
-        present = begin < jnp.minimum(edges[s + 1], first + TOK)
         for j in range(4):
-            live = (
-                present
-                & (begin - edges[s] < j * TOK + TOK - 1)
-                & (history[0, s] - WINDOW + j * TOK + TOK - 1 >= SINKS)
-            )
+            live = lives[s][j]
             block = CACHE_BLOCK + 4 * s + j
 
             @pl.when(live)
@@ -511,6 +527,12 @@
     pairs = lax.div(count + 1, jnp.int32(2))
     for copy in copies:
         copy.wait()
+    for s in range(SEQS):
+
+        @pl.when(wanted[s])
+        def _():
+            for copy in history_copies(s):
+                copy.wait()
 
     per = QH // KVH
     scale = 1.0 / math.sqrt(HD) / math.log(2.0)
@@ -526,15 +548,18 @@
         sums[...] = jnp.zeros(sums.shape, F32)
 
         def score(i, nothing):
-            for part in range(2):
-                block = listed[2 * i + part]
-                key = keys[pl.ds(block * 8, 8), :, lanes].reshape(TOK, HD)
-                offset_rows = bias[block]
-                for r in range(per):
-                    at = slice(r * TOK, (r + 1) * TOK)
-                    got = nt(rows[at, :], key) * scale + offset_rows
-                    scores[2 * i + part, at, :] = got
-                    top[at, :] = jnp.maximum(top[at, :], got)
+            blocks = [listed[2 * i + part] for part in range(2)]
+            key = [keys[pl.ds(b * 8, 8), :, lanes].reshape(TOK, HD) for b in blocks]
+            key = jnp.concatenate(key, axis=0)
+            left_bias, right_bias = bias[blocks[0]], bias[blocks[1]]
+            for r in range(per):
+                at = slice(r * TOK, (r + 1) * TOK)
+                made = nt(rows[at, :], key) * scale
+                left = made[:, :TOK] + left_bias
+                right = made[:, TOK:] + right_bias
+                scores[2 * i, at, :] = left
+                scores[2 * i + 1, at, :] = right
+                top[at, :] = jnp.maximum(top[at, :], jnp.maximum(left, right))
             return nothing
 
         lax.fori_loop(0, pairs, score, 0)
@@ -569,7 +594,7 @@
 SMEM = pl.BlockSpec(memory_space=pltpu.SMEM)
 VMEM = pl.BlockSpec(memory_space=pltpu.VMEM)
 ANY = pl.BlockSpec(memory_space=pl.ANY)
-LIMIT = pltpu.CompilerParams(vmem_limit_bytes=48 * 2**20)
+LIMIT = pltpu.CompilerParams(vmem_limit_bytes=60 * 2**20)
 
 
 def full(shape):
@@ -625,7 +650,7 @@
             pltpu.SemaphoreType.DMA((5,)),
         ],
         compiler_params=pltpu.CompilerParams(
-            collective_id=0, has_side_effects=True, vmem_limit_bytes=48 * 2**20
+            collective_id=0, has_side_effects=True, vmem_limit_bytes=60 * 2**20
         ),
     )(home, lengths, saved, made, cache_keys, cache_values, turn_keys, turn_values)
 

time: 125 us -> 120 us (0.960)
  the two profiles are of different devices: /device:TPU:44 before, /device:TPU:33 now
where the time goes in v4:
time: 120 us; the launch traced here: 118 us
  Pallas kernels  112 us (93%)
  local copies, waits for them, and re-layouts  4.55 us (4%)
    pallas_call x1, Pallas kernels, exchange(): pl.pallas_call(exchange_kernel, out_shape=(jax.ShapeDtypeStruct((2, CHIPS...  84.7 us
    pallas_call x1, Pallas kernels, attention(): pl.pallas_call(attention_kernel, out_shape=jax.ShapeDtypeStruct((TOK, QH...  13.8 us
    pallas_call x1, Pallas kernels, outputs(): pl.pallas_call(output_kernel, grid=(STEPS,), out_shape=jax.ShapeDtypeStru...  8.07 us
    pallas_call x1, Pallas kernels, summaries(): pl.pallas_call(summary_kernel, grid=(STEPS,), out_shape=jax.ShapeDtypeStr...  5.42 us
    unnamed x10, local copies, waits for them, and re-layouts  2.87 us

profile of v4, /device:TPU:33, one launch (start us, length us, event | category | flops | bytes accessed | tf_op | source)
XLA Modules:
  0.0 118.1 jit_solution(7859781754935415081)
XLA Ops:
  0.6 1.4 %copy.22 = bf16[1,128,64]{2,1,0:T(8,128)(2,1)} copy(bf16[1,128,64]{1,2,0:T(8,128)(2,1)} %param.18) | data formatting | bytes 32768 | tf_op args[1]
  2.1 1.4 %copy.23 = bf16[1,128,64]{2,1,0:T(8,128)(2,1)} copy(bf16[1,128,64]{1,2,0:T(8,128)(2,1)} %param.19) | data formatting | bytes 32768 | tf_op args[2]
  3.5 0.0 copy-start
  3.5 5.4 %shard_map.176.made = f32[2,16,72,256]{3,2,1,0:T(8,128)} custom-call(s32[1,3]{1,0:T(1,128)} %lengths.7, bf16[128,8192]{1,0:T(8,128)(2,1)} %bitcast.17, bf16[128,64]{1,0:T(8,128)(2,1)} %bitcast.23, bf16[128,64]{1,0:T(8,128)(2,1)} %bitcast.25, bf16[128,512]{1,0:T(8,128)(2,1)} %bitcast.21), custom_call_target="tpu_custom_call" | custom-call | tf_op jit(solution)/shard_map/pallas_call | solution.py:609
  8.9 0.0 copy-done
  8.9 0.0 copy-start.3
  8.9 0.1 convert_element_type.9
  9.0 0.2 convert_element_type.10
  9.2 0.8 copy.25.saved
  10.0 84.7 %shard_map.177 = (bf16[2,16,64,256]{3,2,1,0:T(8,128)(2,1)}, bf16[2,16,2,64,256]{4,3,2,1,0:T(8,128)(2,1)}, bf16[32,2,3,16,512]{4,3,2,1,0:T(8,128)(2,1)}, bf16[40,16,1024]{2,1,0:T(8,128)(2,1)}) custom-call(s32[24]{0:T(128)} %home.1, s32[1,3]{1,0:T(1,128)} %lengths.7, bf16[3,64,256]{2,1,0:T(8,128)(2,1)} %copy.25.saved, f32[2,16,72,256]{3,2,1,0:T(8,128)} %shard_map.176.made, ...), custom_call_target="tpu_custom_call" | custom-call | tf_op jit(solution)/shard_map/pallas_call | solution.py:627
  94.7 0.0 copy-done.3
  94.7 0.7 broadcast_in_dim.9
  95.4 0.0 copy-start.1
  95.4 0.0 copy-start.2
  95.4 8.1 %shard_map.178 = bf16[128,8192]{1,0:T(8,128)(2,1)} custom-call(s32[1,3]{1,0:T(1,128)} %lengths.7, bf16[128,8192]{1,0:T(8,128)(2,1)} %bitcast.18, bf16[128,64]{1,0:T(8,128)(2,1)} %bitcast.24, bf16[128,64]{1,0:T(8,128)(2,1)} %bitcast.26, bf16[128,512]{1,0:T(8,128)(2,1)} %bitcast.22, bf16[128,512]{1,0:T(8,128)(2,1)} %bitcast.28, f32[1,8192]{1,0:T(1,128)} %bitcast.29, ...), custom_call_target="tpu_custom_call" | custom-call | tf_op jit(solution)/shard_map/pallas_call | solution.py:659
  103.5 0.0 copy-done.1
  103.5 0.0 copy-done.2
  103.5 0.7 fusion.2
  104.3 13.8 %shard_map.179 = bf16[128,4096]{1,0:T(8,128)(2,1)} custom-call(s32[1,3]{1,0:T(1,128)} %lengths.7, s32[1,3]{1,0:T(1,128)} %history.1, bf16[128,4096]{1,0:T(8,128)(2,1)} %bitcast.34, bf16[40,16,1024]{2,1,0:T(8,128)(2,1)} %get-tuple-element.8.band, bf16[8,16,1024]{2,1,0:T(8,128)(2,1)} %bitcast.27, bf16[32,2,3,16,512]{4,3,2,1,0:T(8,128)(2,1)} %get-tuple-element.9.cache), custom_call_target="tpu_custom_call" | custom-call | flops 2500000000 | bytes 8000000 | tf_op jit(solution)/shard_map/pallas_call | solution.py:682
  (2 shorter events, 0.0 us)
Async XLA Ops:
  3.5 5.4 %copy-start = (f32[1,3,2,8192]{3,2,1,0:T(2,128)S(1)}, f32[1,3,2,8192]{3,2,1,0:T(2,128)}, u32[]{:S(2)}) copy-start(f32[1,3,2,8192]{3,2,1,0:T(2,128)} %param.23) | copy-start | bytes 589828
  8.9 85.8 %copy-start.3 = (f32[64]{0:T(128)S(1)}, f32[64]{0:T(128)}, u32[]{:S(2)}) copy-start(f32[64]{0:T(128)} %param.22) | copy-start | bytes 772
  95.4 8.1 %copy-start.1 = (bf16[1,3,4,512]{3,2,1,0:T(4,128)(2,1)S(1)}, bf16[1,3,4,512]{3,2,1,0:T(4,128)(2,1)}, u32[]{:S(2)}) copy-start(bf16[1,3,4,512]{3,2,1,0:T(4,128)(2,1)} %param.32) | copy-start | bytes 36868
  95.4 8.1 %copy-start.2 = (bf16[1,3,4,512]{3,2,1,0:T(4,128)(2,1)S(1)}, bf16[1,3,4,512]{3,2,1,0:T(4,128)(2,1)}, u32[]{:S(2)}) copy-start(bf16[1,3,4,512]{3,2,1,0:T(4,128)(2,1)} %param.33) | copy-start | bytes 36868

commit v5 on v4

--- a/solution.py
+++ b/solution.py
@@ -70,39 +70,6 @@
     return jnp.where(rows == step * HEADS + lanes // P_SIZE, 1.0, 0.0).astype(BF16)
 
 
-def summary_kernel(lengths, x, dt, dlog, write, send, weight):
-    step = pl.program_id(0)
-    first = lax.axis_index("ctx") * TOK
-    one, two = starts_of(lengths)
-    one, two = one - first, two - first
-    mask = jnp.where(same_causal(one, two), 1.0, 0.0).astype(BF16)
-    rates = dlog[...]
-
-    @pl.when(step == 0)
-    def _():
-        run = nn(mask, rates).T
-        u = iota((1, TOK), 1)
-        last = (TOK - 1 >= one).astype(I32) + (TOK - 1 >= two).astype(I32)
-        held = segment(u, one, two) == last
-        gap = jnp.where(held, run[:, TOK - 1 :] - run, -jnp.inf)
-        weight[...] = jnp.exp(gap) * dt[...].astype(F32).T
-
-    turned = write[...].astype(F32).T
-    for k in range(HEADS):
-        row = weight[pl.ds(step * HEADS + k, 1), :]
-        b = k // G
-        loads = (row * turned[b * N : (b + 1) * N]).astype(BF16)
-        made = nn(loads, x[:, k * P_SIZE : (k + 1) * P_SIZE])
-        lane = (k % 2) * P_SIZE
-        j = k // 2
-        send[j % 2, j // 2, :N, lane : lane + P_SIZE] = made
-    spread = nn(rates, spread_matrix(step)).astype(BF16)
-    carry = jnp.exp(nn(mask[TOK - 16 :], spread)[15:16])
-    for j in range(HEADS // 2):
-        row = carry[:, j * PAIR : (j + 1) * PAIR]
-        send[j % 2, j // 2, N:, :] = jnp.broadcast_to(row, (8, PAIR))
-
-
 def await_bytes(ref, sem):
     pltpu.make_async_copy(ref, ref, sem).wait()
 
@@ -111,7 +78,10 @@
     home,
     lengths,
     saved,
-    made,
+    x,
+    steps,
+    rates,
+    write,
     cache_keys,
     cache_values,
     turn_keys,
@@ -120,6 +90,9 @@
     extras,
     caches,
     band,
+    inputs,
+    weight,
+    made,
     theirs,
     packed,
     recv,
@@ -135,12 +108,12 @@
     local,
 ):
     group, me = lax.axis_index("sess"), lax.axis_index("ctx")
-    x, deep = group // 2, group % 2
+    across, deep = group // 2, group % 2
     y, z, core = me // 8, (me // 2) % 4, me % 2
     chip = me // 2
     sibling = me + 1 - 2 * core
     partner = group + 1 - 2 * deep
-    x_groups = [((x + i) % 4) * 2 + deep for i in range(1, 4)]
+    x_groups = [((across + i) % 4) * 2 + deep for i in range(1, 4)]
     y_peers = [((y + i) % 4) * 8 + z * 2 + core for i in range(1, 4)]
     z_before = y * 8 + ((z + 3) % 4) * 2 + core
     z_after = [y * 8 + ((z + i) % 4) * 2 + core for i in range(1, 4)]
@@ -159,6 +132,7 @@
         copy_in(turn_keys, band.at[pl.ds(8 * REACH, 8), :, pl.ds(0, half)], 2),
         copy_in(turn_values, band.at[pl.ds(8 * REACH, 8), :, pl.ds(half, half)], 3),
         copy_in(saved, stored.at[group], 4),
+        copy_in(x, inputs, 5),
     ]
 
     barrier = pltpu.get_barrier_semaphore()
@@ -201,7 +175,6 @@
     push("home_z", saved, stored.at[group], me, partner)
     for to in x_groups:
         push("home_x", saved, stored.at[group], me, to)
-    push("pair", made.at[1 - core], theirs, sibling)
     mine[2].wait()
     mine[3].wait()
     push("band_2", slot(0), slot(2), onward)
@@ -211,11 +184,44 @@
     spread("cache", caches, me)
     push("cache_core", caches.at[me], caches.at[me], sibling)
 
+    one, two = starts_of(lengths)
+    here_one, here_two = one - me * TOK, two - me * TOK
+    mask = jnp.where(same_causal(here_one, here_two), 1.0, 0.0).astype(BF16)
+    run = nt(rates[...], mask)
+    u = iota((1, TOK), 1)
+    last = (TOK - 1 >= here_one).astype(I32) + (TOK - 1 >= here_two).astype(I32)
+    held = segment(u, here_one, here_two) == last
+    gap = jnp.where(held, run[:, TOK - 1 :] - run, -jnp.inf)
+    weight[...] = jnp.exp(gap) * steps[...].astype(F32)
+    turned_rates = rates[...].astype(F32).T.astype(BF16)
+    mine[5].wait()
+
+    def summarize(step, nothing):
+        turned = write[:, pl.ds(pl.multiple_of(step * 2 * N, 2 * N), 2 * N)].astype(F32).T
+        spread_rates = nn(turned_rates, spread_matrix(step)).astype(BF16)
+        carry = jnp.exp(nn(mask[TOK - 16 :], spread_rates)[15:16])
+        for k in range(HEADS):
+            row = weight[pl.ds(step * HEADS + k, 1), :]
+            b = k // G
+            loads = (row * turned[b * N : (b + 1) * N]).astype(BF16)
+            at = pl.multiple_of(step * WIDE + k * P_SIZE, P_SIZE)
+            lane = (k % 2) * P_SIZE
+            j = k // 2
+            made[j % 2, step * (CHIPS // STEPS) + j // 2, :N, lane : lane + P_SIZE] = nn(
+                loads, inputs[:, pl.ds(at, P_SIZE)]
+            )
+        for j in range(HEADS // 2):
+            row = carry[:, j * PAIR : (j + 1) * PAIR]
+            made[j % 2, step * (CHIPS // STEPS) + j // 2, N:, :] = jnp.broadcast_to(row, (8, PAIR))
+        part = pl.ds(step * (CHIPS // STEPS), CHIPS // STEPS)
+        push("pair", made.at[1 - core, part], theirs.at[part], sibling)
+        return nothing
+
+    lax.fori_loop(0, STEPS, summarize, 0)
+
     arrive("home_z", stored.at[0])
     for to in x_groups:
         push("home_x", stored.at[partner], stored.at[partner], me, to)
-
-    one, two = starts_of(lengths)
 
     def inside(c):
         end = c * TOK + TOK - 1
@@ -378,7 +384,7 @@
 )
 
 
-def output_kernel(lengths, x, dt, dlog, write, read, gain, state, extra, out, run_rows, step_rows):
+def output_kernel(lengths, gain, x, steps, rates, write, read, state, extra, out, run_rows, step_rows):
     step = pl.program_id(0)
     first = lax.axis_index("ctx") * TOK
     one, two = starts_of(lengths)
@@ -386,18 +392,17 @@
     seen = same_causal(one, two)
     mask = jnp.where(seen, 1.0, 0.0).astype(BF16)
     bias = jnp.where(seen, 0.0, -jnp.inf)
-    rates = dlog[...]
 
     @pl.when(step == 0)
     def _():
-        run_rows[...] = nn(mask, rates).T
-        step_rows[...] = dt[...].astype(F32).T
+        run_rows[...] = nt(rates[...], mask)
+        step_rows[...] = steps[...].astype(F32)
 
     t = iota((TOK, N), 0)
     new_one = (t >= one) & (t < two) & (one >= 0)
     new_two = (t >= two) & (two >= 0)
-    spread = nn(rates, spread_matrix(step)).astype(BF16)
-    run = nn(mask, spread)
+    turned = rates[...].astype(F32).T.astype(BF16)
+    run = nn(mask, nn(turned, spread_matrix(step)).astype(BF16))
     for b in range(HEADS // G):
         c = read[:, b * N : (b + 1) * N].astype(F32)
         c_in = jnp.where(new_one | new_two, 0.0, c).astype(BF16)
@@ -422,7 +427,7 @@
                 result = (
                     nn(mixing, x_h)
                     + jnp.exp(run_t) * from_state[:, i * P_SIZE : (i + 1) * P_SIZE]
-                    + gain[:, lanes] * x_h.astype(F32)
+                    + gain[step * HEADS + k] * x_h.astype(F32)
                 )
                 out[:, lanes] = result.astype(BF16)
 
@@ -432,7 +437,8 @@
     history,
     queries,
     band,
-    sinks,
+    sink_keys,
+    sink_values,
     cache,
     out,
     keys,
@@ -463,7 +469,6 @@
         )
     copies = [
         pltpu.make_async_copy(band, keys.at[pl.ds(0, 8 * SINK_BLOCK)], sems.at[0]),
-        pltpu.make_async_copy(sinks, keys.at[pl.ds(8 * SINK_BLOCK, 8)], sems.at[1]),
     ]
     for copy in copies:
         copy.start()
@@ -487,6 +492,12 @@
                 copy.start()
 
     keys[8 * NULL_BLOCK :] = jnp.zeros((8, 16, 2 * KVH * HD), BF16)
+    half = KVH * HD
+    keys[8 * SINK_BLOCK + 1 : 8 * CACHE_BLOCK] = jnp.zeros((7, 16, 2 * half), BF16)
+    for kv, sinks in enumerate((sink_keys, sink_values)):
+        parts = [sinks[s].astype(F32) for s in range(SEQS)] + [jnp.zeros((4, half), F32)]
+        both = jnp.concatenate(parts, axis=0).astype(BF16)
+        keys[8 * SINK_BLOCK, :, kv * half : (kv + 1) * half] = both
 
     t = first + iota((TOK, TOK), 0)
     u = iota((TOK, TOK), 1)
@@ -605,25 +616,20 @@
     return pl.BlockSpec((rows, width), lambda i: (0, i))
 
 
-def summaries(lengths, x, dt, dlog, write):
-    return pl.pallas_call(
-        summary_kernel,
-        grid=(STEPS,),
-        out_shape=jax.ShapeDtypeStruct((2, CHIPS, N + 8, PAIR), F32),
-        in_specs=[
-            SMEM,
-            lane_block(TOK, WIDE),
-            full((TOK, H)),
-            full((TOK, H)),
-            lane_block(TOK, 2 * N),
-        ],
-        out_specs=pl.BlockSpec((2, CHIPS // STEPS, N + 8, PAIR), lambda i: (0, i, 0, 0)),
-        scratch_shapes=[pltpu.VMEM((H, TOK), F32)],
-        compiler_params=LIMIT,
-    )(lengths, x, dt, dlog, write)
-
-
-def exchange(groups, home, lengths, saved, made, cache_keys, cache_values, turn_keys, turn_values):
+def exchange(
+    groups,
+    home,
+    lengths,
+    saved,
+    x,
+    steps,
+    rates,
+    write,
+    cache_keys,
+    cache_values,
+    turn_keys,
+    turn_values,
+):
     return pl.pallas_call(
         exchange_kernel,
         out_shape=(
@@ -632,9 +638,12 @@
             jax.ShapeDtypeStruct((CTX, 2) + cache_keys.shape, BF16),
             jax.ShapeDtypeStruct((8 * (REACH + 1), 16, 2 * KVH * HD), BF16),
         ),
-        in_specs=[SMEM, SMEM, ANY, VMEM, ANY, ANY, ANY, ANY],
+        in_specs=[SMEM, SMEM, ANY, ANY, VMEM, VMEM, VMEM, ANY, ANY, ANY, ANY],
         out_specs=(ANY, ANY, ANY, ANY),
         scratch_shapes=[
+            pltpu.VMEM((TOK, H * P_SIZE), BF16),
+            pltpu.VMEM((H, TOK), F32),
+            pltpu.VMEM((2, CHIPS, N + 8, PAIR), F32),
             pltpu.VMEM((CHIPS, N + 8, PAIR), F32),
             pltpu.VMEM((CHIPS, ROWS, PAIR), BF16),
             pltpu.VMEM((CHIPS, ROWS, PAIR), BF16),
@@ -647,42 +656,54 @@
             pltpu.VMEM((CHIPS, 2, N, PAIR), BF16),
             pltpu.SemaphoreType.DMA((len(EXCHANGES),)),
             pltpu.SemaphoreType.DMA((len(EXCHANGES),)),
-            pltpu.SemaphoreType.DMA((5,)),
+            pltpu.SemaphoreType.DMA((6,)),
         ],
         compiler_params=pltpu.CompilerParams(
             collective_id=0, has_side_effects=True, vmem_limit_bytes=60 * 2**20
         ),
-    )(home, lengths, saved, made, cache_keys, cache_values, turn_keys, turn_values)
-
-
-def outputs(lengths, x, dt, dlog, write, read, gain, state, extra):
+    )(
+        home,
+        lengths,
+        saved,
+        x,
+        steps,
+        rates,
+        write,
+        cache_keys,
+        cache_values,
+        turn_keys,
+        turn_values,
+    )
+
+
+def outputs(lengths, gain, x, steps, rates, write, read, state, extra):
     return pl.pallas_call(
         output_kernel,
         grid=(STEPS,),
         out_shape=jax.ShapeDtypeStruct((TOK, H * P_SIZE), BF16),
         in_specs=[
             SMEM,
+            SMEM,
             lane_block(TOK, WIDE),
-            full((TOK, H)),
-            full((TOK, H)),
+            full((H, TOK)),
+            full((H, TOK)),
             lane_block(TOK, 2 * N),
             lane_block(TOK, 2 * N),
-            lane_block(1, WIDE),
             pl.BlockSpec((2, CHIPS // STEPS, N, PAIR), lambda i: (0, i, 0, 0)),
             pl.BlockSpec((2, CHIPS // STEPS, 2, N, PAIR), lambda i: (0, i, 0, 0, 0)),
         ],
         out_specs=lane_block(TOK, WIDE),
         scratch_shapes=[pltpu.VMEM((H, TOK), F32), pltpu.VMEM((H, TOK), F32)],
         compiler_params=LIMIT,
-    )(lengths, x, dt, dlog, write, read, gain, state, extra)
-
-
-def attention(lengths, history, queries, band, sinks, cache):
+    )(lengths, gain, x, steps, rates, write, read, state, extra)
+
+
+def attention(lengths, history, queries, band, sink_keys, sink_values, cache):
     rows = (QH // KVH) * TOK
     return pl.pallas_call(
         attention_kernel,
         out_shape=jax.ShapeDtypeStruct((TOK, QH * HD), BF16),
-        in_specs=[SMEM, SMEM, VMEM, ANY, ANY, ANY],
+        in_specs=[SMEM, SMEM, VMEM, ANY, VMEM, VMEM, ANY],
         out_specs=VMEM,
         scratch_shapes=[
             pltpu.VMEM((8 * BLOCKS, 16, 2 * KVH * HD), BF16),
@@ -699,7 +720,7 @@
         cost_estimate=pl.CostEstimate(
             flops=2_500_000_000, bytes_accessed=8_000_000, transcendentals=5_000_000
         ),
-    )(lengths, history, queries, band, sinks, cache)
+    )(lengths, history, queries, band, sink_keys, sink_values, cache)
 
 
 def shards(
@@ -721,31 +742,30 @@
     sink_keys,
     sink_values,
 ):
-    x, dt, dlog = mamba_input[0], step_size[0], decay_log[0]
+    x, steps, rates = mamba_input[0], step_size[0].T, decay_log[0].T
     write, read = state_write[0], state_read[0]
     saved = saved_states[0].astype(BF16).reshape(SEQS, 2, P_SIZE, N)
     saved = saved.transpose(0, 3, 1, 2).reshape(SEQS, N, PAIR)
-    sinks = jnp.concatenate(
-        [sink_keys[0].reshape(SEQS * SINKS, -1), sink_values[0].reshape(SEQS * SINKS, -1)], axis=1
-    )
-    sinks = jnp.pad(sinks, ((0, TOK - SEQS * SINKS), (0, 0))).reshape(8, 16, 2 * KVH * HD)
-    gain = jnp.repeat(skip_gain, P_SIZE)[None]
-
-    made = summaries(turn_lengths, x, dt, dlog, write)
+
     groups = lax.axis_size("sess")
     state, extras, caches, band = exchange(
         groups,
         home_slot,
         turn_lengths,
         saved,
-        made,
+        x,
+        steps,
+        rates,
+        write,
         cache_keys[0],
         cache_values[0],
         turn_keys[0].reshape(8, 16, KVH * HD),
         turn_values[0].reshape(8, 16, KVH * HD),
     )
-    attended = attention(turn_lengths, history_lengths, queries[0], band, sinks, caches)
-    mixed = outputs(turn_lengths, x, dt, dlog, write, read, gain, state, extras)
+    attended = attention(
+        turn_lengths, history_lengths, queries[0], band, sink_keys[0], sink_values[0], caches
+    )
+    mixed = outputs(turn_lengths, skip_gain, x, steps, rates, write, read, state, extras)
     return (mixed[None], attended[None])
 
 

time: 120 us -> 109 us (0.908); the launches traced: 118 us -> 109 us
  Pallas kernels: 112 us -> 106 us
  local copies, waits for them, and re-layouts: 4.55 us -> 0.97 us
    pallas_call x1, Pallas kernels: 84.7 us -> 79 us  [exchange(): pl.pallas_call(exchange_kernel, out_shape=(jax.ShapeDtypeStruct((2, CHIPS...]
    pallas_call x1 -> x0, Pallas kernels: 5.42 us -> none  [summaries(): pl.pallas_call(summary_kernel, grid=(STEPS,), out_shape=jax.ShapeDtypeStr...]
    pallas_call x1, Pallas kernels: 13.8 us -> 19.1 us  [attention(): pl.pallas_call(attention_kernel, out_shape=jax.ShapeDtypeStruct((TOK, QH...]
    unnamed x10 -> x0, local copies, waits for them, and re-layouts: 2.87 us -> none
where the time goes in v5:
time: 109 us
  Pallas kernels  106 us (97%)
    pallas_call x1, Pallas kernels, exchange(): pl.pallas_call(exchange_kernel, out_shape=(jax.ShapeDtypeStruct((2, CHIPS...  79 us
    pallas_call x1, Pallas kernels, attention(): pl.pallas_call(attention_kernel, out_shape=jax.ShapeDtypeStruct((TOK, QH...  19.1 us
    pallas_call x1, Pallas kernels, outputs(): pl.pallas_call(output_kernel, grid=(STEPS,), out_shape=jax.ShapeDtypeStru...  8.11 us

profile of v5, /device:TPU:33, one launch (start us, length us, event | category | flops | bytes accessed | tf_op | source)
XLA Modules:
  0.0 108.8 jit_solution(10834004214640918291)
XLA Ops:
  0.6 1.0 convert_element_type.7
  1.6 0.2 convert_element_type.8
  1.8 0.8 copy.21.saved
  2.6 79.0 %shard_map.176 = (bf16[2,16,64,256]{3,2,1,0:T(8,128)(2,1)}, bf16[2,16,2,64,256]{4,3,2,1,0:T(8,128)(2,1)}, bf16[32,2,3,16,512]{4,3,2,1,0:T(8,128)(2,1)}, bf16[40,16,1024]{2,1,0:T(8,128)(2,1)}) custom-call(s32[24]{0:T(128)} %home.1, s32[1,3]{1,0:T(1,128)} %lengths.5, bf16[3,64,256]{2,1,0:T(8,128)(2,1)} %copy.21.saved, bf16[128,8192]{1,0:T(8,128)(2,1)} %bitcast.21, ...), custom_call_target="tpu_custom_call" | custom-call | tf_op jit(solution)/shard_map/pallas_call | solution.py:633
  81.6 8.1 %shard_map.177 = bf16[128,8192]{1,0:T(8,128)(2,1)} custom-call(s32[1,3]{1,0:T(1,128)} %lengths.5, f32[64]{0:T(128)} %gain.1, bf16[128,8192]{1,0:T(8,128)(2,1)} %bitcast.22, bf16[64,128]{1,0:T(8,128)(2,1)} %bitcast.31, bf16[64,128]{1,0:T(8,128)(2,1)} %bitcast.33, bf16[128,512]{1,0:T(8,128)(2,1)} %bitcast.26, bf16[128,512]{1,0:T(8,128)(2,1)} %bitcast.27, ...), custom_call_target="tpu_custom_call" | custom-call | tf_op jit(solution)/shard_map/pallas_call | solution.py:680
  89.7 19.1 %shard_map.178 = bf16[128,4096]{1,0:T(8,128)(2,1)} custom-call(s32[1,3]{1,0:T(1,128)} %lengths.5, s32[1,3]{1,0:T(1,128)} %history.1, bf16[128,4096]{1,0:T(8,128)(2,1)} %bitcast.36, bf16[40,16,1024]{2,1,0:T(8,128)(2,1)} %get-tuple-element.8.band, bf16[3,4,512]{2,1,0:T(4,128)(2,1)} %bitcast.37, bf16[3,4,512]{2,1,0:T(4,128)(2,1)} %bitcast.38, ...), custom_call_target="tpu_custom_call" | custom-call | flops 2500000000 | bytes 8000000 | tf_op jit(solution)/shard_map/pallas_call | solution.py:703

commit v6 on v5

--- a/solution.py
+++ b/solution.py
@@ -77,11 +77,13 @@
 def exchange_kernel(
     home,
     lengths,
+    gain,
     saved,
     x,
     steps,
     rates,
     write,
+    read,
     cache_keys,
     cache_values,
     turn_keys,
@@ -90,8 +92,12 @@
     extras,
     caches,
     band,
+    partial,
     inputs,
     weight,
+    run_rows,
+    step_rows,
+    inner,
     made,
     theirs,
     packed,
@@ -186,8 +192,12 @@
 
     one, two = starts_of(lengths)
     here_one, here_two = one - me * TOK, two - me * TOK
-    mask = jnp.where(same_causal(here_one, here_two), 1.0, 0.0).astype(BF16)
+    seen = same_causal(here_one, here_two)
+    mask = jnp.where(seen, 1.0, 0.0).astype(BF16)
+    bias = jnp.where(seen, 0.0, -jnp.inf)
     run = nt(rates[...], mask)
+    run_rows[...] = run
+    step_rows[...] = steps[...].astype(F32)
     u = iota((1, TOK), 1)
     last = (TOK - 1 >= here_one).astype(I32) + (TOK - 1 >= here_two).astype(I32)
     held = segment(u, here_one, here_two) == last
@@ -262,12 +272,35 @@
     lax.fori_loop(0, CHIPS, combine, 0)
     own_summary = copy_in(packed.at[chip], recv.at[chip], 0)
 
+    def within(step, nothing):
+        spread_rates = nn(turned_rates, spread_matrix(step)).astype(BF16)
+        run_wide = nn(mask, spread_rates)
+        two_groups = pl.ds(pl.multiple_of(step * 2 * N, 2 * N), 2 * N)
+        writes, reads = write[:, two_groups], read[:, two_groups]
+        for b in range(HEADS // G):
+            crossed = nt(reads[:, b * N : (b + 1) * N], writes[:, b * N : (b + 1) * N])
+            for k in range(b * G, (b + 1) * G):
+                at = pl.ds(step * HEADS + k, 1)
+                lanes = pl.ds(pl.multiple_of(step * WIDE + k * P_SIZE, P_SIZE), P_SIZE)
+                decay = run_wide[:, k * P_SIZE : (k + 1) * P_SIZE] - run_rows[at, :] + bias
+                mixing = (crossed * jnp.exp(decay) * step_rows[at, :]).astype(BF16)
+                x_h = inputs[:, lanes]
+                inner[:, lanes] = nn(mixing, x_h) + gain[step * HEADS + k] * x_h.astype(F32)
+        return nothing
+
+    def hand_on(step):
+        lanes = pl.ds(step * WIDE, WIDE)
+        return copy_in(inner.at[:, lanes], partial.at[:, lanes], 6 + step)
+
     arrive("cache_1", caches.at[0])
     push("cache_2", caches.at[z_after[0]], caches.at[z_after[0]], z_before)
     spread("cache", caches, z_after[0])
     push("cache_core", caches.at[z_after[0]], caches.at[z_after[0]], sibling)
     arrive("band_2", slot(2))
     push("band_4", slot(2), slot(4), onward)
+
+    lax.fori_loop(0, 2, within, 0)
+    handed = [hand_on(0), hand_on(1)]
 
     mine[4].wait()
     arrive("home_x", stored.at[pl.ds(0, 6)])
@@ -281,6 +314,9 @@
     for to in y_peers:
         push("extra_y", extra, plane.at[chip], to)
     own_extra = copy_in(extra, plane.at[chip], 1)
+
+    lax.fori_loop(2, STEPS, within, 0)
+    handed += [hand_on(2), hand_on(3)]
 
     arrive("cache_2", caches.at[0])
     push("cache_3", caches.at[z_after[1]], caches.at[z_after[1]], z_before)
@@ -355,8 +391,8 @@
     arrive("cache_core", caches.at[pl.ds(0, CHIPS)])
     arrive("band_core", band.at[pl.ds(0, 16)])
     arrive("state_core", state.at[0])
-    keep_extra.wait()
-    keep_state.wait()
+    for copy in handed + [keep_extra, keep_state]:
+        copy.wait()
     for kind, ref in counts.items():
         await_bytes(ref, sent.at[kinds[kind]])
 
@@ -384,20 +420,12 @@
 )
 
 
-def output_kernel(lengths, gain, x, steps, rates, write, read, state, extra, out, run_rows, step_rows):
+def output_kernel(lengths, rates, read, partial, state, extra, out):
     step = pl.program_id(0)
     first = lax.axis_index("ctx") * TOK
     one, two = starts_of(lengths)
     one, two = one - first, two - first
-    seen = same_causal(one, two)
-    mask = jnp.where(seen, 1.0, 0.0).astype(BF16)
-    bias = jnp.where(seen, 0.0, -jnp.inf)
-
-    @pl.when(step == 0)
-    def _():
-        run_rows[...] = nt(rates[...], mask)
-        step_rows[...] = steps[...].astype(F32)
-
+    mask = jnp.where(same_causal(one, two), 1.0, 0.0).astype(BF16)
     t = iota((TOK, N), 0)
     new_one = (t >= one) & (t < two) & (one >= 0)
     new_two = (t >= two) & (two >= 0)
@@ -408,7 +436,6 @@
         c_in = jnp.where(new_one | new_two, 0.0, c).astype(BF16)
         c_one = jnp.where(new_one, c, 0.0).astype(BF16)
         c_two = jnp.where(new_two, c, 0.0).astype(BF16)
-        both = nt(read[:, b * N : (b + 1) * N], write[:, b * N : (b + 1) * N])
         for j in range(G // 2):
             chunk = b * (G // 2) + j
             from_state = (
@@ -416,20 +443,9 @@
                 + nn(c_one, extra[chunk % 2, chunk // 2, 0])
                 + nn(c_two, extra[chunk % 2, chunk // 2, 1])
             )
-            for i in range(2):
-                k = chunk * 2 + i
-                lanes = slice(k * P_SIZE, (k + 1) * P_SIZE)
-                at = pl.ds(step * HEADS + k, 1)
-                run_t = run[:, lanes]
-                decay = jnp.exp(run_t - run_rows[at, :] + bias)
-                mixing = (both * decay * step_rows[at, :]).astype(BF16)
-                x_h = x[:, lanes]
-                result = (
-                    nn(mixing, x_h)
-                    + jnp.exp(run_t) * from_state[:, i * P_SIZE : (i + 1) * P_SIZE]
-                    + gain[step * HEADS + k] * x_h.astype(F32)
-                )
-                out[:, lanes] = result.astype(BF16)
+            lanes = slice(chunk * PAIR, (chunk + 1) * PAIR)
+            result = partial[:, lanes] + jnp.exp(run[:, lanes]) * from_state
+            out[:, lanes] = result.astype(BF16)
 
 
 def attention_kernel(
@@ -620,11 +636,13 @@
     groups,
     home,
     lengths,
+    gain,
     saved,
     x,
     steps,
     rates,
     write,
+    read,
     cache_keys,
     cache_values,
     turn_keys,
@@ -637,12 +655,16 @@
             jax.ShapeDtypeStruct((2, CHIPS, 2, N, PAIR), BF16),
             jax.ShapeDtypeStruct((CTX, 2) + cache_keys.shape, BF16),
             jax.ShapeDtypeStruct((8 * (REACH + 1), 16, 2 * KVH * HD), BF16),
+            jax.ShapeDtypeStruct((TOK, H * P_SIZE), F32),
         ),
-        in_specs=[SMEM, SMEM, ANY, ANY, VMEM, VMEM, VMEM, ANY, ANY, ANY, ANY],
-        out_specs=(ANY, ANY, ANY, ANY),
+        in_specs=[SMEM, SMEM, SMEM, ANY, ANY, VMEM, VMEM, VMEM, VMEM, ANY, ANY, ANY, ANY],
+        out_specs=(ANY, ANY, ANY, ANY, ANY),
         scratch_shapes=[
             pltpu.VMEM((TOK, H * P_SIZE), BF16),
             pltpu.VMEM((H, TOK), F32),
+            pltpu.VMEM((H, TOK), F32),
+            pltpu.VMEM((H, TOK), F32),
+            pltpu.VMEM((TOK, H * P_SIZE), F32),
             pltpu.VMEM((2, CHIPS, N + 8, PAIR), F32),
             pltpu.VMEM((CHIPS, N + 8, PAIR), F32),
             pltpu.VMEM((CHIPS, ROWS, PAIR), BF16),
@@ -656,7 +678,7 @@
             pltpu.VMEM((CHIPS, 2, N, PAIR), BF16),
             pltpu.SemaphoreType.DMA((len(EXCHANGES),)),
             pltpu.SemaphoreType.DMA((len(EXCHANGES),)),
-            pltpu.SemaphoreType.DMA((6,)),
+            pltpu.SemaphoreType.DMA((10,)),
         ],
         compiler_params=pltpu.CompilerParams(
             collective_id=0, has_side_effects=True, vmem_limit_bytes=60 * 2**20
@@ -664,11 +686,13 @@
     )(
         home,
         lengths,
+        gain,
         saved,
         x,
         steps,
         rates,
         write,
+        read,
         cache_keys,
         cache_values,
         turn_keys,
@@ -676,26 +700,22 @@
     )
 
 
-def outputs(lengths, gain, x, steps, rates, write, read, state, extra):
+def outputs(lengths, rates, read, partial, state, extra):
     return pl.pallas_call(
         output_kernel,
         grid=(STEPS,),
         out_shape=jax.ShapeDtypeStruct((TOK, H * P_SIZE), BF16),
         in_specs=[
             SMEM,
-            SMEM,
-            lane_block(TOK, WIDE),
-            full((H, TOK)),
             full((H, TOK)),
             lane_block(TOK, 2 * N),
-            lane_block(TOK, 2 * N),
+            lane_block(TOK, WIDE),
             pl.BlockSpec((2, CHIPS // STEPS, N, PAIR), lambda i: (0, i, 0, 0)),
             pl.BlockSpec((2, CHIPS // STEPS, 2, N, PAIR), lambda i: (0, i, 0, 0, 0)),
         ],
         out_specs=lane_block(TOK, WIDE),
-        scratch_shapes=[pltpu.VMEM((H, TOK), F32), pltpu.VMEM((H, TOK), F32)],
         compiler_params=LIMIT,
-    )(lengths, gain, x, steps, rates, write, read, state, extra)
+    )(lengths, rates, read, partial, state, extra)
 
 
 def attention(lengths, history, queries, band, sink_keys, sink_values, cache):
@@ -748,15 +768,17 @@
     saved = saved.transpose(0, 3, 1, 2).reshape(SEQS, N, PAIR)
 
     groups = lax.axis_size("sess")
-    state, extras, caches, band = exchange(
+    state, extras, caches, band, partial = exchange(
         groups,
         home_slot,
         turn_lengths,
+        skip_gain,
         saved,
         x,
         steps,
         rates,
         write,
+        read,
         cache_keys[0],
         cache_values[0],
         turn_keys[0].reshape(8, 16, KVH * HD),
@@ -765,7 +787,7 @@
     attended = attention(
         turn_lengths, history_lengths, queries[0], band, sink_keys[0], sink_values[0], caches
     )
-    mixed = outputs(turn_lengths, skip_gain, x, steps, rates, write, read, state, extras)
+    mixed = outputs(turn_lengths, rates, read, partial, state, extras)
     return (mixed[None], attended[None])
 
 

time: 109 us -> 105 us (0.963)
  the two profiles are of different devices: /device:TPU:33 before, /device:TPU:38 now
where the time goes in v6:
time: 105 us
  Pallas kernels  103 us (98%)
    pallas_call x1, Pallas kernels, exchange(): pl.pallas_call(exchange_kernel, out_shape=(jax.ShapeDtypeStruct((2, CHIPS...  79.1 us
    pallas_call x1, Pallas kernels, attention(): pl.pallas_call(attention_kernel, out_shape=jax.ShapeDtypeStruct((TOK, QH...  16.6 us
    pallas_call x1, Pallas kernels, outputs(): pl.pallas_call(output_kernel, grid=(STEPS,), out_shape=jax.ShapeDtypeStru...  6.89 us

profile of v6, /device:TPU:38, one launch (start us, length us, event | category | flops | bytes accessed | tf_op | source)
XLA Modules:
  0.0 105.2 jit_solution(6614892930892069382)
XLA Ops:
  0.6 1.0 convert_element_type.7
  1.6 0.2 convert_element_type.8
  1.8 0.8 copy.21.saved
  2.6 79.1 %shard_map.176 = (bf16[2,16,64,256]{3,2,1,0:T(8,128)(2,1)}, bf16[2,16,2,64,256]{4,3,2,1,0:T(8,128)(2,1)}, bf16[32,2,3,16,512]{4,3,2,1,0:T(8,128)(2,1)}, bf16[40,16,1024]{2,1,0:T(8,128)(2,1)}, f32[128,8192]{1,0:T(8,128)}) custom-call(s32[24]{0:T(128)} %home.1, s32[1,3]{1,0:T(1,128)} %lengths.5, f32[64]{0:T(128)} %gain.1, bf16[3,64,256]{2,1,0:T(8,128)(2,1)} %copy.21.saved, ...), custom_call_target="tpu_custom_call" | custom-call | tf_op jit(solution)/shard_map/pallas_call | solution.py:651
  81.7 6.9 %shard_map.177 = bf16[128,8192]{1,0:T(8,128)(2,1)} custom-call(s32[1,3]{1,0:T(1,128)} %lengths.5, bf16[64,128]{1,0:T(8,128)(2,1)} %bitcast.30, bf16[128,512]{1,0:T(8,128)(2,1)} %bitcast.25, f32[128,8192]{1,0:T(8,128)} %get-tuple-element.7.partial, bf16[2,16,64,256]{3,2,1,0:T(8,128)(2,1)} %get-tuple-element.8.state, ...), custom_call_target="tpu_custom_call" | custom-call | tf_op jit(solution)/shard_map/pallas_call | solution.py:704
  88.6 16.6 %shard_map.178 = bf16[128,4096]{1,0:T(8,128)(2,1)} custom-call(s32[1,3]{1,0:T(1,128)} %lengths.5, s32[1,3]{1,0:T(1,128)} %history.1, bf16[128,4096]{1,0:T(8,128)(2,1)} %bitcast.34, bf16[40,16,1024]{2,1,0:T(8,128)(2,1)} %get-tuple-element.10.band, bf16[3,4,512]{2,1,0:T(4,128)(2,1)} %bitcast.35, bf16[3,4,512]{2,1,0:T(4,128)(2,1)} %bitcast.36, ...), custom_call_target="tpu_custom_call" | custom-call | flops 2500000000 | bytes 8000000 | tf_op jit(solution)/shard_map/pallas_call | solution.py:723

commit v7 on v6

--- a/solution.py
+++ b/solution.py
@@ -9,6 +9,7 @@
 from jax.sharding import PartitionSpec as P
 
 TOK = 128
+HALF = TOK // 2
 REACH = 4
 SEQS = 3
 SINKS = 4
@@ -473,16 +474,19 @@
     edges = [jnp.int32(0), one, two, jnp.int32(CTX * TOK)]
     lives = []
     for s in range(SEQS):
-        begin = jnp.maximum(edges[s], first)
-        present = begin < jnp.minimum(edges[s + 1], first + TOK)
-        lives.append(
-            [
-                present
-                & (begin - edges[s] < j * TOK + TOK - 1)
-                & (history[0, s] - WINDOW + j * TOK + TOK - 1 >= SINKS)
-                for j in range(4)
-            ]
-        )
+        lives.append([])
+        for part in range(2):
+            from_token = first + part * HALF
+            begin = jnp.maximum(edges[s], from_token)
+            present = begin < jnp.minimum(edges[s + 1], from_token + HALF)
+            lives[s].append(
+                [
+                    present
+                    & (begin - edges[s] < j * TOK + TOK - 1)
+                    & (history[0, s] - WINDOW + j * TOK + TOK - 1 >= SINKS)
+                    for j in range(4)
+                ]
+            )
     copies = [
         pltpu.make_async_copy(band, keys.at[pl.ds(0, 8 * SINK_BLOCK)], sems.at[0]),
     ]
@@ -499,7 +503,8 @@
             for kv in range(2)
         ]
 
-    wanted = [lives[s][0] | lives[s][1] | lives[s][2] | lives[s][3] for s in range(SEQS)]
+    needed = [[lives[s][0][j] | lives[s][1][j] for j in range(4)] for s in range(SEQS)]
+    wanted = [needed[s][0] | needed[s][1] | needed[s][2] | needed[s][3] for s in range(SEQS)]
     for s in range(SEQS):
 
         @pl.when(wanted[s])
@@ -519,39 +524,41 @@
     u = iota((TOK, TOK), 1)
     owner = segment(t, one, two)
     offset = t - jnp.where(owner == 2, two, jnp.where(owner == 1, one, 0))
-    count = jnp.int32(0)
-    head_owner = (first >= one).astype(I32) + (first >= two).astype(I32)
     for b in range(REACH + 1):
         pos = first + (b - REACH) * TOK + u
         gap = t - pos
         ok = (pos >= 0) & (segment(pos, one, two) == owner) & (gap >= 0) & (gap < WINDOW)
         bias[b] = jnp.where(ok, 0.0, -jnp.inf)
-        end = first + (b - REACH) * TOK + TOK - 1
-        end_owner = (end >= one).astype(I32) + (end >= two).astype(I32)
-        live = (end >= 0) & (end_owner >= head_owner)
-        listed[count] = b
-        count = count + live.astype(I32)
-    bias[SINK_BLOCK] = jnp.where(
-        (u < SEQS * SINKS) & (u // SINKS == owner), 0.0, -jnp.inf
-    )
-    listed[count] = SINK_BLOCK
-    count = count + 1
+    bias[SINK_BLOCK] = jnp.where((u < SEQS * SINKS) & (u // SINKS == owner), 0.0, -jnp.inf)
     for s in range(SEQS):
         for j in range(4):
-            live = lives[s][j]
-            block = CACHE_BLOCK + 4 * s + j
-
-            @pl.when(live)
+
+            @pl.when(needed[s][j])
             def _():
                 slot = j * TOK + u
                 ok = (owner == s) & (slot > offset) & (history[0, s] - WINDOW + slot >= SINKS)
-                bias[block] = jnp.where(ok, 0.0, -jnp.inf)
-
-            listed[count] = block
+                bias[CACHE_BLOCK + 4 * s + j] = jnp.where(ok, 0.0, -jnp.inf)
+
+    bias[NULL_BLOCK] = jnp.full((TOK, TOK), -jnp.inf, F32)
+    pairs = []
+    for part in range(2):
+        count = jnp.int32(0)
+        from_token = first + part * HALF
+        from_owner = (from_token >= one).astype(I32) + (from_token >= two).astype(I32)
+        for b in range(REACH + 1):
+            end = first + (b - REACH) * TOK + TOK - 1
+            end_owner = (end >= one).astype(I32) + (end >= two).astype(I32)
+            live = (end >= 0) & (end_owner >= from_owner)
+            listed[part, count] = b
             count = count + live.astype(I32)
-    bias[NULL_BLOCK] = jnp.full((TOK, TOK), -jnp.inf, F32)
-    listed[count] = NULL_BLOCK
-    pairs = lax.div(count + 1, jnp.int32(2))
+        listed[part, count] = SINK_BLOCK
+        count = count + 1
+        for s in range(SEQS):
+            for j in range(4):
+                listed[part, count] = CACHE_BLOCK + 4 * s + j
+                count = count + lives[s][part][j].astype(I32)
+        listed[part, count] = NULL_BLOCK
+        pairs.append(lax.div(count + 1, jnp.int32(2)))
     for copy in copies:
         copy.wait()
     for s in range(SEQS):
@@ -567,52 +574,55 @@
     def one_head(number, nothing):
         lanes = pl.ds(pl.multiple_of(number * HD, HD), HD)
         value_lanes = pl.ds(pl.multiple_of(number * HD + KVH * HD, HD), HD)
-        for r in range(per):
-            wide = pl.ds(pl.multiple_of((number * per + r) * HD, HD), HD)
-            rows[r * TOK : (r + 1) * TOK, :] = queries[:, wide]
-        top[...] = jnp.full(top.shape, -jnp.inf, F32)
-        total[...] = jnp.zeros(total.shape, F32)
-        sums[...] = jnp.zeros(sums.shape, F32)
-
-        def score(i, nothing):
-            blocks = [listed[2 * i + part] for part in range(2)]
-            key = [keys[pl.ds(b * 8, 8), :, lanes].reshape(TOK, HD) for b in blocks]
-            key = jnp.concatenate(key, axis=0)
-            left_bias, right_bias = bias[blocks[0]], bias[blocks[1]]
+
+        def wide(r):
+            return pl.ds(pl.multiple_of((number * per + r) * HD, HD), HD)
+
+        for part in range(2):
+            tokens = slice(part * HALF, (part + 1) * HALF)
             for r in range(per):
-                at = slice(r * TOK, (r + 1) * TOK)
-                made = nt(rows[at, :], key) * scale
-                left = made[:, :TOK] + left_bias
-                right = made[:, TOK:] + right_bias
-                scores[2 * i, at, :] = left
-                scores[2 * i + 1, at, :] = right
-                top[at, :] = jnp.maximum(top[at, :], jnp.maximum(left, right))
-            return nothing
-
-        lax.fori_loop(0, pairs, score, 0)
-        top[...] = jnp.broadcast_to(jnp.max(top[...], axis=1, keepdims=True), top.shape)
-
-        def weigh(i, nothing):
-            values = []
-            for part in range(2):
-                block = listed[2 * i + part]
-                values.append(keys[pl.ds(block * 8, 8), :, value_lanes].reshape(TOK, HD))
-            value = jnp.concatenate(values, axis=0)
+                rows[r * HALF : (r + 1) * HALF, :] = queries[tokens, wide(r)]
+            top[...] = jnp.full(top.shape, -jnp.inf, F32)
+            total[...] = jnp.zeros(total.shape, F32)
+            sums[...] = jnp.zeros(sums.shape, F32)
+
+            def score(i, nothing, part=part, tokens=tokens):
+                blocks = [listed[part, 2 * i + side] for side in range(2)]
+                key = [keys[pl.ds(b * 8, 8), :, lanes].reshape(TOK, HD) for b in blocks]
+                key = jnp.concatenate(key, axis=0)
+                shift = [bias[b, tokens, :] for b in blocks]
+                shift = [jnp.concatenate([b, b], axis=0) for b in shift]
+                for r in range(per // 2):
+                    at = slice(r * TOK, (r + 1) * TOK)
+                    made = nt(rows[at, :], key) * scale
+                    left = made[:, :TOK] + shift[0]
+                    right = made[:, TOK:] + shift[1]
+                    scores[2 * i, at, :] = left
+                    scores[2 * i + 1, at, :] = right
+                    top[at, :] = jnp.maximum(top[at, :], jnp.maximum(left, right))
+                return nothing
+
+            lax.fori_loop(0, pairs[part], score, 0)
+            top[...] = jnp.broadcast_to(jnp.max(top[...], axis=1, keepdims=True), top.shape)
+
+            def weigh(i, nothing, part=part):
+                blocks = [listed[part, 2 * i + side] for side in range(2)]
+                value = [keys[pl.ds(b * 8, 8), :, value_lanes].reshape(TOK, HD) for b in blocks]
+                value = jnp.concatenate(value, axis=0)
+                for r in range(per // 2):
+                    at = slice(r * TOK, (r + 1) * TOK)
+                    left = jnp.exp2(scores[2 * i, at, :] - top[at, :])
+                    right = jnp.exp2(scores[2 * i + 1, at, :] - top[at, :])
+                    total[at, :] += left + right
+                    both = jnp.concatenate([left.astype(BF16), right.astype(BF16)], axis=1)
+                    sums[at, :] += nn(both, value)
+                return nothing
+
+            lax.fori_loop(0, pairs[part], weigh, 0)
             for r in range(per):
-                at = slice(r * TOK, (r + 1) * TOK)
-                left = jnp.exp2(scores[2 * i, at, :] - top[at, :])
-                right = jnp.exp2(scores[2 * i + 1, at, :] - top[at, :])
-                total[at, :] += left + right
-                both = jnp.concatenate([left.astype(BF16), right.astype(BF16)], axis=1)
-                sums[at, :] += nn(both, value)
-            return nothing
-
-        lax.fori_loop(0, pairs, weigh, 0)
-        for r in range(per):
-            at = slice(r * TOK, (r + 1) * TOK)
-            whole = jnp.sum(total[at, :], axis=1, keepdims=True)
-            wide = pl.ds(pl.multiple_of((number * per + r) * HD, HD), HD)
-            out[:, wide] = (sums[at, :] / whole).astype(BF16)
+                at = slice(r * HALF, (r + 1) * HALF)
+                whole = jnp.sum(total[at, :], axis=1, keepdims=True)
+                out[tokens, wide(r)] = (sums[at, :] / whole).astype(BF16)
         return nothing
 
     lax.fori_loop(0, KVH, one_head, 0)
@@ -719,7 +729,7 @@
 
 
 def attention(lengths, history, queries, band, sink_keys, sink_values, cache):
-    rows = (QH // KVH) * TOK
+    rows = (QH // KVH) * HALF
     return pl.pallas_call(
         attention_kernel,
         out_shape=jax.ShapeDtypeStruct((TOK, QH * HD), BF16),
@@ -733,7 +743,7 @@
             pltpu.VMEM((rows, TOK), F32),
             pltpu.VMEM((rows, HD), F32),
             pltpu.VMEM((BLOCKS, TOK, TOK), F32),
-            pltpu.SMEM((BLOCKS + 1,), I32),
+            pltpu.SMEM((2, BLOCKS + 1), I32),
             pltpu.SemaphoreType.DMA((8,)),
         ],
         compiler_params=LIMIT,

time: 105 us -> 108 us (1.029)
  the two profiles are of different devices: /device:TPU:38 before, /device:TPU:33 now
where the time goes in v7:
time: 108 us
  Pallas kernels  105 us (97%)
    pallas_call x1, Pallas kernels, exchange(): pl.pallas_call(exchange_kernel, out_shape=(jax.ShapeDtypeStruct((2, CHIPS...  79.8 us
    pallas_call x1, Pallas kernels, attention(): pl.pallas_call(attention_kernel, out_shape=jax.ShapeDtypeStruct((TOK, QH...  18.2 us
    pallas_call x1, Pallas kernels, outputs(): pl.pallas_call(output_kernel, grid=(STEPS,), out_shape=jax.ShapeDtypeStru...  6.91 us

profile of v7, /device:TPU:33, one launch (start us, length us, event | category | flops | bytes accessed | tf_op | source)
XLA Modules:
  0.0 107.6 jit_solution(11271049820717335504)
XLA Ops:
  0.6 1.0 convert_element_type.7
  1.6 0.2 convert_element_type.8
  1.8 0.8 copy.21.saved
  2.6 79.8 %shard_map.176 = (bf16[2,16,64,256]{3,2,1,0:T(8,128)(2,1)}, bf16[2,16,2,64,256]{4,3,2,1,0:T(8,128)(2,1)}, bf16[32,2,3,16,512]{4,3,2,1,0:T(8,128)(2,1)}, bf16[40,16,1024]{2,1,0:T(8,128)(2,1)}, f32[128,8192]{1,0:T(8,128)}) custom-call(s32[24]{0:T(128)} %home.1, s32[1,3]{1,0:T(1,128)} %lengths.5, f32[64]{0:T(128)} %gain.1, bf16[3,64,256]{2,1,0:T(8,128)(2,1)} %copy.21.saved, ...), custom_call_target="tpu_custom_call" | custom-call | tf_op jit(solution)/shard_map/pallas_call | solution.py:661
  82.5 6.9 %shard_map.177 = bf16[128,8192]{1,0:T(8,128)(2,1)} custom-call(s32[1,3]{1,0:T(1,128)} %lengths.5, bf16[64,128]{1,0:T(8,128)(2,1)} %bitcast.30, bf16[128,512]{1,0:T(8,128)(2,1)} %bitcast.25, f32[128,8192]{1,0:T(8,128)} %get-tuple-element.7.partial, bf16[2,16,64,256]{3,2,1,0:T(8,128)(2,1)} %get-tuple-element.8.state, ...), custom_call_target="tpu_custom_call" | custom-call | tf_op jit(solution)/shard_map/pallas_call | solution.py:714
  89.4 18.2 %shard_map.178 = bf16[128,4096]{1,0:T(8,128)(2,1)} custom-call(s32[1,3]{1,0:T(1,128)} %lengths.5, s32[1,3]{1,0:T(1,128)} %history.1, bf16[128,4096]{1,0:T(8,128)(2,1)} %bitcast.34, bf16[40,16,1024]{2,1,0:T(8,128)(2,1)} %get-tuple-element.10.band, bf16[3,4,512]{2,1,0:T(4,128)(2,1)} %bitcast.35, bf16[3,4,512]{2,1,0:T(4,128)(2,1)} %bitcast.36, ...), custom_call_target="tpu_custom_call" | custom-call | flops 2500000000 | bytes 8000000 | tf_op jit(solution)/shard_map/pallas_call | solution.py:733

commit v8 on v6

--- a/solution.py
+++ b/solution.py
@@ -564,58 +564,64 @@
     per = QH // KVH
     scale = 1.0 / math.sqrt(HD) / math.log(2.0)
 
-    def one_head(number, nothing):
-        lanes = pl.ds(pl.multiple_of(number * HD, HD), HD)
-        value_lanes = pl.ds(pl.multiple_of(number * HD + KVH * HD, HD), HD)
-        for r in range(per):
-            wide = pl.ds(pl.multiple_of((number * per + r) * HD, HD), HD)
-            rows[r * TOK : (r + 1) * TOK, :] = queries[:, wide]
+    def heads(pair, nothing):
+        def lanes(h, shift=0):
+            return pl.ds(pl.multiple_of((pair * 2 + h) * HD + shift, HD), HD)
+
+        def wide(h, r):
+            return pl.ds(pl.multiple_of(((pair * 2 + h) * per + r) * HD, HD), HD)
+
+        for h in range(2):
+            for r in range(per):
+                rows[h, r * TOK : (r + 1) * TOK, :] = queries[:, wide(h, r)]
         top[...] = jnp.full(top.shape, -jnp.inf, F32)
         total[...] = jnp.zeros(total.shape, F32)
         sums[...] = jnp.zeros(sums.shape, F32)
 
         def score(i, nothing):
-            blocks = [listed[2 * i + part] for part in range(2)]
-            key = [keys[pl.ds(b * 8, 8), :, lanes].reshape(TOK, HD) for b in blocks]
-            key = jnp.concatenate(key, axis=0)
+            blocks = [listed[2 * i + side] for side in range(2)]
             left_bias, right_bias = bias[blocks[0]], bias[blocks[1]]
+            for h in range(2):
+                key = [keys[pl.ds(b * 8, 8), :, lanes(h)].reshape(TOK, HD) for b in blocks]
+                key = jnp.concatenate(key, axis=0)
+                for r in range(per):
+                    at = slice(r * TOK, (r + 1) * TOK)
+                    made = nt(rows[h, at, :], key) * scale
+                    left = made[:, :TOK] + left_bias
+                    right = made[:, TOK:] + right_bias
+                    scores[2 * i, h, at, :] = left
+                    scores[2 * i + 1, h, at, :] = right
+                    top[h, at, :] = jnp.maximum(top[h, at, :], jnp.maximum(left, right))
+            return nothing
+
+        lax.fori_loop(0, pairs, score, 0)
+        top[...] = jnp.broadcast_to(jnp.max(top[...], axis=2, keepdims=True), top.shape)
+
+        def weigh(i, nothing):
+            blocks = [listed[2 * i + side] for side in range(2)]
+            for h in range(2):
+                value = [
+                    keys[pl.ds(b * 8, 8), :, lanes(h, KVH * HD)].reshape(TOK, HD) for b in blocks
+                ]
+                value = jnp.concatenate(value, axis=0)
+                for r in range(per):
+                    at = slice(r * TOK, (r + 1) * TOK)
+                    left = jnp.exp2(scores[2 * i, h, at, :] - top[h, at, :])
+                    right = jnp.exp2(scores[2 * i + 1, h, at, :] - top[h, at, :])
+                    total[h, at, :] += left + right
+                    both = jnp.concatenate([left.astype(BF16), right.astype(BF16)], axis=1)
+                    sums[h, at, :] += nn(both, value)
+            return nothing
+
+        lax.fori_loop(0, pairs, weigh, 0)
+        for h in range(2):
             for r in range(per):
                 at = slice(r * TOK, (r + 1) * TOK)
-                made = nt(rows[at, :], key) * scale
-                left = made[:, :TOK] + left_bias
-                right = made[:, TOK:] + right_bias
-                scores[2 * i, at, :] = left
-                scores[2 * i + 1, at, :] = right
-                top[at, :] = jnp.maximum(top[at, :], jnp.maximum(left, right))
-            return nothing
-
-        lax.fori_loop(0, pairs, score, 0)
-        top[...] = jnp.broadcast_to(jnp.max(top[...], axis=1, keepdims=True), top.shape)
-
-        def weigh(i, nothing):
-            values = []
-            for part in range(2):
-                block = listed[2 * i + part]
-                values.append(keys[pl.ds(block * 8, 8), :, value_lanes].reshape(TOK, HD))
-            value = jnp.concatenate(values, axis=0)
-            for r in range(per):
-                at = slice(r * TOK, (r + 1) * TOK)
-                left = jnp.exp2(scores[2 * i, at, :] - top[at, :])
-                right = jnp.exp2(scores[2 * i + 1, at, :] - top[at, :])
-                total[at, :] += left + right
-                both = jnp.concatenate([left.astype(BF16), right.astype(BF16)], axis=1)
-                sums[at, :] += nn(both, value)
-            return nothing
-
-        lax.fori_loop(0, pairs, weigh, 0)
-        for r in range(per):
-            at = slice(r * TOK, (r + 1) * TOK)
-            whole = jnp.sum(total[at, :], axis=1, keepdims=True)
-            wide = pl.ds(pl.multiple_of((number * per + r) * HD, HD), HD)
-            out[:, wide] = (sums[at, :] / whole).astype(BF16)
+                whole = jnp.sum(total[h, at, :], axis=1, keepdims=True)
+                out[:, wide(h, r)] = (sums[h, at, :] / whole).astype(BF16)
         return nothing
 
-    lax.fori_loop(0, KVH, one_head, 0)
+    lax.fori_loop(0, KVH // 2, heads, 0)
 
 
 SMEM = pl.BlockSpec(memory_space=pltpu.SMEM)
@@ -727,11 +733,11 @@
         out_specs=VMEM,
         scratch_shapes=[
             pltpu.VMEM((8 * BLOCKS, 16, 2 * KVH * HD), BF16),
-            pltpu.VMEM((rows, HD), BF16),
-            pltpu.VMEM((BLOCKS + 1, rows, TOK), F32),
-            pltpu.VMEM((rows, TOK), F32),
-            pltpu.VMEM((rows, TOK), F32),
-            pltpu.VMEM((rows, HD), F32),
+            pltpu.VMEM((2, rows, HD), BF16),
+            pltpu.VMEM((BLOCKS + 1, 2, rows, TOK), F32),
+            pltpu.VMEM((2, rows, TOK), F32),
+            pltpu.VMEM((2, rows, TOK), F32),
+            pltpu.VMEM((2, rows, HD), F32),
             pltpu.VMEM((BLOCKS, TOK, TOK), F32),
             pltpu.SMEM((BLOCKS + 1,), I32),
             pltpu.SemaphoreType.DMA((8,)),

time: 105 us -> 101 us (0.962)
  the two profiles are of different devices: /device:TPU:38 before, /device:TPU:33 now
where the time goes in v8:
time: 101 us
  Pallas kernels  98.3 us (97%)
    pallas_call x1, Pallas kernels, exchange(): pl.pallas_call(exchange_kernel, out_shape=(jax.ShapeDtypeStruct((2, CHIPS...  79.8 us
    pallas_call x1, Pallas kernels, attention(): pl.pallas_call(attention_kernel, out_shape=jax.ShapeDtypeStruct((TOK, QH...  11.5 us
    pallas_call x1, Pallas kernels, outputs(): pl.pallas_call(output_kernel, grid=(STEPS,), out_shape=jax.ShapeDtypeStru...  6.91 us

profile of v8, /device:TPU:33, one launch (start us, length us, event | category | flops | bytes accessed | tf_op | source)
XLA Modules:
  0.0 100.9 jit_solution(5982332086106196959)
XLA Ops:
  0.6 1.0 convert_element_type.7
  1.6 0.2 convert_element_type.8
  1.8 0.8 copy.21.saved
  2.6 79.8 %shard_map.176 = (bf16[2,16,64,256]{3,2,1,0:T(8,128)(2,1)}, bf16[2,16,2,64,256]{4,3,2,1,0:T(8,128)(2,1)}, bf16[32,2,3,16,512]{4,3,2,1,0:T(8,128)(2,1)}, bf16[40,16,1024]{2,1,0:T(8,128)(2,1)}, f32[128,8192]{1,0:T(8,128)}) custom-call(s32[24]{0:T(128)} %home.1, s32[1,3]{1,0:T(1,128)} %lengths.5, f32[64]{0:T(128)} %gain.1, bf16[3,64,256]{2,1,0:T(8,128)(2,1)} %copy.21.saved, ...), custom_call_target="tpu_custom_call" | custom-call | tf_op jit(solution)/shard_map/pallas_call | solution.py:657
  82.5 6.9 %shard_map.177 = bf16[128,8192]{1,0:T(8,128)(2,1)} custom-call(s32[1,3]{1,0:T(1,128)} %lengths.5, bf16[64,128]{1,0:T(8,128)(2,1)} %bitcast.30, bf16[128,512]{1,0:T(8,128)(2,1)} %bitcast.25, f32[128,8192]{1,0:T(8,128)} %get-tuple-element.7.partial, bf16[2,16,64,256]{3,2,1,0:T(8,128)(2,1)} %get-tuple-element.8.state, ...), custom_call_target="tpu_custom_call" | custom-call | tf_op jit(solution)/shard_map/pallas_call | solution.py:710
  89.4 11.5 %shard_map.178 = bf16[128,4096]{1,0:T(8,128)(2,1)} custom-call(s32[1,3]{1,0:T(1,128)} %lengths.5, s32[1,3]{1,0:T(1,128)} %history.1, bf16[128,4096]{1,0:T(8,128)(2,1)} %bitcast.34, bf16[40,16,1024]{2,1,0:T(8,128)(2,1)} %get-tuple-element.10.band, bf16[3,4,512]{2,1,0:T(4,128)(2,1)} %bitcast.35, bf16[3,4,512]{2,1,0:T(4,128)(2,1)} %bitcast.36, ...), custom_call_target="tpu_custom_call" | custom-call | flops 2500000000 | bytes 8000000 | tf_op jit(solution)/shard_map/pallas_call | solution.py:729
